TPU v7x, 32 devices: a whole 2x2x4 slice. The times are simulated.
32 devices in a mesh: seq: 8 (over z, y), tp: 4 (over x, core).
Axes of the slice: x: 2, y: 2, z: 4, core: 2. Of those that a mesh axis runs over, the one named last changes fastest.
Arguments:
- query_proj: bfloat16 [1536, 3072], P('seq', 'tp'), may hold values from -6 to 6
- key_proj: bfloat16 [1536, 3072], P('seq', 'tp'), may hold values from -6 to 6
- value_proj: bfloat16 [1536, 3072], P('seq', 'tp'), may hold values from -6 to 6
- attn_output: bfloat16 [1536, 3072], P('seq', 'tp')
- out_grad: bfloat16 [1536, 3072], P('seq', 'tp'), may hold values from -6 to 6
- log_norm: float32 [1536, 24], P('seq', 'tp')
- router_logit: float32 [1536], P('seq'), may hold values from -4 to 4
- keep_positions: int32 [1536], replicated, may hold values from -1 to 8191, as said below
Outputs:
- query_grad: bfloat16 [1536, 3072], P('seq', 'tp')
- key_grad: bfloat16 [1536, 3072], P('seq', 'tp')
- value_grad: bfloat16 [1536, 3072], P('seq', 'tp')
- router_grad: float32 [1536], P('seq')
Inputs may be any that keep to these rules, and one draw needn't show every extreme that they name: `keep_positions`: slots s*192 to (s+1)*192 - 1 hold the kept positions of tokens s*1024 to (s+1)*1024 - 1 in increasing order, followed by -1 in the unused slots. Exactly 1024 tokens are kept in all; some shard fills all 192 slots and some shard keeps only 64.
All inputs are finite; a program needn't handle non-finite values.
Results may differ from a plain program's by a relative error of at most 0.03.
Values may be sent and summed in bfloat16 or wider, within the bound.
No kernel may reach another device: no remote copies, remote signals or barrier semaphores. Data moves between devices by JAX's collectives and lax.ppermute only.
A program may use at most 128 MiB of HBM per device.

v0:
```python
import jax
import jax.numpy as jnp
from jax import lax
from jax.sharding import PartitionSpec as P


def pick_block(total_rows):
    for size in (1024, 512):
        if total_rows % size == 0:
            return size
    return total_rows


def body(
    query_proj, key_proj, value_proj, attn_output, out_grad, log_norm, router_logit, keep_positions
):
    slots = query_proj.shape[0]
    heads = log_norm.shape[1]
    feature_count = query_proj.shape[1]
    head_dim = feature_count // heads
    scale = head_dim ** (-0.5)
    shard = lax.axis_index("seq")
    my_positions = lax.dynamic_slice_in_dim(keep_positions, shard * slots, slots)
    my_valid = my_positions >= 0
    gate = jax.nn.sigmoid(router_logit)
    slope = gate * (1.0 - gate)
    grad_wide = out_grad.astype(jnp.float32)
    output_wide = attn_output.astype(jnp.float32)
    partial_dot = jnp.sum(grad_wide * output_wide, axis=1)
    total_dot = lax.psum(partial_dot, "tp")
    router_grad = jnp.where(my_valid, slope * total_dot, jnp.float32(0.0))
    dout = (gate[:, None] * grad_wide).astype(jnp.bfloat16)
    delta = jnp.sum(
        (dout.astype(jnp.float32) * output_wide).reshape(slots, heads, head_dim), axis=2
    )
    local_key = key_proj.reshape(slots, heads, head_dim)
    local_value = value_proj.reshape(slots, heads, head_dim)
    query_all, dout_all = (
        lax.all_gather(query_proj, "seq", axis=0, tiled=True),
        lax.all_gather(dout, "seq", axis=0, tiled=True),
    )
    norm_all, delta_all = (
        lax.all_gather(log_norm, "seq", axis=0, tiled=True),
        lax.all_gather(delta, "seq", axis=0, tiled=True),
    )
    total_rows = query_all.shape[0]
    block = pick_block(total_rows)
    steps_count = total_rows // block

    def step(carry, index):
        key_acc, value_acc = carry
        start = index * block
        query_part = lax.dynamic_slice_in_dim(query_all, start, block, 0).reshape(
            block, heads, head_dim
        )
        dout_part = lax.dynamic_slice_in_dim(dout_all, start, block, 0).reshape(
            block, heads, head_dim
        )
        norm_part = lax.dynamic_slice_in_dim(norm_all, start, block, 0)
        delta_part = lax.dynamic_slice_in_dim(delta_all, start, block, 0)
        position_part = lax.dynamic_slice_in_dim(keep_positions, start, block, 0)
        allowed = (
            (position_part >= 0)[:, None]
            & my_valid[None, :]
            & (my_positions[None, :] <= position_part[:, None])
        )
        scores = (
            jnp.einsum("qhd,khd->hqk", query_part, local_key, preferred_element_type=jnp.float32)
            * scale
        )
        prob = jnp.where(allowed[None], jnp.exp(scores - norm_part.T[:, :, None]), jnp.float32(0.0))
        prob_low = prob.astype(jnp.bfloat16)
        dprob = jnp.einsum(
            "qhd,khd->hqk", dout_part, local_value, preferred_element_type=jnp.float32
        )
        dscore = (prob * (dprob - delta_part.T[:, :, None]) * scale).astype(jnp.bfloat16)
        value_acc = value_acc + jnp.einsum(
            "hqk,qhd->khd", prob_low, dout_part, preferred_element_type=jnp.float32
        )
        key_acc = key_acc + jnp.einsum(
            "hqk,qhd->khd", dscore, query_part, preferred_element_type=jnp.float32
        )
        term = jnp.einsum(
            "hqk,khd->qhd", dscore, local_key, preferred_element_type=jnp.float32
        ).reshape(block, feature_count)
        return ((key_acc, value_acc), term)

    empty = jnp.zeros((slots, heads, head_dim), jnp.float32)
    (key_acc, value_acc), key_terms = lax.scan(
        step, (empty, empty), jnp.arange(steps_count, dtype=jnp.int32)
    )
    key_grad = key_acc.reshape(slots, feature_count).astype(jnp.bfloat16)
    value_grad = value_acc.reshape(slots, feature_count).astype(jnp.bfloat16)
    key_terms = key_terms.reshape(total_rows, feature_count)
    key_grad, value_grad, terms = (key_grad, value_grad, key_terms)
    query_grad = lax.psum_scatter(terms, "seq", scatter_dimension=0, tiled=True).astype(
        jnp.bfloat16
    )
    return (query_grad, key_grad, value_grad, router_grad)


def solution(mesh):
    placed = (
        P("seq", "tp"),
        P("seq", "tp"),
        P("seq", "tp"),
        P("seq", "tp"),
        P("seq", "tp"),
        P("seq", "tp"),
        P("seq"),
        P(),
    )
    return jax.shard_map(
        body,
        mesh=mesh,
        in_specs=placed,
        out_specs=(P("seq", "tp"), P("seq", "tp"), P("seq", "tp"), P("seq")),
        check_vma=False,
    )
```

profile of v0, /device:TPU:0, one launch (start us, length us, event | category | flops | bytes accessed | tf_op | source)
XLA Modules:
  0.0 266.1 jit_solution(17717001706590042693)
XLA Ops:
  9.2 8.3 %psum.7 = f32[192]{0:T(256)S(1)} all-reduce(f32[192]{0:T(256)S(1)} %fusion.11), channel_id=1, replica_groups=mesh['seq'=8,'tp'=4] {'tp'}, use_global_device_ids=true, to_apply=%region_5.6 | all-reduce | flops 192 | bytes 1536 | tf_op jit(solution)/shard_map/psum | solution.py:30
  17.5 1.3 fusion.13
  18.9 2.0 convert_multiply_fusion.1
  21.0 31.0 %all-gather = f32[8,192,6]{1,2,0:T(8,128)S(1)} all-gather(f32[1,192,6]{1,2,0:T(8,128)S(1)} %bitcast.93), channel_id=1, replica_groups=mesh['seq'=8,'tp'=4] {'seq'}, dimensions={0}, use_global_device_ids=true | all-gather | bytes 41472 | tf_op jit(solution)/shard_map/all_gather | solution.py:43
  52.5 30.7 %all-gather.1 = f32[8,192,6]{1,2,0:T(8,128)S(1)} all-gather(f32[1,192,6]{1,2,0:T(8,128)S(1)} %copy.47), channel_id=1, replica_groups=mesh['seq'=8,'tp'=4] {'seq'}, dimensions={0}, use_global_device_ids=true | all-gather | bytes 41472 | tf_op jit(solution)/shard_map/all_gather | solution.py:44
  84.3 35.1 %all-gather.7.cloned.1.call-done = bf16[1536,768]{1,0:T(8,128)(2,1)} async-done(((bf16[192,768]{1,0:T(8,128)(2,1)}), bf16[1536,768]{1,0:T(8,128)(2,1)}) %all-gather.7.cloned.1.call-update) | async-done | bytes 2359312 | tf_op jit(solution)/shard_map/all_gather | solution.py:40
  119.3 44.4 %while.15 = (s32[]{:T(128)}, f32[192,6,128]{2,0,1:T(8,128)}, f32[192,6,128]{2,0,1:T(8,128)}, f32[3,512,768]{2,1,0:T(8,128)}, s32[3]{0:T(128)S(1)}, /*index=5*/bf...) while((s32[]{:T(128)}, f32[192,6,128]{2,0,1:T(8,128)}, ...), condition=%wide.region_2.3_spmd.clone, body=%wide.region_1.0_spmd.clone.sunk | while | flops 762348032 | bytes 31551680 | solution.py:89
  121.5 1.5 constant_dynamic-slice_fusion.3
  123.6 1.4 fusion.52
  125.0 1.4 fusion.54
  126.4 1.9 multiply_convert_fusion.2
  128.3 1.3 fusion.53
  129.6 1.4 fusion.55
  131.5 1.3 constant_dynamic-update-slice_fusion.2
  134.9 1.5 constant_dynamic-slice_fusion.3
  137.0 1.4 fusion.52
  138.4 2.5 fusion.54
  140.9 1.9 multiply_convert_fusion.2
  142.8 2.4 fusion.53
  145.2 1.4 fusion.55
  147.0 1.3 constant_dynamic-update-slice_fusion.2
  150.4 1.5 constant_dynamic-slice_fusion.3
  152.5 1.4 fusion.52
  153.9 2.5 fusion.54
  156.4 1.9 multiply_convert_fusion.2
  158.3 2.4 fusion.53
  160.7 1.4 fusion.55
  162.5 1.3 constant_dynamic-update-slice_fusion.2
  163.8 1.8 copy_bitcast_fusion.1
  165.6 1.8 copy_bitcast_fusion
  167.4 90.3 %reduce-scatter.2.cloned.1.call-done = f32[192,768]{1,0:T(8,128)} async-done(((f32[1536,768]{1,0:T(8,128)}), f32[192,768]{1,0:T(8,128)}) %reduce-scatter.2.cloned.1.call-update) | async-done | bytes 589840 | tf_op jit(solution)/shard_map/reduce_scatter | solution.py:96
  257.8 1.8 convert_element_type.37
  (47 shorter events, 11.2 us)
Async XLA Ops:
  7.2 76.2 %copy-start = (bf16[192,768]{1,0:T(8,128)(2,1)S(1)}, bf16[192,768]{1,0:T(8,128)(2,1)}, u32[]{:S(2)}) copy-start(bf16[192,768]{1,0:T(8,128)(2,1)} %param.11) | copy-start | bytes 884740
  7.2 13.8 %copy-start.2 = (f32[192,6]{0,1:T(8,128)S(1)}, f32[192,6]{0,1:T(8,128)}, u32[]{:S(2)}) copy-start(f32[192,6]{0,1:T(8,128)} %param.15) | copy-start | bytes 13828
  7.2 77.1 %all-gather.5.cloned.1.call-start = ((), (), s32[]{:S(2)}) async-start(), calls=%async_computation.1 | async-start | bytes 2654208 | tf_op jit(solution)/shard_map/all_gather | solution.py:39
  7.9 111.4 %all-gather.7.cloned.1.call-start = ((), (), s32[]{:S(2)}) async-start(), calls=%async_computation.2 | async-start | bytes 2654208 | tf_op jit(solution)/shard_map/all_gather | solution.py:40
  18.9 64.5 %copy-start.1 = (bf16[192,768]{1,0:T(8,128)(2,1)S(1)}, bf16[192,768]{1,0:T(8,128)(2,1)}, u32[]{:S(2)}) copy-start(bf16[192,768]{1,0:T(8,128)(2,1)} %param.12) | copy-start | bytes 884740
  20.9 236.9 %reduce-scatter.2.cloned.1.call-start = ((), (), s32[]{:S(2)}) async-start(), calls=%async_computation.3 | async-start | bytes 5308416 | tf_op jit(solution)/shard_map/reduce_scatter | solution.py:96
Sparse Core Ops, SparseCore 0:
  10.2 55.5 all-gather.4
  68.6 50.7 all-gather.6
  163.9 93.7 reduce-scatter.1
where the time goes:
time: 267 us; the launch traced here: 266 us
  waiting for transfers between devices  126 us (47%)
  blocking collectives  70 us (26%)
  matrix products  26.6 us (10%)
  local copies, waits for them, and re-layouts  14.4 us (5%)
  between operations  13.8 us (5%)
  other arithmetic  13 us (5%)
    reduce_scatter x1, waiting for transfers between devices, body(): lax.psum_scatter(terms, 'seq', scatter_dimension=0, tiled=True)  90.3 us
    all_gather x1, waiting for transfers between devices, body(): lax.all_gather(dout, 'seq', axis=0, tiled=True)  35.1 us
    all_gather x1, blocking collectives, body(): lax.all_gather(log_norm, 'seq', axis=0, tiled=True)  31 us
    all_gather x1, blocking collectives, body(): lax.all_gather(delta, 'seq', axis=0, tiled=True)  30.7 us
    psum x1, blocking collectives, body(): total_dot = lax.psum(partial_dot, 'tp')  8.34 us
    dot_general x3, matrix products, step(): jnp.einsum('hqk,qhd->khd', prob_low, dout_part, preferred_element_type=jn...  6.47 us
    dot_general x3, matrix products, step(): jnp.einsum('hqk,qhd->khd', dscore, query_part, preferred_element_type=jnp...  6.1 us
    dot_general x3, matrix products, step(): jnp.einsum('qhd,khd->hqk', dout_part, local_value, preferred_element_type...  5.61 us
  transfers between devices with their start and end apart: 3, of which 2 were waited for; matrix products, arithmetic and copies ran while one was open for 4% of the time, Pallas kernels for 0%

commit v1 on v0

v1 whole, which is shorter than its diff:
```python
import functools
import math

import jax
import jax.numpy as jnp
from jax import lax
from jax.experimental import pallas as pl
from jax.experimental.pallas import tpu as pltpu
from jax.sharding import PartitionSpec as P


LANES = 128
PIECE = 8
GROUP = 4
ONE = 6 * GROUP
PACK = 4
TILE = 16
BIG = 1e30
VMEM = 24 * 1024 * 1024
HOME_FLOPS = 1024
PREP_VMEM = 63 * 1024 * 1024
F32 = jnp.float32
BF16 = jnp.bfloat16
NT = (((1,), (1,)), ((), ()))
NN = (((1,), (0,)), ((), ()))
TN = (((0,), (0,)), ((), ()))


def dot(left, right, dims):
    return lax.dot_general(left, right, dims, preferred_element_type=F32)


def pieces(rows):
    high = rows.astype(BF16).astype(F32)
    rest = rows - high
    middle = rest.astype(BF16).astype(F32)
    return [high, middle, rest - middle]


def split_exact(product):
    high = product.astype(BF16)
    return high, (product - high.astype(F32)).astype(BF16)


def used_slots(positions, shard, slots):
    table = positions[...]
    place = lax.broadcasted_iota(jnp.int32, table.shape, 0) * LANES
    place = place + lax.broadcasted_iota(jnp.int32, table.shape, 1)
    mine = (place >= shard * slots) & (place < (shard + 1) * slots) & (table >= 0)
    count = jnp.sum(jnp.where(mine, 1.0, 0.0), axis=1, keepdims=True)
    return jnp.sum(count, axis=0, keepdims=True)


def pack(ext):
    quarter = ext.shape[0] // PACK
    total = ext[:quarter]
    for part in range(1, PACK):
        rows = ext[part * quarter:(part + 1) * quarter]
        total = total + pltpu.roll(rows, part * LANES // PACK, 1)
    groups = [total[at:at + TILE] for at in range(0, quarter, TILE)]
    return jnp.concatenate(groups, axis=1).astype(BF16)


def unpack(packed):
    wide = packed.astype(F32)
    groups = [wide[:, at:at + LANES] for at in range(0, wide.shape[1], LANES)]
    total = jnp.concatenate(groups, axis=0)
    parts = [total]
    for part in range(1, PACK):
        parts.append(pltpu.roll(total, LANES - part * LANES // PACK, 1))
    return jnp.concatenate(parts, axis=0).astype(BF16)


def key_ext(positions, shard, slots):
    count = used_slots(positions, shard, slots)
    slot = lax.broadcasted_iota(jnp.int32, (slots, LANES), 0).astype(F32)
    lane = lax.broadcasted_iota(jnp.int32, (slots, LANES), 1)
    return jnp.where((lane == ONE) & (slot >= count), -BIG, 0.0).astype(BF16)


def prep_kernel(plan, heads, *refs):
    sources, (query, key, value), rest = refs[:5], refs[5:8], refs[8:]
    dots, outs, rest = rest[0], rest[1:len(plan) + 1], rest[len(plan) + 1:]
    held, (bank, sems, done) = rest[:5], rest[5:]
    output, grad, logit, norm, positions = held
    slots, width = grad.shape
    half = width // 2
    rows = 2 * slots + TILE
    copies = [
        pltpu.make_async_copy(source, dest, sems.at[i])
        for i, (source, dest) in enumerate(zip(sources, held))
    ]
    for at in range(2):
        for source, base in ((key, at), (value, at + 0.5), (query, at + 2)):
            first = int(base) * rows + (slots if base % 1 else 0)
            copies.append(
                pltpu.make_async_copy(
                    source.at[:, pl.ds(at * half, half)],
                    bank.at[pl.ds(first, slots), :],
                    sems.at[len(copies)],
                )
            )
    for copy in copies:
        copy.start()
    for copy in copies[:5]:
        copy.wait()
    head_dim = width // heads
    root = math.sqrt(head_dim)
    shard = lax.axis_index("seq")
    level = shard // 2
    count = used_slots(positions, shard, slots)
    lane = lax.broadcasted_iota(jnp.int32, (PIECE, slots), 1).astype(F32)
    used = lane < count
    gate_row = jax.nn.sigmoid(logit[...])
    gate = jnp.transpose(jnp.broadcast_to(gate_row, (LANES, slots)))
    head_of = lax.broadcasted_iota(jnp.int32, (PIECE, width), 1) // head_dim
    head_row = lax.broadcasted_iota(jnp.int32, (PIECE, width), 0)
    pick = (head_of == head_row).astype(BF16)
    ones = jnp.ones((PIECE, width), BF16)
    dout_parts, delta_parts, dot_parts = [], [], []
    for h in range(heads):
        cols = pl.ds(h * head_dim, head_dim)
        wide = grad[:, cols].astype(F32)
        out = output[:, cols].astype(F32)
        dout = (wide * gate).astype(BF16)
        dout_parts.append(dout)
        delta_parts.append(dout.astype(F32) * out)
        dot_parts.append(wide * out)
    delta_high, delta_low = split_exact(jnp.concatenate(delta_parts, axis=1))
    delta = dot(pick, delta_high, NT) + dot(pick, delta_low, NT)
    dot_high, dot_low = split_exact(jnp.concatenate(dot_parts, axis=1))
    dots[...] = (dot(ones, dot_high, NT) + dot(ones, dot_low, NT))[:1]

    pad = jnp.zeros((PIECE - heads, slots), F32)
    scaled = jnp.where(used, jnp.concatenate([norm[...] * root, pad], axis=0), BIG)
    delta = jnp.where(used, delta, 0.0)
    first = lax.broadcasted_iota(jnp.int32, (PIECE, slots), 0) == 0
    stack = pieces(scaled) + pieces(delta) + [jnp.where(first, 1.0, 0.0)]
    stack.append(jnp.zeros((PIECE * (PIECE - len(stack)), slots), F32))
    stats = jnp.concatenate(stack, axis=0).astype(BF16)
    source = lax.broadcasted_iota(jnp.int32, (PIECE * PIECE, LANES), 0)
    target = lax.broadcasted_iota(jnp.int32, (PIECE * PIECE, LANES), 1)
    piece, head = source // PIECE, source % PIECE

    def ext(first_head):
        local = head - first_head
        taken = (local >= 0) & (local < heads // 2) & (piece < 6)
        column = jnp.where(taken, piece * GROUP + local, -1)
        column = jnp.where(source == 6 * PIECE, ONE, column)
        return dot(stats, (column == target).astype(BF16), TN)

    per = heads // 2
    for at in range(2):
        bank[pl.ds(at * rows + 2 * slots, TILE), :] = jnp.zeros((TILE, half), BF16)
        base = (2 + at) * rows
        bank[pl.ds(base + slots, slots), :] = jnp.concatenate(
            dout_parts[at * per:(at + 1) * per], axis=1
        )
        bank[pl.ds(base + 2 * slots, TILE), :] = pack(ext(at * per))
    for copy in copies[5:]:
        copy.wait()
    moves = []
    for out, blocks in zip(outs, plan):
        for place, block in enumerate(blocks(level)):
            start = pl.multiple_of(jnp.int32(block) * rows, TILE)
            moves.append(
                pltpu.make_async_copy(
                    bank.at[pl.ds(start, rows), :],
                    out.at[pl.ds(place * rows, rows), :],
                    done.at[len(moves)],
                )
            )
    for move in moves:
        move.start()
    for move in moves:
        move.wait()


def head_marks(head, is_value):
    lane = lax.broadcasted_iota(jnp.int32, (1, LANES), 1)
    base = (3 * GROUP if is_value else 0) + head
    marked = (lane == base) | (lane == base + GROUP) | (lane == base + 2 * GROUP)
    return jnp.where(marked, -1.0, 0.0).astype(BF16)


def meet(down, movings, stays, positions, heads, mask, emit, add):
    half = movings[0][0].shape[1]
    slots = emit.slots
    head_dim = half // (heads // 2)
    scale = head_dim ** -0.5
    to_log2 = scale * math.log2(math.e)

    def stats(blocks, queries):
        parts = []
        for ref, at, shard in blocks:
            if queries:
                parts.append(unpack(ref[pl.ds(at + 2 * slots, TILE), :]))
            else:
                parts.append(key_ext(positions, shard, slots))
        return jnp.concatenate(parts, axis=0)

    def load(blocks, which, cols):
        parts = [ref[pl.ds(at + which * slots, slots), cols] for ref, at, _ in blocks]
        return jnp.concatenate(parts, axis=0)

    moving_ext, stay_ext = stats(movings, down), stats(stays, not down)
    for h in range(heads // 2):
        cols = pl.ds(h * head_dim, head_dim)
        m1, m2 = load(movings, 0, cols), load(movings, 1, cols)
        r1, r2 = load(stays, 0, cols), load(stays, 1, cols)
        key_mark, value_mark = head_marks(h, False), head_marks(h, True)
        if down:
            m1_ext, m2_ext = moving_ext, moving_ext
            r1_ext = stay_ext + key_mark
            r2_ext = jnp.broadcast_to(value_mark, stay_ext.shape)
        else:
            m1_ext = moving_ext + key_mark
            m2_ext = jnp.broadcast_to(value_mark, moving_ext.shape)
            r1_ext, r2_ext = stay_ext, stay_ext
        scores = dot(
            jnp.concatenate([m1, m1_ext], axis=1), jnp.concatenate([r1, r1_ext], axis=1), NT
        )
        if mask is not None:
            scores = jnp.where(mask, scores, -BIG)
        prob = jnp.exp2(scores * to_log2)
        dprob = dot(
            jnp.concatenate([m2, m2_ext], axis=1), jnp.concatenate([r2, r2_ext], axis=1), NT
        )
        dscore = (prob * dprob * scale).astype(BF16)
        prob = prob.astype(BF16)
        emit(0, cols, dot(dscore, r1, NN))
        add(0, cols, dot(dscore, m1, TN))
        if down:
            add(1, cols, dot(prob, m2, TN))
        else:
            emit(1, cols, dot(prob, r2, NN))


class Store:
    def __init__(self, slots, targets, fresh):
        self.slots, self.targets, self.fresh = slots, targets, fresh

    def __call__(self, which, cols, term):
        for i, (ref, base) in enumerate(self.targets):
            rows = pl.ds(base + which * self.slots, self.slots)
            part = term[i * self.slots:(i + 1) * self.slots]
            part = part if self.fresh else ref[rows, cols] + part
            ref[rows, cols] = part.astype(ref.dtype)


def causal(down, slots, shard=None):
    shape = (slots, slots if shard is None else 2 * slots)
    row = lax.broadcasted_iota(jnp.int32, shape, 0)
    place = lax.broadcasted_iota(jnp.int32, shape, 1)
    if shard is not None:
        place = jnp.where(place < slots, place, slots - shard % 2 * (slots + 1))
    return place <= row if down else place >= row


def router_part(positions, logit, dots, slots, shard):
    gate = jax.nn.sigmoid(logit[...])
    lane = lax.broadcasted_iota(jnp.int32, (1, slots), 1).astype(F32)
    used = lane < used_slots(positions, shard, slots)
    return jnp.where(used, gate * (1.0 - gate) * dots[...], 0.0)


FOUR_PLAN = (
    lambda level: [jnp.where(level < 2, 0, 2), jnp.where(level < 2, 1, 3)],
    lambda level: [jnp.where(level < 2, 2, 0), jnp.where(level < 2, 3, 1)],
    lambda level: [jnp.where(level % 2 == 0, 0, 3)],
    lambda level: [jnp.where(level < 2, 1, 2)],
)


def gate_kernel(*refs):
    pass


def four_home_kernel(heads, positions, mine, own, grads, own_total):
    slots = grads.shape[0] // 4
    rows = 2 * slots + TILE
    shard = lax.axis_index("seq")
    for down in (True, False):

        @pl.when((shard < 4) == down)
        def _():
            for at in range(2):
                base = 2 * slots * at
                meet(
                    down, [(mine, at * rows, shard)], [(own, at * rows, shard)],
                    positions, heads, causal(down, slots),
                    Store(slots, [(grads, base)], True),
                    Store(slots, [(own_total, base)], True),
                )


def four_guest_kernel(
    heads, positions, dots_in, mine, near, cross, grads_in, grads, near_total, cross_total, dots
):
    slots = grads.shape[0] // 4
    rows = 2 * slots + TILE
    shard = lax.axis_index("seq")
    grads[...] = grads_in[...]
    dots[...] = dots_in[...]
    for level in (1, 2):
        at = level - 1

        @pl.when(shard // 2 == level)
        def _():
            meet(
                level == 1, [(mine, at * rows, shard)],
                [(near, 0, shard - 2), (cross, 0, (shard - 2) ^ 1)],
                positions, heads, None,
                Store(slots, [(grads, 2 * slots * at)], False),
                Store(slots, [(near_total, 0), (cross_total, 0)], True),
            )


def four_pair_kernel(
    heads, positions, mine, own, other, near, grads_in, own_in, grads, own_total, other_total, back
):
    slots = grads.shape[0] // 4
    rows = 2 * slots + TILE
    shard = lax.axis_index("seq")
    grads[...] = grads_in[...]
    own_total[...] = own_in[...]
    other_total[...] = jnp.zeros(other_total.shape, F32)
    for down in (True, False):

        @pl.when(((shard < 4) == down) & (shard % 2 == int(down)))
        def _():
            for at in range(2):
                base = 2 * slots * at
                meet(
                    down, [(mine, at * rows, shard)], [(other, at * rows, shard ^ 1)],
                    positions, heads, None,
                    Store(slots, [(grads, base)], False),
                    Store(slots, [(other_total, base)], True),
                )

    for level in (0, 3):
        at = 1 if level == 0 else 0
        base = 2 * slots * at

        @pl.when(shard // 2 == level)
        def _():
            meet(
                level == 0, [(near, 0, shard - 2)],
                [(own, at * rows, shard), (other, at * rows, shard ^ 1)],
                positions, heads, None,
                Store(slots, [(back, 0)], True),
                Store(slots, [(own_total, base), (other_total, base)], False),
            )


def four_far_meet(heads, level, block, reach, refs, positions, back, totals):
    own, other, near, cross = refs
    slots = back.shape[0] // 2
    at = (level - 1) * (2 * slots + TILE)
    shard = lax.axis_index("seq")
    meet(
        level == 1, [(block, 0, shard - 2 * reach)],
        [
            (own, at, shard), (other, at, shard ^ 1),
            (near, 0, shard - 2), (cross, 0, (shard - 2) ^ 1),
        ],
        positions, heads, None,
        Store(slots, [(back, 0)], True),
        Store(slots, [(ref, 0) for ref in totals], reach == 1),
    )


def four_middle_kernel(heads, positions, own, other, near, cross, middle, back, *totals):
    for level in (1, 2):

        @pl.when(lax.axis_index("seq") // 2 == level)
        def _():
            four_far_meet(
                heads, level, middle, 1, (own, other, near, cross), positions, back, totals
            )


def four_far_kernel(
    heads, positions, logit, dots, own, other, near, cross, skip,
    own_in, other_in, near_in, cross_in, own_mid, other_mid, near_mid, cross_mid, step_back,
    own_total, other_low, near_low, cross_low, skip_back, router, *totals
):
    slots = near_in.shape[0] // 2
    shard = lax.axis_index("seq")
    own_total[...] = own_in[...]
    other_low[...] = other_in[...].astype(BF16)
    router[...] = router_part(positions, logit, dots, slots, shard)
    inner = (shard >= 2) & (shard < 6)

    @pl.when(jnp.logical_not(inner))
    def _():
        near_low[...] = step_back[...]

    for level in (1, 2):
        part = pl.ds(2 * slots * (level - 1), 2 * slots)

        @pl.when(shard // 2 == level)
        def _():
            totals[0][...] = own_in[part, :] + own_mid[...]
            totals[1][...] = other_in[part, :] + other_mid[...]
            totals[2][...] = near_in[...] + near_mid[...]
            totals[3][...] = cross_in[...] + cross_mid[...]
            four_far_meet(
                heads, level, skip, 2, (own, other, near, cross), positions, skip_back, totals
            )
            own_total[part, :] = totals[0][...]
            other_low[part, :] = totals[1][...].astype(BF16)
            near_low[...] = totals[2][...].astype(BF16)
            cross_low[...] = totals[3][...].astype(BF16)


def four_join_kernel(
    heads, grads, own, other, near, cross, middle, skip, query_grad, key_grad, value_grad
):
    slots, half = grads.shape[0] // 4, grads.shape[1]
    shard = lax.axis_index("seq")

    def part(ref, at, which):
        return ref[pl.ds((2 * at + which) * slots, slots), :].astype(F32)

    def first(refs, which):
        return sum(part(ref, 0, which) for ref in refs)

    for down in (True, False):

        @pl.when((shard < 4) == down)
        def _():
            guest, late = (0, 1) if down else (1, 0)
            inner = (shard >= 2) & (shard < 6)
            for at in range(2):
                cols = pl.ds(at * half, half)
                extra = [cross] if at == guest else [middle, skip]
                if down:
                    moving, staying = [query_grad], [key_grad, value_grad]
                else:
                    moving, staying = [key_grad, value_grad], [query_grad]
                for which, out in enumerate(moving):
                    total = part(grads, at, which)
                    if at == late:
                        total = total + jnp.where(inner, part(near, 0, which), 0.0)
                    out[:, cols] = total.astype(BF16)
                for which, out in enumerate(staying):
                    total = part(own, at, which) + part(other, at, which) + first(extra, which)
                    if at == guest:
                        total = total + jnp.where(inner, 0.0, part(near, 0, which))
                    out[:, cols] = total.astype(BF16)


def four_levels(prep, shape, positions, logit, slots, heads, width):
    double, block, total = shape(4 * slots + 2 * TILE), shape(2 * slots + TILE), shape(2 * slots, F32)
    totals, low = shape(4 * slots, F32), shape(2 * slots)
    own, mine, near_send, far_send, dots = prep(FOUR_PLAN, [double, double, block, block])
    near_send, far_send = call(
        gate_kernel, [block, block], near_send, far_send,
        ins=[pltpu.HBM] * 2, outs=[pltpu.HBM] * 2, aliases={0: 0, 1: 1},
    )

    def pairs(levels, flip=0):
        return [(2 * a + c, 2 * b + (c ^ flip)) for a, b in levels for c in range(2)]

    near = lax.ppermute(near_send, "seq", pairs([(0, 1), (1, 0), (2, 3), (3, 2)]))
    cross = lax.ppermute(near_send, "seq", pairs([(0, 1), (3, 2)], 1))
    other = lax.ppermute(own, "seq", pairs([(i, i) for i in range(4)], 1))
    middle = lax.ppermute(far_send, "seq", pairs([(1, 2), (2, 1)]))
    skip = lax.ppermute(far_send, "seq", pairs([(0, 2), (3, 1)]))
    grads, own_total = call(
        functools.partial(four_home_kernel, heads),
        [totals] * 2,
        positions, mine, own,
        flops=HOME_FLOPS,
    )
    grads, near_total, cross_total, dots = call(
        functools.partial(four_guest_kernel, heads),
        [totals, total, total, shape(1, F32, slots)],
        positions, dots, mine, near, cross, grads,
    )
    dots = sum_over(dots, "tp")
    grads, own_total, other_total, step_back = call(
        functools.partial(four_pair_kernel, heads),
        [totals] * 3 + [low],
        positions, mine, own, other, near, grads, own_total,
    )
    middle_back, *middles = call(
        functools.partial(four_middle_kernel, heads),
        [low] + [total] * 4,
        positions, own, other, near, cross, middle,
    )
    own_total, other_low, near_low, cross_low, skip_back, router = call(
        functools.partial(four_far_kernel, heads),
        [totals, shape(4 * slots), low, low, low, shape(1, F32, slots)],
        positions, logit, dots, own, other, near, cross, skip,
        own_total, other_total, near_total, cross_total, *middles, step_back,
        scratch=[pltpu.VMEM(total.shape, F32)] * 4,
    )
    near = lax.ppermute(near_low, "seq", pairs([(0, 1), (1, 0), (2, 3), (3, 2)]))
    cross = lax.ppermute(cross_low, "seq", pairs([(1, 0), (2, 3)], 1))
    skip = lax.ppermute(skip_back, "seq", pairs([(2, 0), (1, 3)]))
    middle = lax.ppermute(middle_back, "seq", pairs([(1, 2), (2, 1)]))
    other = lax.ppermute(other_low, "seq", pairs([(i, i) for i in range(4)], 1))
    outs = call(
        functools.partial(four_join_kernel, heads),
        [shape(slots, BF16, width)] * 3,
        grads, own_total, other, near, cross, middle, skip,
    )
    return *outs, router


def ring_plan(levels):
    sends = [
        lambda level, step=step: [jnp.where(level >= step, 2, 1)] for step in range(1, levels)
    ]
    return (lambda level: [0, 3], lambda level: [2], lambda level: [1], *sends)


def ring_home_kernel(
    heads, positions, logit, dots, down, up, own, other, grads, own_total, other_total, router
):
    slots = grads.shape[0] // 3
    rows = 2 * slots + TILE
    shard = lax.axis_index("seq")
    for goes_down, mine, at, base, stay_base in ((True, down, 0, 0, 0), (False, up, rows, 1, 2)):
        meet(
            goes_down, [(mine, 0, shard)], [(own, at, shard), (other, at, shard ^ 1)],
            positions, heads, causal(goes_down, slots, shard),
            Store(slots, [(grads, base * slots)], True),
            Store(slots, [(own_total, stay_base * slots), (other_total, stay_base * slots)], True),
        )
    router[...] = router_part(positions, logit, dots, slots, shard)


def ring_away_kernel(
    step, levels, heads, positions, own, other, block, own_in, other_in,
    back, own_total, other_total, *low
):
    slots = own_in.shape[0] // 3
    own_total[...] = own_in[...]
    other_total[...] = other_in[...]
    rows = 2 * slots + TILE
    shard = lax.axis_index("seq")
    for goes_down, at, base in ((True, 0, 0), (False, rows, 2 * slots)):

        @pl.when((shard // 2 + step < levels) == goes_down)
        def _():
            meet(
                goes_down, [(block, 0, shard + 2 * (step - levels))],
                [(own, at, shard), (other, at, shard ^ 1)],
                positions, heads, None,
                Store(slots, [(back, 0)], True),
                Store(slots, [(own_total, base), (other_total, base)], False),
            )

    for ref in low:
        ref[...] = other_total[...].astype(BF16)


def ring_join_kernel(heads, grads, own, other, *refs):
    back, (query_grad, key_grad, value_grad) = refs[:-3], refs[-3:]
    slots, half = grads.shape[0] // 3, grads.shape[1]
    level = lax.axis_index("seq") // 2
    low, high = pl.ds(0, half), pl.ds(half, half)
    parts = [pl.ds(i * slots, slots) for i in range(3)]
    stays = [(own[rows, :] + other[rows, :].astype(F32)).astype(BF16) for rows in parts]
    key_grad[:, low], value_grad[:, low], query_grad[:, high] = stays
    query_sum, key_sum, value_sum = [grads[rows, :] for rows in parts]
    for step, ref in enumerate(back, 1):
        went_down = level >= step
        first, second = ref[parts[0], :].astype(F32), ref[parts[1], :].astype(F32)
        query_sum = query_sum + jnp.where(went_down, first, 0.0)
        key_sum = key_sum + jnp.where(went_down, 0.0, first)
        value_sum = value_sum + jnp.where(went_down, 0.0, second)
    query_grad[:, low] = query_sum.astype(BF16)
    key_grad[:, high] = key_sum.astype(BF16)
    value_grad[:, high] = value_sum.astype(BF16)


def ring_levels(prep, shape, positions, logit, slots, heads, width, shards):
    levels = shards // 2
    block, total = shape(2 * slots + TILE), shape(3 * slots, F32)
    own, down, up, *sends, dots = prep(
        ring_plan(levels), [shape(4 * slots + 2 * TILE)] + [block] * (levels + 1)
    )
    pair = [(s, s ^ 1) for s in range(shards)]
    arrived = [
        lax.ppermute(send, "seq", [(s, (s - 2 * step) % shards) for s in range(shards)])
        for step, send in enumerate(sends, 1)
    ]
    other = lax.ppermute(own, "seq", pair)
    dots = sum_over(dots, "tp")
    grads, own_total, other_total, router = call(
        functools.partial(ring_home_kernel, heads),
        [total] * 3 + [shape(1, F32, slots)],
        positions, logit, dots, down, up, own, other,
    )
    backs, low = [], [other_total.astype(BF16)]
    for step, arrival in enumerate(arrived, 1):
        back, own_total, other_total, *low = call(
            functools.partial(ring_away_kernel, step, levels, heads),
            [shape(2 * slots), total, total] + [shape(3 * slots)] * (step == levels - 1),
            positions, own, other, arrival, own_total, other_total,
            )
        backs.append(
            lax.ppermute(back, "seq", [(s, (s + 2 * step) % shards) for s in range(shards)])
        )
    outs = call(
        functools.partial(ring_join_kernel, heads),
        [shape(slots, BF16, width)] * 3,
        grads, own_total, lax.ppermute(low[0], "seq", pair), *backs,
    )
    return *outs, router


def call(kernel, out_shape, *args, scratch=(), ins=None, outs=None, limit=VMEM, flops=1024, aliases=None):
    ins = ins or [pltpu.VMEM] * len(args)
    outs = outs or [pltpu.VMEM] * len(out_shape)
    return pl.pallas_call(
        kernel,
        out_shape=out_shape,
        in_specs=[pl.BlockSpec(memory_space=space) for space in ins],
        out_specs=[pl.BlockSpec(memory_space=space) for space in outs],
        scratch_shapes=list(scratch),
        input_output_aliases=aliases or {},
        compiler_params=pltpu.CompilerParams(vmem_limit_bytes=limit),
        cost_estimate=pl.CostEstimate(flops=flops, bytes_accessed=1024, transcendentals=0),
    )(*args)


def sum_over(values, axis):
    size = lax.axis_size(axis)
    if size & (size - 1):
        return lax.psum(values, axis)
    reach = 1
    while reach < size:
        pairs = [(i, i ^ reach) for i in range(size)]
        values = values + lax.ppermute(values, axis, pairs)
        reach *= 2
    return values


def body(
    query_proj, key_proj, value_proj, attn_output, out_grad, log_norm, router_logit, keep_positions
):
    slots, width = query_proj.shape
    heads = log_norm.shape[1]
    half = width // 2
    shards = lax.axis_size("seq")
    logit = router_logit.reshape(1, slots)
    positions = keep_positions.reshape(-1, LANES)

    def shape(rows, dtype=BF16, columns=half):
        return jax.ShapeDtypeStruct((rows, columns), dtype)

    sources = (
        attn_output, out_grad, logit, log_norm.T, positions, query_proj, key_proj, value_proj
    )

    def prep(plan, shapes):
        dots, *outs = call(
            functools.partial(prep_kernel, plan, heads),
            [shape(1, F32, slots)] + shapes,
            *sources,
            scratch=[pltpu.VMEM(a.shape, a.dtype) for a in sources[:5]]
            + [pltpu.VMEM((4 * (2 * slots + TILE), half), BF16)]
            + [pltpu.SemaphoreType.DMA((11,)), pltpu.SemaphoreType.DMA((2 * len(plan),))],
            ins=[pltpu.HBM] * len(sources),
            outs=[pltpu.VMEM] + [pltpu.HBM] * len(shapes),
            limit=PREP_VMEM,
        )
        return *outs, dots

    if shards == 8:
        query_grad, key_grad, value_grad, router = four_levels(
            prep, shape, positions, logit, slots, heads, width
        )
    else:
        query_grad, key_grad, value_grad, router = ring_levels(
            prep, shape, positions, logit, slots, heads, width, shards
        )
    return query_grad, key_grad, value_grad, router.reshape(slots)


def solution(mesh):
    wide = P("seq", "tp")
    return jax.shard_map(
        body,
        mesh=mesh,
        in_specs=(wide,) * 6 + (P("seq"), P()),
        out_specs=(wide, wide, wide, P("seq")),
        check_vma=False,
    )
```

time: 267 us -> 61.6 us (0.23)
  waiting for transfers between devices: 126 us -> 21.1 us
  blocking collectives: 70 us -> 0 us
  starting transfers between devices: 0.12 us -> 27.1 us
  matrix products: 26.6 us -> 0 us
  other arithmetic: 13 us -> 0.01 us
  between operations: 13.8 us -> 0.82 us
  local copies, waits for them, and re-layouts: 14.4 us -> 2.16 us
  Pallas kernels: 0 us -> 10.1 us
    reduce_scatter x1 -> x0, waiting for transfers between devices: 90.3 us -> none  [body(): lax.psum_scatter(terms, 'seq', scatter_dimension=0, tiled=True)]
    all_gather x2 -> x0, blocking collectives: 61.7 us -> none  [the longest x1 31 us: body(): lax.all_gather(log_norm, 'seq', axis=0, tiled=True)]
    all_gather x2 -> x0, waiting for transfers between devices: 35.1 us -> none  [the longest x1 35.1 us: body(): lax.all_gather(dout, 'seq', axis=0, tiled=True)]
    ppermute x0 -> x12, starting transfers between devices: none -> 27.1 us  [the longest x1 7.38 us: four_levels(): lax.ppermute(near_low, 'seq', pairs([(0, 1), (1, 0), (2, 3), (3, 2)]))]
    dot_general x15 -> x0, matrix products: 26.6 us -> none  [the longest x3 6.47 us: step(): jnp.einsum('hqk,qhd->khd', prob_low, dout_part, preferred_element_type=jn...]
    ppermute x0 -> x12, waiting for transfers between devices: none -> 21.1 us  [the longest x1 5.56 us: four_levels(): cross = lax.ppermute(cross_low, 'seq', pairs([(1, 0), (2, 3)], 1))]
    pallas_call x0 -> x8, Pallas kernels: none -> 10.1 us  [call(): pl.pallas_call(kernel, out_shape=out_shape, in_specs=[pl.BlockSpec(memory...]
    psum x1 -> x0, blocking collectives: 8.34 us -> none  [body(): total_dot = lax.psum(partial_dot, 'tp')]
  transfers between devices with their start and end apart: 3 -> 12, of which waited for: 2 -> 6; matrix products, arithmetic and copies ran while one was open for 4% -> 0% of each run, Pallas kernels for 0% -> 7%
where the time goes in v1:
time: 61.6 us; the launch traced here: 61.3 us
  starting transfers between devices  27.1 us (44%)
  waiting for transfers between devices  21.1 us (34%)
  Pallas kernels  10.1 us (16%)
  local copies, waits for them, and re-layouts  2.16 us (4%)
  between operations  0.82 us (1%)
    pallas_call x8, Pallas kernels, call(): pl.pallas_call(kernel, out_shape=out_shape, in_specs=[pl.BlockSpec(memory...  10.1 us
    ppermute x1, starting transfers between devices, four_levels(): lax.ppermute(near_low, 'seq', pairs([(0, 1), (1, 0), (2, 3), (3, 2)]))  7.38 us
    ppermute x1, waiting for transfers between devices, four_levels(): cross = lax.ppermute(cross_low, 'seq', pairs([(1, 0), (2, 3)], 1))  5.56 us
    ppermute x1, starting transfers between devices, four_levels(): skip = lax.ppermute(far_send, 'seq', pairs([(0, 2), (3, 1)]))  5.15 us
    ppermute x1, waiting for transfers between devices, four_levels(): skip = lax.ppermute(skip_back, 'seq', pairs([(2, 0), (1, 3)]))  5.04 us
    ppermute x1, waiting for transfers between devices, four_levels(): lax.ppermute(near_low, 'seq', pairs([(0, 1), (1, 0), (2, 3), (3, 2)]))  4.65 us
    ppermute x2, waiting for transfers between devices, sum_over(): values = values + lax.ppermute(values, axis, pairs)  3.2 us
    ppermute x1, starting transfers between devices, four_levels(): other = lax.ppermute(own, 'seq', pairs([(i, i) for i in range(4)], 1))  3.03 us
  transfers between devices with their start and end apart: 12, of which 6 were waited for; matrix products, arithmetic and copies ran while one was open for 0% of the time, Pallas kernels for 7%

profile of v1, /device:TPU:0, one launch (start us, length us, event | category | flops | bytes accessed | tf_op | source)
XLA Modules:
  0.0 61.3 jit_solution(15256221282974010771)
XLA Ops:
  0.6 3.9 %shard_map.111 = (f32[1,192]{1,0:T(1,128)}, bf16[800,384]{1,0:T(8,128)(2,1)}, bf16[800,384]{1,0:T(8,128)(2,1)}, bf16[400,384]{1,0:T(8,128)(2,1)}, bf16[400,384]{1,0:T(8,128)(2,1)}) custom-call(bf16[192,768]{1,0:T(8,128)(2,1)} %refs_0_.1, bf16[192,768]{1,0:T(8,128)(2,1)} %refs_1_.1, f32[1,192]{1,0:T(1,128)} %bitcast.10, f32[6,192]{1,0:T(8,128)} %bitcast.12, ...), custom_call_target="tpu_custom_call" | custom-call | flops 1024 | bytes 1024 | tf_op jit(solution)/shard_map/pallas_call | solution.py:620
  4.6 0.0 copy-start.6
  4.6 3.0 %collective-permute-start = (bf16[800,384]{1,0:T(8,128)(2,1)}, bf16[800,384]{1,0:T(8,128)(2,1)S(1)}, u32[]{:S(2)}, u32[]{:S(2)}) collective-permute-start(bf16[800,384]{1,0:T(8,128)(2,1)} %get-tuple-element.36.own), channel_id=1, source_target_pairs={{0,4},{4,0},{8,12},{12,8},{16,20},{20,16},{24,28},{28,24},{1,5},{5... | collective-permute-start | bytes 1843208 | tf_op jit(solution)/shard_map/ppermute | solution.py:468
  7.6 1.6 %collective-permute-start.1 = (bf16[400,384]{1,0:T(8,128)(2,1)}, bf16[400,384]{1,0:T(8,128)(2,1)S(1)}, u32[]{:S(2)}, u32[]{:S(2)}) collective-permute-start(bf16[400,384]{1,0:T(8,128)(2,1)} %get-tuple-element.39), channel_id=1, source_target_pairs={{0,8},{4,12},{8,0},{12,4},{16,24},{20,28},{24,16},{28,20},{1,9},{5... | collective-permute-start | bytes 921608 | tf_op jit(solution)/shard_map/ppermute | solution.py:466
  9.2 1.9 %collective-permute-start.2 = (bf16[400,384]{1,0:T(8,128)(2,1)}, bf16[400,384]{1,0:T(8,128)(2,1)S(1)}, u32[]{:S(2)}, u32[]{:S(2)}) collective-permute-start(bf16[400,384]{1,0:T(8,128)(2,1)} %get-tuple-element.39), channel_id=1, source_target_pairs={{0,12},{4,8},{24,20},{28,16},{1,13},{5,9},{25,21},{29,17},{2,14},{... | collective-permute-start | bytes 921608 | tf_op jit(solution)/shard_map/ppermute | solution.py:467
  11.1 0.7 %collective-permute-start.6 = (bf16[400,384]{1,0:T(8,128)(2,1)}, bf16[400,384]{1,0:T(8,128)(2,1)S(1)}, u32[]{:S(2)}, u32[]{:S(2)}) collective-permute-start(bf16[400,384]{1,0:T(8,128)(2,1)} %get-tuple-element.46), channel_id=1, source_target_pairs={{8,16},{12,20},{16,8},{20,12},{9,17},{13,21},{17,9},{21,13},{10,18... | collective-permute-start | bytes 921608 | tf_op jit(solution)/shard_map/ppermute | solution.py:469
  11.8 5.1 %collective-permute-start.5 = (bf16[400,384]{1,0:T(8,128)(2,1)}, bf16[400,384]{1,0:T(8,128)(2,1)S(1)}, u32[]{:S(2)}, u32[]{:S(2)}) collective-permute-start(bf16[400,384]{1,0:T(8,128)(2,1)} %get-tuple-element.46), channel_id=1, source_target_pairs={{0,16},{4,20},{24,8},{28,12},{1,17},{5,21},{25,9},{29,13},{2,18},{... | collective-permute-start | bytes 921608 | tf_op jit(solution)/shard_map/ppermute | solution.py:470
  17.0 1.1 %copy-done = bf16[800,384]{1,0:T(8,128)(2,1)S(1)} copy-done((bf16[800,384]{1,0:T(8,128)(2,1)S(1)}, bf16[800,384]{1,0:T(8,128)(2,1)}, u32[]{:S(2)}) %copy-start) | copy-done | bytes 614424
  18.0 1.1 %copy-done.2 = bf16[800,384]{1,0:T(8,128)(2,1)S(1)} copy-done((bf16[800,384]{1,0:T(8,128)(2,1)S(1)}, bf16[800,384]{1,0:T(8,128)(2,1)}, u32[]{:S(2)}) %copy-start.2) | copy-done | bytes 614424
  19.1 2.1 %shard_map.113 = (f32[768,384]{1,0:T(8,128)S(1)}, f32[768,384]{1,0:T(8,128)S(1)}) custom-call(s32[12,128]{1,0:T(8,128)S(1)} %bitcast.5, bf16[800,384]{1,0:T(8,128)(2,1)S(1)} %copy-done.2, bf16[800,384]{1,0:T(8,128)(2,1)S(1)} %copy-done), custom_call_target="tpu_custom_call" | custom-call | flops 1024 | bytes 1024 | tf_op jit(solution)/shard_map/pallas_call | solution.py:620
  21.2 2.7 %collective-permute-done.2.cross = bf16[400,384]{1,0:T(8,128)(2,1)S(1)} collective-permute-done((bf16[400,384]{1,0:T(8,128)(2,1)}, bf16[400,384]{1,0:T(8,128)(2,1)S(1)}, u32[]{:S(2)}, u32[]{:S(2)}) %collective-permute-start.2) | collective-permute-done | bytes 307232 | tf_op jit(solution)/shard_map/ppermute | solution.py:467
  23.9 0.1 shard_map.114
  24.0 0.1 collective-permute-start.3
  24.1 1.1 %collective-permute-done.3 = f32[1,192]{1,0:T(1,128)S(1)} collective-permute-done((f32[1,192]{1,0:T(1,128)S(1)}, f32[1,192]{1,0:T(1,128)S(1)}, u32[]{:S(2)}, u32[]{:S(2)}) %collective-permute-start.3) | collective-permute-done | bytes 800 | tf_op jit(solution)/shard_map/ppermute | solution.py:639
  25.2 1.5 %collective-permute-start.4 = (f32[1,192]{1,0:T(1,128)S(1)}, f32[1,192]{1,0:T(1,128)S(1)}, u32[]{:S(2)}, u32[]{:S(2)}) collective-permute-start(f32[1,192]{1,0:T(1,128)S(1)} %add.6), channel_id=1, source_target_pairs={{0,2},{1,3},{2,0},{3,1},{4,6},{5,7},{6,4},{7,5},{8,10},{9,11},{10,... | collective-permute-start | bytes 2312 | tf_op jit(solution)/shard_map/ppermute | solution.py:639
  26.7 2.1 %collective-permute-done.4 = f32[1,192]{1,0:T(1,128)S(1)} collective-permute-done((f32[1,192]{1,0:T(1,128)S(1)}, f32[1,192]{1,0:T(1,128)S(1)}, u32[]{:S(2)}, u32[]{:S(2)}) %collective-permute-start.4) | collective-permute-done | bytes 800 | tf_op jit(solution)/shard_map/ppermute | solution.py:639
  28.8 0.0 collective-permute-done.6.middle
  28.8 0.0 collective-permute-done.other
  28.8 0.0 copy-start.5
  28.8 1.9 %shard_map.115 = (f32[768,384]{1,0:T(8,128)S(1)}, f32[768,384]{1,0:T(8,128)S(1)}, f32[768,384]{1,0:T(8,128)S(1)}, bf16[384,384]{1,0:T(8,128)(2,1)S(1)}) custom-call(s32[12,128]{1,0:T(8,128)S(1)} %bitcast.8, bf16[800,384]{1,0:T(8,128)(2,1)S(1)} %copy-done.3, bf16[800,384]{1,0:T(8,128)(2,1)S(1)} %copy-done.1, bf16[800,384]{1,0:T(8,128)(2,1)S(1)} %collective-permute-done.other, ...), custom_call_target="tpu_custom_call" | custom-call | flops 1024 | bytes 1024 | tf_op jit(solution)/shard_map/pallas_call | solution.py:620
  30.7 0.0 collective-permute-done.5.skip
  30.7 0.8 %shard_map.117 = (f32[768,384]{1,0:T(8,128)S(1)}, bf16[768,384]{1,0:T(8,128)(2,1)S(1)}, bf16[384,384]{1,0:T(8,128)(2,1)S(1)}, bf16[384,384]{1,0:T(8,128)(2,1)S(1...) custom-call(s32[12,128]{1,0:T(8,128)S(1)} %bitcast.9, f32[1,192]{1,0:T(1,128)S(1)} %bitcast.11, f32[1,192]{1,0:T(1,128)S(1)} %add.7.dots, ...), custom_call_target="tpu_custom_call" | custom-call | flops 1024 | bytes 1024 | tf_op jit(solution)/shard_map/pallas_call | solution.py:620
  31.5 2.6 %collective-permute-start.7 = (bf16[768,384]{1,0:T(8,128)(2,1)S(1)}, bf16[768,384]{1,0:T(8,128)(2,1)S(1)}, u32[]{:S(2)}, u32[]{:S(2)}) collective-permute-start(bf16[768,384]{1,0:T(8,128)(2,1)S(1)} %get-tuple-element.57), channel_id=1, source_target_pairs={{0,4},{4,0},{8,12},{12,8},{16,20},{20,16},{24,28},{28,24},{1,5},{5... | collective-permute-start | bytes 1769480 | tf_op jit(solution)/shard_map/ppermute | solution.py:504
  34.1 7.4 %collective-permute-start.8 = (bf16[384,384]{1,0:T(8,128)(2,1)S(1)}, bf16[384,384]{1,0:T(8,128)(2,1)S(1)}, u32[]{:S(2)}, u32[]{:S(2)}) collective-permute-start(bf16[384,384]{1,0:T(8,128)(2,1)S(1)} %get-tuple-element.58), channel_id=1, source_target_pairs={{0,8},{4,12},{8,0},{12,4},{16,24},{20,28},{24,16},{28,20},{1,9},{5... | collective-permute-start | bytes 884744 | tf_op jit(solution)/shard_map/ppermute | solution.py:500
  41.5 1.3 %collective-permute-start.9 = (bf16[384,384]{1,0:T(8,128)(2,1)S(1)}, bf16[384,384]{1,0:T(8,128)(2,1)S(1)}, u32[]{:S(2)}, u32[]{:S(2)}) collective-permute-start(bf16[384,384]{1,0:T(8,128)(2,1)S(1)} %get-tuple-element.59), channel_id=1, source_target_pairs={{8,4},{12,0},{16,28},{20,24},{9,5},{13,1},{17,29},{21,25},{10,6},{... | collective-permute-start | bytes 884744 | tf_op jit(solution)/shard_map/ppermute | solution.py:501
  42.8 0.7 %collective-permute-start.10 = (bf16[384,384]{1,0:T(8,128)(2,1)S(1)}, bf16[384,384]{1,0:T(8,128)(2,1)S(1)}, u32[]{:S(2)}, u32[]{:S(2)}) collective-permute-start(bf16[384,384]{1,0:T(8,128)(2,1)S(1)} %get-tuple-element.60), channel_id=1, source_target_pairs={{8,16},{12,20},{16,8},{20,12},{9,17},{13,21},{17,9},{21,13},{10,18... | collective-permute-start | bytes 884744 | tf_op jit(solution)/shard_map/ppermute | solution.py:503
  43.5 1.3 %collective-permute-start.11 = (bf16[384,384]{1,0:T(8,128)(2,1)S(1)}, bf16[384,384]{1,0:T(8,128)(2,1)S(1)}, u32[]{:S(2)}, u32[]{:S(2)}) collective-permute-start(bf16[384,384]{1,0:T(8,128)(2,1)S(1)} %get-tuple-element.61), channel_id=1, source_target_pairs={{16,0},{20,4},{8,24},{12,28},{17,1},{21,5},{9,25},{13,29},{18,2},{... | collective-permute-start | bytes 884744 | tf_op jit(solution)/shard_map/ppermute | solution.py:502
  44.8 4.6 %collective-permute-done.8.near = bf16[384,384]{1,0:T(8,128)(2,1)S(1)} collective-permute-done((bf16[384,384]{1,0:T(8,128)(2,1)S(1)}, bf16[384,384]{1,0:T(8,128)(2,1)S(1)}, u32[]{:S(2)}, u32[]{:S(2)}) %collective-permute-start.8) | collective-permute-done | bytes 294944 | tf_op jit(solution)/shard_map/ppermute | solution.py:500
  49.4 5.6 %collective-permute-done.9.cross = bf16[384,384]{1,0:T(8,128)(2,1)S(1)} collective-permute-done((bf16[384,384]{1,0:T(8,128)(2,1)S(1)}, bf16[384,384]{1,0:T(8,128)(2,1)S(1)}, u32[]{:S(2)}, u32[]{:S(2)}) %collective-permute-start.9) | collective-permute-done | bytes 294944 | tf_op jit(solution)/shard_map/ppermute | solution.py:501
  55.0 0.0 collective-permute-done.10.middle
  55.0 5.0 %collective-permute-done.11.skip = bf16[384,384]{1,0:T(8,128)(2,1)S(1)} collective-permute-done((bf16[384,384]{1,0:T(8,128)(2,1)S(1)}, bf16[384,384]{1,0:T(8,128)(2,1)S(1)}, u32[]{:S(2)}, u32[]{:S(2)}) %collective-permute-start.11) | collective-permute-done | bytes 294944 | tf_op jit(solution)/shard_map/ppermute | solution.py:502
  60.0 1.3 %shard_map.118 = (bf16[192,768]{1,0:T(8,128)(2,1)}, bf16[192,768]{1,0:T(8,128)(2,1)}, bf16[192,768]{1,0:T(8,128)(2,1)}) custom-call(f32[768,384]{1,0:T(8,128)S(1)} %get-tuple-element.44.grads, f32[768,384]{1,0:T(8,128)S(1)} %get-tuple-element.56.own, bf16[768,384]{1,0:T(8,128)(2,1)S(1)} %collective-permute-done.7.other, ...), custom_call_target="tpu_custom_call" | custom-call | flops 1024 | bytes 1024 | tf_op jit(solution)/shard_map/pallas_call | solution.py:620
  (16 shorter events, 0.1 us)
Async XLA Ops:
  0.6 16.3 %copy-start.4 = (s32[1536]{0:T(1024)S(1)}, s32[1536]{0:T(1024)}, u32[]{:S(2)}) copy-start(s32[1536]{0:T(1024)} %param.15) | copy-start | bytes 18436
  4.6 19.3 %copy-start.3 = (bf16[800,384]{1,0:T(8,128)(2,1)S(1)}, bf16[800,384]{1,0:T(8,128)(2,1)}, u32[]{:S(2)}) copy-start(bf16[800,384]{1,0:T(8,128)(2,1)} %get-tuple-element.35.mine) | copy-start | bytes 1843204
  4.6 19.3 %copy-start.6 = (f32[1,192]{1,0:T(1,128)S(1)}, f32[1,192]{1,0:T(1,128)}, u32[]{:S(2)}) copy-start(f32[1,192]{1,0:T(1,128)} %get-tuple-element.40.dots_in) | copy-start | bytes 2308
  4.6 24.2 %collective-permute-start = (bf16[800,384]{1,0:T(8,128)(2,1)}, bf16[800,384]{1,0:T(8,128)(2,1)S(1)}, u32[]{:S(2)}, u32[]{:S(2)}) collective-permute-start(bf16[800,384]{1,0:T(8,128)(2,1)} %get-tuple-element.36.own), channel_id=1, source_target_pairs={{0,4},{4,0},{8,12},{12,8},{16,20},{20,16},{24,28},{28,24},{1,5},{5... | collective-permute-start | bytes 1843208 | tf_op jit(solution)/shard_map/ppermute | solution.py:468
  7.6 13.6 %collective-permute-start.1 = (bf16[400,384]{1,0:T(8,128)(2,1)}, bf16[400,384]{1,0:T(8,128)(2,1)S(1)}, u32[]{:S(2)}, u32[]{:S(2)}) collective-permute-start(bf16[400,384]{1,0:T(8,128)(2,1)} %get-tuple-element.39), channel_id=1, source_target_pairs={{0,8},{4,12},{8,0},{12,4},{16,24},{20,28},{24,16},{28,20},{1,9},{5... | collective-permute-start | bytes 921608 | tf_op jit(solution)/shard_map/ppermute | solution.py:466
  9.2 14.7 %collective-permute-start.2 = (bf16[400,384]{1,0:T(8,128)(2,1)}, bf16[400,384]{1,0:T(8,128)(2,1)S(1)}, u32[]{:S(2)}, u32[]{:S(2)}) collective-permute-start(bf16[400,384]{1,0:T(8,128)(2,1)} %get-tuple-element.39), channel_id=1, source_target_pairs={{0,12},{4,8},{24,20},{28,16},{1,13},{5,9},{25,21},{29,17},{2,14},{... | collective-permute-start | bytes 921608 | tf_op jit(solution)/shard_map/ppermute | solution.py:467
  11.1 17.6 %collective-permute-start.6 = (bf16[400,384]{1,0:T(8,128)(2,1)}, bf16[400,384]{1,0:T(8,128)(2,1)S(1)}, u32[]{:S(2)}, u32[]{:S(2)}) collective-permute-start(bf16[400,384]{1,0:T(8,128)(2,1)} %get-tuple-element.46), channel_id=1, source_target_pairs={{8,16},{12,20},{16,8},{20,12},{9,17},{13,21},{17,9},{21,13},{10,18... | collective-permute-start | bytes 921608 | tf_op jit(solution)/shard_map/ppermute | solution.py:469
  11.8 18.9 %collective-permute-start.5 = (bf16[400,384]{1,0:T(8,128)(2,1)}, bf16[400,384]{1,0:T(8,128)(2,1)S(1)}, u32[]{:S(2)}, u32[]{:S(2)}) collective-permute-start(bf16[400,384]{1,0:T(8,128)(2,1)} %get-tuple-element.46), channel_id=1, source_target_pairs={{0,16},{4,20},{24,8},{28,12},{1,17},{5,21},{25,9},{29,13},{2,18},{... | collective-permute-start | bytes 921608 | tf_op jit(solution)/shard_map/ppermute | solution.py:470
  17.0 1.1 %copy-start = (bf16[800,384]{1,0:T(8,128)(2,1)S(1)}, bf16[800,384]{1,0:T(8,128)(2,1)}, u32[]{:S(2)}) copy-start(bf16[800,384]{1,0:T(8,128)(2,1)} %get-tuple-element.36.own) | copy-start | bytes 1843204
  18.0 1.1 %copy-start.2 = (bf16[800,384]{1,0:T(8,128)(2,1)S(1)}, bf16[800,384]{1,0:T(8,128)(2,1)}, u32[]{:S(2)}) copy-start(bf16[800,384]{1,0:T(8,128)(2,1)} %get-tuple-element.35.mine) | copy-start | bytes 1843204
  23.9 4.9 %copy-start.1 = (bf16[800,384]{1,0:T(8,128)(2,1)S(1)}, bf16[800,384]{1,0:T(8,128)(2,1)}, u32[]{:S(2)}) copy-start(bf16[800,384]{1,0:T(8,128)(2,1)} %get-tuple-element.36.own) | copy-start | bytes 1843204
  24.0 1.2 %collective-permute-start.3 = (f32[1,192]{1,0:T(1,128)S(1)}, f32[1,192]{1,0:T(1,128)S(1)}, u32[]{:S(2)}, u32[]{:S(2)}) collective-permute-start(f32[1,192]{1,0:T(1,128)S(1)} %get-tuple-element.45), channel_id=1, source_target_pairs={{0,1},{1,0},{2,3},{3,2},{4,5},{5,4},{6,7},{7,6},{8,9},{9,8},{10,11... | collective-permute-start | bytes 2312 | tf_op jit(solution)/shard_map/ppermute | solution.py:639
  25.2 3.6 %collective-permute-start.4 = (f32[1,192]{1,0:T(1,128)S(1)}, f32[1,192]{1,0:T(1,128)S(1)}, u32[]{:S(2)}, u32[]{:S(2)}) collective-permute-start(f32[1,192]{1,0:T(1,128)S(1)} %add.6), channel_id=1, source_target_pairs={{0,2},{1,3},{2,0},{3,1},{4,6},{5,7},{6,4},{7,5},{8,10},{9,11},{10,... | collective-permute-start | bytes 2312 | tf_op jit(solution)/shard_map/ppermute | solution.py:639
  28.8 1.9 %copy-start.5 = (f32[192]{0:T(256)S(1)}, f32[192]{0:T(256)}, u32[]{:S(2)}) copy-start(f32[192]{0:T(256)} %param.14) | copy-start | bytes 2308
  31.5 28.5 %collective-permute-start.7 = (bf16[768,384]{1,0:T(8,128)(2,1)S(1)}, bf16[768,384]{1,0:T(8,128)(2,1)S(1)}, u32[]{:S(2)}, u32[]{:S(2)}) collective-permute-start(bf16[768,384]{1,0:T(8,128)(2,1)S(1)} %get-tuple-element.57), channel_id=1, source_target_pairs={{0,4},{4,0},{8,12},{12,8},{16,20},{20,16},{24,28},{28,24},{1,5},{5... | collective-permute-start | bytes 1769480 | tf_op jit(solution)/shard_map/ppermute | solution.py:504
  34.1 15.3 %collective-permute-start.8 = (bf16[384,384]{1,0:T(8,128)(2,1)S(1)}, bf16[384,384]{1,0:T(8,128)(2,1)S(1)}, u32[]{:S(2)}, u32[]{:S(2)}) collective-permute-start(bf16[384,384]{1,0:T(8,128)(2,1)S(1)} %get-tuple-element.58), channel_id=1, source_target_pairs={{0,8},{4,12},{8,0},{12,4},{16,24},{20,28},{24,16},{28,20},{1,9},{5... | collective-permute-start | bytes 884744 | tf_op jit(solution)/shard_map/ppermute | solution.py:500
  41.5 13.5 %collective-permute-start.9 = (bf16[384,384]{1,0:T(8,128)(2,1)S(1)}, bf16[384,384]{1,0:T(8,128)(2,1)S(1)}, u32[]{:S(2)}, u32[]{:S(2)}) collective-permute-start(bf16[384,384]{1,0:T(8,128)(2,1)S(1)} %get-tuple-element.59), channel_id=1, source_target_pairs={{8,4},{12,0},{16,28},{20,24},{9,5},{13,1},{17,29},{21,25},{10,6},{... | collective-permute-start | bytes 884744 | tf_op jit(solution)/shard_map/ppermute | solution.py:501
  42.8 12.2 %collective-permute-start.10 = (bf16[384,384]{1,0:T(8,128)(2,1)S(1)}, bf16[384,384]{1,0:T(8,128)(2,1)S(1)}, u32[]{:S(2)}, u32[]{:S(2)}) collective-permute-start(bf16[384,384]{1,0:T(8,128)(2,1)S(1)} %get-tuple-element.60), channel_id=1, source_target_pairs={{8,16},{12,20},{16,8},{20,12},{9,17},{13,21},{17,9},{21,13},{10,18... | collective-permute-start | bytes 884744 | tf_op jit(solution)/shard_map/ppermute | solution.py:503
  43.5 16.5 %collective-permute-start.11 = (bf16[384,384]{1,0:T(8,128)(2,1)S(1)}, bf16[384,384]{1,0:T(8,128)(2,1)S(1)}, u32[]{:S(2)}, u32[]{:S(2)}) collective-permute-start(bf16[384,384]{1,0:T(8,128)(2,1)S(1)} %get-tuple-element.61), channel_id=1, source_target_pairs={{16,0},{20,4},{8,24},{12,28},{17,1},{21,5},{9,25},{13,29},{18,2},{... | collective-permute-start | bytes 884744 | tf_op jit(solution)/shard_map/ppermute | solution.py:502

commit v2 on v1

--- a/solution.py
+++ b/solution.py
@@ -17,7 +17,6 @@
 TILE = 16
 BIG = 1e30
 VMEM = 24 * 1024 * 1024
-HOME_FLOPS = 1024
 PREP_VMEM = 63 * 1024 * 1024
 F32 = jnp.float32
 BF16 = jnp.bfloat16
@@ -261,7 +260,7 @@
     gate = jax.nn.sigmoid(logit[...])
     lane = lax.broadcasted_iota(jnp.int32, (1, slots), 1).astype(F32)
     used = lane < used_slots(positions, shard, slots)
-    return jnp.where(used, gate * (1.0 - gate) * dots[...], 0.0)
+    return jnp.where(used, gate * (1.0 - gate) * dots, 0.0)
 
 
 FOUR_PLAN = (
@@ -276,10 +275,11 @@
     pass
 
 
-def four_home_kernel(heads, positions, mine, own, grads, own_total):
+def four_home_kernel(heads, positions, mine, own, dots_in, grads, own_total, dots):
     slots = grads.shape[0] // 4
     rows = 2 * slots + TILE
     shard = lax.axis_index("seq")
+    dots[...] = dots_in[...]
     for down in (True, False):
 
         @pl.when((shard < 4) == down)
@@ -295,52 +295,63 @@
 
 
 def four_guest_kernel(
-    heads, positions, dots_in, mine, near, cross, grads_in, grads, near_total, cross_total, dots
+    heads, positions, after, mine, near, cross, turn, grads, near_total, cross_total
 ):
+    turn[...] = after[...]
+    slots = grads.shape[0] // 2
+    rows = 2 * slots + TILE
+    shard = lax.axis_index("seq")
+    for level in (1, 2):
+
+        @pl.when(shard // 2 == level)
+        def _():
+            meet(
+                level == 1, [(mine, (level - 1) * rows, shard)],
+                [(near, 0, shard - 2), (cross, 0, (shard - 2) ^ 1)],
+                positions, heads, None,
+                Store(slots, [(grads, 0)], True),
+                Store(slots, [(near_total, 0), (cross_total, 0)], True),
+            )
+
+
+def meets_pair(shard):
+    return (shard % 2 == 1) == (shard < 4)
+
+
+def four_pair_kernel(
+    heads, positions, after, mine, own, other, near,
+    turn, grads, other_total, own_near, other_near, back, early
+):
+    turn[...] = after[...]
     slots = grads.shape[0] // 4
     rows = 2 * slots + TILE
     shard = lax.axis_index("seq")
-    grads[...] = grads_in[...]
-    dots[...] = dots_in[...]
-    for level in (1, 2):
-        at = level - 1
-
-        @pl.when(shard // 2 == level)
-        def _():
-            meet(
-                level == 1, [(mine, at * rows, shard)],
-                [(near, 0, shard - 2), (cross, 0, (shard - 2) ^ 1)],
-                positions, heads, None,
-                Store(slots, [(grads, 2 * slots * at)], False),
-                Store(slots, [(near_total, 0), (cross_total, 0)], True),
-            )
-
-
-def four_pair_kernel(
-    heads, positions, mine, own, other, near, grads_in, own_in, grads, own_total, other_total, back
-):
-    slots = grads.shape[0] // 4
-    rows = 2 * slots + TILE
-    shard = lax.axis_index("seq")
-    grads[...] = grads_in[...]
-    own_total[...] = own_in[...]
-    other_total[...] = jnp.zeros(other_total.shape, F32)
+    meets = meets_pair(shard)
     for down in (True, False):
 
-        @pl.when(((shard < 4) == down) & (shard % 2 == int(down)))
+        @pl.when(meets & ((shard < 4) == down))
         def _():
             for at in range(2):
                 base = 2 * slots * at
                 meet(
                     down, [(mine, at * rows, shard)], [(other, at * rows, shard ^ 1)],
                     positions, heads, None,
-                    Store(slots, [(grads, base)], False),
+                    Store(slots, [(grads, base)], True),
                     Store(slots, [(other_total, base)], True),
                 )
 
+    for at in range(2):
+
+        @pl.when(meets & (shard // 2 % 2 == at))
+        def _():
+            early[...] = other_total[pl.ds(2 * slots * at, 2 * slots), :].astype(BF16)
+
+    @pl.when(jnp.logical_not(meets))
+    def _():
+        early[...] = jnp.zeros(early.shape, BF16)
+
     for level in (0, 3):
         at = 1 if level == 0 else 0
-        base = 2 * slots * at
 
         @pl.when(shard // 2 == level)
         def _():
@@ -349,7 +360,7 @@
                 [(own, at * rows, shard), (other, at * rows, shard ^ 1)],
                 positions, heads, None,
                 Store(slots, [(back, 0)], True),
-                Store(slots, [(own_total, base), (other_total, base)], False),
+                Store(slots, [(own_near, 0), (other_near, 0)], True),
             )
 
 
@@ -370,7 +381,10 @@
     )
 
 
-def four_middle_kernel(heads, positions, own, other, near, cross, middle, back, *totals):
+def four_middle_kernel(
+    heads, positions, after, dots, dots_near, own, other, near, cross, middle, back, dots_sum, *totals
+):
+    dots_sum[...] = dots[...] + dots_near[...]
     for level in (1, 2):
 
         @pl.when(lax.axis_index("seq") // 2 == level)
@@ -381,73 +395,75 @@
 
 
 def four_far_kernel(
-    heads, positions, logit, dots, own, other, near, cross, skip,
-    own_in, other_in, near_in, cross_in, own_mid, other_mid, near_mid, cross_mid, step_back,
-    own_total, other_low, near_low, cross_low, skip_back, router, *totals
+    heads, positions, own, other, near, cross, skip,
+    other_pair, other_near, near_in, cross_in, own_mid, other_mid, near_mid, cross_mid, step_back,
+    own_total, late, near_low, cross_low, skip_back, *totals
 ):
     slots = near_in.shape[0] // 2
     shard = lax.axis_index("seq")
-    own_total[...] = own_in[...]
-    other_low[...] = other_in[...].astype(BF16)
-    router[...] = router_part(positions, logit, dots, slots, shard)
-    inner = (shard >= 2) & (shard < 6)
-
-    @pl.when(jnp.logical_not(inner))
-    def _():
-        near_low[...] = step_back[...]
-
-    for level in (1, 2):
-        part = pl.ds(2 * slots * (level - 1), 2 * slots)
+    meets = meets_pair(shard)
+    for level in range(4):
+        part = pl.ds(2 * slots * (1 - level % 2), 2 * slots)
 
         @pl.when(shard // 2 == level)
         def _():
-            totals[0][...] = own_in[part, :] + own_mid[...]
-            totals[1][...] = other_in[part, :] + other_mid[...]
-            totals[2][...] = near_in[...] + near_mid[...]
-            totals[3][...] = cross_in[...] + cross_mid[...]
+            paired = jnp.where(meets, other_pair[part, :], 0.0)
+            if level in (0, 3):
+                late[...] = (paired + other_near[...]).astype(BF16)
+                near_low[...] = step_back[...]
+                return
+            own_total[...] = own_mid[...]
+            totals[0][...] = paired + other_mid[...]
+            totals[1][...] = near_in[...] + near_mid[...]
+            totals[2][...] = cross_in[...] + cross_mid[...]
             four_far_meet(
-                heads, level, skip, 2, (own, other, near, cross), positions, skip_back, totals
+                heads, level, skip, 2, (own, other, near, cross), positions, skip_back,
+                (own_total, *totals),
             )
-            own_total[part, :] = totals[0][...]
-            other_low[part, :] = totals[1][...].astype(BF16)
-            near_low[...] = totals[2][...].astype(BF16)
-            cross_low[...] = totals[3][...].astype(BF16)
+            late[...] = totals[0][...].astype(BF16)
+            near_low[...] = totals[1][...].astype(BF16)
+            cross_low[...] = totals[2][...].astype(BF16)
 
 
 def four_join_kernel(
-    heads, grads, own, other, near, cross, middle, skip, query_grad, key_grad, value_grad
+    heads, positions, logit, dots, dots_far, grads, grads_guest, grads_pair, own, own_near, own_far,
+    early, near, cross, skip, middle, late,
+    query_grad, key_grad, value_grad, router
 ):
     slots, half = grads.shape[0] // 4, grads.shape[1]
     shard = lax.axis_index("seq")
-
-    def part(ref, at, which):
+    meets = meets_pair(shard)
+    router[...] = router_part(positions, logit, dots[...] + dots_far[...], slots, shard)
+
+    def part(ref, which, at=0):
         return ref[pl.ds((2 * at + which) * slots, slots), :].astype(F32)
 
-    def first(refs, which):
-        return sum(part(ref, 0, which) for ref in refs)
-
-    for down in (True, False):
-
-        @pl.when((shard < 4) == down)
-        def _():
-            guest, late = (0, 1) if down else (1, 0)
-            inner = (shard >= 2) & (shard < 6)
+    for level in range(4):
+        inner = level in (1, 2)
+
+        @pl.when(shard // 2 == level)
+        def _():
+            if level < 2:
+                moving, staying = [query_grad], [key_grad, value_grad]
+            else:
+                moving, staying = [key_grad, value_grad], [query_grad]
             for at in range(2):
                 cols = pl.ds(at * half, half)
-                extra = [cross] if at == guest else [middle, skip]
-                if down:
-                    moving, staying = [query_grad], [key_grad, value_grad]
+                center = inner and at == level - 1
+                early_half = at == level % 2
+                for which, out in enumerate(moving):
+                    total = part(grads, which, at)
+                    total = total + jnp.where(meets, part(grads_pair, which, at), 0.0)
+                    if inner:
+                        total = total + part(grads_guest if center else near, which)
+                    out[:, cols] = total.astype(BF16)
+                if inner:
+                    extra = [own_far] if center else [middle]
                 else:
-                    moving, staying = [key_grad, value_grad], [query_grad]
-                for which, out in enumerate(moving):
-                    total = part(grads, at, which)
-                    if at == late:
-                        total = total + jnp.where(inner, part(near, 0, which), 0.0)
-                    out[:, cols] = total.astype(BF16)
+                    extra = [near, cross] if early_half else [own_near, skip]
+                extra.append(early if early_half else late)
                 for which, out in enumerate(staying):
-                    total = part(own, at, which) + part(other, at, which) + first(extra, which)
-                    if at == guest:
-                        total = total + jnp.where(inner, 0.0, part(near, 0, which))
+                    total = part(own, which, at) + sum(part(ref, which) for ref in extra)
                     out[:, cols] = total.astype(BF16)
 
 
@@ -468,46 +484,47 @@
     other = lax.ppermute(own, "seq", pairs([(i, i) for i in range(4)], 1))
     middle = lax.ppermute(far_send, "seq", pairs([(1, 2), (2, 1)]))
     skip = lax.ppermute(far_send, "seq", pairs([(0, 2), (3, 1)]))
-    grads, own_total = call(
+    grads, own_total, dots = call(
         functools.partial(four_home_kernel, heads),
-        [totals] * 2,
-        positions, mine, own,
-        flops=HOME_FLOPS,
-    )
-    grads, near_total, cross_total, dots = call(
-        functools.partial(four_guest_kernel, heads),
-        [totals, total, total, shape(1, F32, slots)],
-        positions, dots, mine, near, cross, grads,
-    )
-    dots = sum_over(dots, "tp")
-    grads, own_total, other_total, step_back = call(
+        [totals] * 2 + [shape(1, F32, slots)],
+        positions, mine, own, dots,
+    )
+    row = shape(1, F32, slots)
+    dots, grads_guest, near_total, cross_total = call(
+        functools.partial(four_guest_kernel, heads), [row] + [total] * 3,
+        positions, dots, mine, near, cross,
+    )
+    turn, grads_pair, other_total, own_near, other_near, step_back, early = call(
         functools.partial(four_pair_kernel, heads),
-        [totals] * 3 + [low],
-        positions, mine, own, other, near, grads, own_total,
-    )
-    middle_back, *middles = call(
+        [row, totals, totals, total, total, low, low],
+        positions, dots, mine, own, other, near,
+    )
+    dots_near = lax.ppermute(dots, "tp", [(i, i ^ 1) for i in range(4)])
+    early = lax.ppermute(early, "seq", pairs([(i, i) for i in range(4)], 1))
+    middle_back, dots, *middles = call(
         functools.partial(four_middle_kernel, heads),
-        [low] + [total] * 4,
-        positions, own, other, near, cross, middle,
-    )
-    own_total, other_low, near_low, cross_low, skip_back, router = call(
+        [low, row] + [total] * 4,
+        positions, turn, dots, dots_near, own, other, near, cross, middle,
+    )
+    dots_far = lax.ppermute(dots, "tp", [(i, i ^ 2) for i in range(4)])
+    own_far, late, near_low, cross_low, skip_back = call(
         functools.partial(four_far_kernel, heads),
-        [totals, shape(4 * slots), low, low, low, shape(1, F32, slots)],
-        positions, logit, dots, own, other, near, cross, skip,
-        own_total, other_total, near_total, cross_total, *middles, step_back,
-        scratch=[pltpu.VMEM(total.shape, F32)] * 4,
+        [total, low, low, low, low],
+        positions, own, other, near, cross, skip,
+        other_total, other_near, near_total, cross_total, *middles, step_back,
+        scratch=[pltpu.VMEM(total.shape, F32)] * 3,
     )
     near = lax.ppermute(near_low, "seq", pairs([(0, 1), (1, 0), (2, 3), (3, 2)]))
     cross = lax.ppermute(cross_low, "seq", pairs([(1, 0), (2, 3)], 1))
     skip = lax.ppermute(skip_back, "seq", pairs([(2, 0), (1, 3)]))
     middle = lax.ppermute(middle_back, "seq", pairs([(1, 2), (2, 1)]))
-    other = lax.ppermute(other_low, "seq", pairs([(i, i) for i in range(4)], 1))
-    outs = call(
+    late = lax.ppermute(late, "seq", pairs([(i, i) for i in range(4)], 1))
+    return call(
         functools.partial(four_join_kernel, heads),
-        [shape(slots, BF16, width)] * 3,
-        grads, own_total, other, near, cross, middle, skip,
-    )
-    return *outs, router
+        [shape(slots, BF16, width)] * 3 + [row],
+        positions, logit, dots, dots_far, grads, grads_guest, grads_pair,
+        own_total, own_near, own_far, early, near, cross, skip, middle, late,
+    )
 
 
 def ring_plan(levels):
@@ -530,7 +547,7 @@
             Store(slots, [(grads, base * slots)], True),
             Store(slots, [(own_total, stay_base * slots), (other_total, stay_base * slots)], True),
         )
-    router[...] = router_part(positions, logit, dots, slots, shard)
+    router[...] = router_part(positions, logit, dots[...], slots, shard)
 
 
 def ring_away_kernel(
@@ -672,7 +689,7 @@
         )
         return *outs, dots
 
-    if shards == 8:
+    if shards == 8 and lax.axis_size("tp") == 4:
         query_grad, key_grad, value_grad, router = four_levels(
             prep, shape, positions, logit, slots, heads, width
         )

time: 61.6 us -> 62.1 us (level)
  waiting for transfers between devices: 21.1 us -> 19.2 us
  starting transfers between devices: 27.1 us -> 28.9 us
  local copies, waits for them, and re-layouts: 2.16 us -> 3.8 us
  Pallas kernels: 10.1 us -> 9.01 us
    ppermute x1, waiting for transfers between devices: 4.65 us -> 10.7 us  [four_levels(): lax.ppermute(near_low, 'seq', pairs([(0, 1), (1, 0), (2, 3), (3, 2)]))]
    ppermute x1, waiting for transfers between devices: 5.04 us -> 0.01 us  [four_levels(): skip = lax.ppermute(skip_back, 'seq', pairs([(2, 0), (1, 3)]))]
    ppermute x1, waiting for transfers between devices: 2.65 us -> 0.01 us  [four_levels(): cross = lax.ppermute(near_send, 'seq', pairs([(0, 1), (3, 2)], 1))]
    ppermute x1, waiting for transfers between devices: 0.01 us -> 2.23 us  [four_levels(): lax.ppermute(near_send, 'seq', pairs([(0, 1), (1, 0), (2, 3), (3, 2)]))]
    ppermute x3 -> x4, waiting for transfers between devices: 3.21 us -> 1.14 us  [the longest x1 1.13 us: four_levels(): dots_near = lax.ppermute(dots, 'tp', [(i, i ^ 1) for i in range(4)])]
    unnamed x14 -> x16, local copies, waits for them, and re-layouts: 2.16 us -> 3.8 us
    ppermute x1, starting transfers between devices: 1.88 us -> 3.43 us  [four_levels(): cross = lax.ppermute(near_send, 'seq', pairs([(0, 1), (3, 2)], 1))]
    ppermute x1, starting transfers between devices: 1.58 us -> 0.07 us  [four_levels(): lax.ppermute(near_send, 'seq', pairs([(0, 1), (1, 0), (2, 3), (3, 2)]))]
  transfers between devices with their start and end apart: 12 -> 13, of which waited for: 6 -> 4; matrix products, arithmetic and copies ran while one was open for 0% -> 0% of each run, Pallas kernels for 7% -> 6%
where the time goes in v2:
time: 62.1 us; the launch traced here: 61.7 us
  starting transfers between devices  28.9 us (47%)
  waiting for transfers between devices  19.2 us (31%)
  Pallas kernels  9.01 us (15%)
  local copies, waits for them, and re-layouts  3.8 us (6%)
  between operations  0.81 us (1%)
    ppermute x1, waiting for transfers between devices, four_levels(): lax.ppermute(near_low, 'seq', pairs([(0, 1), (1, 0), (2, 3), (3, 2)]))  10.7 us
    pallas_call x8, Pallas kernels, call(): pl.pallas_call(kernel, out_shape=out_shape, in_specs=[pl.BlockSpec(memory...  9.01 us
    ppermute x1, starting transfers between devices, four_levels(): skip = lax.ppermute(far_send, 'seq', pairs([(0, 2), (3, 1)]))  6.61 us
    ppermute x1, starting transfers between devices, four_levels(): lax.ppermute(near_low, 'seq', pairs([(0, 1), (1, 0), (2, 3), (3, 2)]))  6.51 us
    ppermute x1, waiting for transfers between devices, four_levels(): cross = lax.ppermute(cross_low, 'seq', pairs([(1, 0), (2, 3)], 1))  5.1 us
    unnamed x16, local copies, waits for them, and re-layouts  3.8 us
    ppermute x1, starting transfers between devices, four_levels(): early = lax.ppermute(early, 'seq', pairs([(i, i) for i in range(4)], 1))  3.69 us
    ppermute x1, starting transfers between devices, four_levels(): cross = lax.ppermute(near_send, 'seq', pairs([(0, 1), (3, 2)], 1))  3.43 us
  transfers between devices with their start and end apart: 13, of which 4 were waited for; matrix products, arithmetic and copies ran while one was open for 0% of the time, Pallas kernels for 6%

profile of v2, /device:TPU:0, one launch (start us, length us, event | category | flops | bytes accessed | tf_op | source)
XLA Modules:
  0.0 61.7 jit_solution(4762714661878476228)
XLA Ops:
  0.6 3.9 %shard_map.111 = (f32[1,192]{1,0:T(1,128)}, bf16[800,384]{1,0:T(8,128)(2,1)}, bf16[800,384]{1,0:T(8,128)(2,1)}, bf16[400,384]{1,0:T(8,128)(2,1)}, bf16[400,384]{1,0:T(8,128)(2,1)}) custom-call(bf16[192,768]{1,0:T(8,128)(2,1)} %refs_0_.1, bf16[192,768]{1,0:T(8,128)(2,1)} %refs_1_.1, f32[1,192]{1,0:T(1,128)} %bitcast.11, f32[6,192]{1,0:T(8,128)} %bitcast.13, ...), custom_call_target="tpu_custom_call" | custom-call | flops 1024 | bytes 1024 | tf_op jit(solution)/shard_map/pallas_call | solution.py:637
  4.6 3.0 %collective-permute-start.2 = (bf16[800,384]{1,0:T(8,128)(2,1)}, bf16[800,384]{1,0:T(8,128)(2,1)S(1)}, u32[]{:S(2)}, u32[]{:S(2)}) collective-permute-start(bf16[800,384]{1,0:T(8,128)(2,1)} %get-tuple-element.41.own), channel_id=1, source_target_pairs={{0,4},{4,0},{8,12},{12,8},{16,20},{20,16},{24,28},{28,24},{1,5},{5... | collective-permute-start | bytes 1843208 | tf_op jit(solution)/shard_map/ppermute | solution.py:484
  7.6 1.0 %copy-done.5 = bf16[400,384]{1,0:T(8,128)(2,1)S(1)} copy-done((bf16[400,384]{1,0:T(8,128)(2,1)S(1)}, bf16[400,384]{1,0:T(8,128)(2,1)}, u32[]{:S(2)}) %copy-start.5) | copy-done | bytes 307224
  8.6 3.4 %collective-permute-start.1 = (bf16[400,384]{1,0:T(8,128)(2,1)}, bf16[400,384]{1,0:T(8,128)(2,1)S(1)}, u32[]{:S(2)}, u32[]{:S(2)}) collective-permute-start(bf16[400,384]{1,0:T(8,128)(2,1)} %get-tuple-element.46), channel_id=1, source_target_pairs={{0,12},{4,8},{24,20},{28,16},{1,13},{5,9},{25,21},{29,17},{2,14},{... | collective-permute-start | bytes 921608 | tf_op jit(solution)/shard_map/ppermute | solution.py:483
  12.0 0.1 collective-permute-start
  12.1 0.7 %collective-permute-start.4 = (bf16[400,384]{1,0:T(8,128)(2,1)S(1)}, bf16[400,384]{1,0:T(8,128)(2,1)S(1)}, u32[]{:S(2)}, u32[]{:S(2)}) collective-permute-start(bf16[400,384]{1,0:T(8,128)(2,1)S(1)} %get-tuple-element.49), channel_id=1, source_target_pairs={{8,16},{12,20},{16,8},{20,12},{9,17},{13,21},{17,9},{21,13},{10,18... | collective-permute-start | bytes 921608 | tf_op jit(solution)/shard_map/ppermute | solution.py:485
  12.8 6.6 %collective-permute-start.6 = (bf16[400,384]{1,0:T(8,128)(2,1)S(1)}, bf16[400,384]{1,0:T(8,128)(2,1)S(1)}, u32[]{:S(2)}, u32[]{:S(2)}) collective-permute-start(bf16[400,384]{1,0:T(8,128)(2,1)S(1)} %get-tuple-element.49), channel_id=1, source_target_pairs={{0,16},{4,20},{24,8},{28,12},{1,17},{5,21},{25,9},{29,13},{2,18},{... | collective-permute-start | bytes 921608 | tf_op jit(solution)/shard_map/ppermute | solution.py:486
  19.4 1.1 %copy-done = bf16[800,384]{1,0:T(8,128)(2,1)S(1)} copy-done((bf16[800,384]{1,0:T(8,128)(2,1)S(1)}, bf16[800,384]{1,0:T(8,128)(2,1)}, u32[]{:S(2)}) %copy-start) | copy-done | bytes 614424
  20.5 1.1 %copy-done.2 = bf16[800,384]{1,0:T(8,128)(2,1)S(1)} copy-done((bf16[800,384]{1,0:T(8,128)(2,1)S(1)}, bf16[800,384]{1,0:T(8,128)(2,1)}, u32[]{:S(2)}) %copy-start.2) | copy-done | bytes 614424
  21.6 0.7 %copy-done.7 = f32[1,192]{1,0:T(1,128)S(1)} copy-done((f32[1,192]{1,0:T(1,128)S(1)}, f32[1,192]{1,0:T(1,128)}, u32[]{:S(2)}) %copy-start.7) | copy-done | bytes 792
  22.2 2.1 %shard_map.112 = (f32[768,384]{1,0:T(8,128)S(1)}, f32[768,384]{1,0:T(8,128)S(1)}, f32[1,192]{1,0:T(1,128)S(1)}) custom-call(s32[12,128]{1,0:T(8,128)S(1)} %bitcast.5, bf16[800,384]{1,0:T(8,128)(2,1)S(1)} %copy-done.2, bf16[800,384]{1,0:T(8,128)(2,1)S(1)} %copy-done, f32[1,192]{1,0:T(1,128)S(1)} %copy-done.7), custom_call_target="tpu_custom_call" | custom-call | flops 1024 | bytes 1024 | tf_op jit(solution)/shard_map/pallas_call | solution.py:637
  24.3 0.0 collective-permute-done.1.cross
  24.4 2.2 %collective-permute-done.near = bf16[400,384]{1,0:T(8,128)(2,1)S(1)} collective-permute-done((bf16[400,384]{1,0:T(8,128)(2,1)}, bf16[400,384]{1,0:T(8,128)(2,1)S(1)}, u32[]{:S(2)}, u32[]{:S(2)}) %collective-permute-start) | collective-permute-done | bytes 307232 | tf_op jit(solution)/shard_map/ppermute | solution.py:482
  26.6 0.0 collective-permute-done.2.other
  26.6 1.6 %shard_map.115 = (f32[1,192]{1,0:T(1,128)S(1)}, f32[768,384]{1,0:T(8,128)S(1)}, f32[768,384]{1,0:T(8,128)S(1)}, f32[384,384]{1,0:T(8,128)S(1)}, f32[384,384]{1,0...) custom-call(s32[12,128]{1,0:T(8,128)S(1)} %bitcast.7, ...), custom_call_target="tpu_custom_call" | custom-call | flops 1024 | bytes 1024 | tf_op jit(solution)/shard_map/pallas_call | solution.py:637
  28.2 3.7 %collective-permute-start.7 = (bf16[384,384]{1,0:T(8,128)(2,1)S(1)}, bf16[384,384]{1,0:T(8,128)(2,1)S(1)}, u32[]{:S(2)}, u32[]{:S(2)}) collective-permute-start(bf16[384,384]{1,0:T(8,128)(2,1)S(1)} %get-tuple-element.66), channel_id=1, source_target_pairs={{0,4},{4,0},{8,12},{12,8},{16,20},{20,16},{24,28},{28,24},{1,5},{5... | collective-permute-start | bytes 884744 | tf_op jit(solution)/shard_map/ppermute | solution.py:503
  31.9 0.0 collective-permute-start.3
  31.9 1.1 %collective-permute-done.3.dots_near = f32[1,192]{1,0:T(1,128)S(1)} collective-permute-done((f32[1,192]{1,0:T(1,128)S(1)}, f32[1,192]{1,0:T(1,128)S(1)}, u32[]{:S(2)}, u32[]{:S(2)}) %collective-permute-start.3) | collective-permute-done | bytes 800 | tf_op jit(solution)/shard_map/ppermute | solution.py:502
  33.0 1.5 %collective-permute-start.5 = (f32[1,192]{1,0:T(1,128)S(1)}, f32[1,192]{1,0:T(1,128)S(1)}, u32[]{:S(2)}, u32[]{:S(2)}) collective-permute-start(f32[1,192]{1,0:T(1,128)S(1)} %get-tuple-element.50.dots), channel_id=1, source_target_pairs={{0,2},{1,3},{2,0},{3,1},{4,6},{5,7},{6,4},{7,5},{8,10},{9,11},{10,... | collective-permute-start | bytes 2312 | tf_op jit(solution)/shard_map/ppermute | solution.py:509
  34.5 0.1 shard_map.117
  34.6 6.5 %collective-permute-start.8 = (bf16[384,384]{1,0:T(8,128)(2,1)S(1)}, bf16[384,384]{1,0:T(8,128)(2,1)S(1)}, u32[]{:S(2)}, u32[]{:S(2)}) collective-permute-start(bf16[384,384]{1,0:T(8,128)(2,1)S(1)} %get-tuple-element.67), channel_id=1, source_target_pairs={{0,8},{4,12},{8,0},{12,4},{16,24},{20,28},{24,16},{28,20},{1,9},{5... | collective-permute-start | bytes 884744 | tf_op jit(solution)/shard_map/ppermute | solution.py:517
  41.1 1.3 %collective-permute-start.9 = (bf16[384,384]{1,0:T(8,128)(2,1)S(1)}, bf16[384,384]{1,0:T(8,128)(2,1)S(1)}, u32[]{:S(2)}, u32[]{:S(2)}) collective-permute-start(bf16[384,384]{1,0:T(8,128)(2,1)S(1)} %get-tuple-element.68), channel_id=1, source_target_pairs={{8,4},{12,0},{16,28},{20,24},{9,5},{13,1},{17,29},{21,25},{10,6},{... | collective-permute-start | bytes 884744 | tf_op jit(solution)/shard_map/ppermute | solution.py:518
  42.4 1.3 %collective-permute-start.10 = (bf16[384,384]{1,0:T(8,128)(2,1)S(1)}, bf16[384,384]{1,0:T(8,128)(2,1)S(1)}, u32[]{:S(2)}, u32[]{:S(2)}) collective-permute-start(bf16[384,384]{1,0:T(8,128)(2,1)S(1)} %get-tuple-element.69), channel_id=1, source_target_pairs={{16,0},{20,4},{8,24},{12,28},{17,1},{21,5},{9,25},{13,29},{18,2},{... | collective-permute-start | bytes 884744 | tf_op jit(solution)/shard_map/ppermute | solution.py:519
  43.7 0.0 collective-permute-done.5.dots_far
  43.7 0.1 collective-permute-start.12
  43.9 0.0 collective-permute-done.7.early
  43.9 0.7 %collective-permute-start.11 = (bf16[384,384]{1,0:T(8,128)(2,1)S(1)}, bf16[384,384]{1,0:T(8,128)(2,1)S(1)}, u32[]{:S(2)}, u32[]{:S(2)}) collective-permute-start(bf16[384,384]{1,0:T(8,128)(2,1)S(1)} %get-tuple-element.70), channel_id=1, source_target_pairs={{8,16},{12,20},{16,8},{20,12},{9,17},{13,21},{17,9},{21,13},{10,18... | collective-permute-start | bytes 884744 | tf_op jit(solution)/shard_map/ppermute | solution.py:520
  44.6 10.7 %collective-permute-done.8.near = bf16[384,384]{1,0:T(8,128)(2,1)S(1)} collective-permute-done((bf16[384,384]{1,0:T(8,128)(2,1)S(1)}, bf16[384,384]{1,0:T(8,128)(2,1)S(1)}, u32[]{:S(2)}, u32[]{:S(2)}) %collective-permute-start.8) | collective-permute-done | bytes 294944 | tf_op jit(solution)/shard_map/ppermute | solution.py:517
  55.3 5.1 %collective-permute-done.9.cross = bf16[384,384]{1,0:T(8,128)(2,1)S(1)} collective-permute-done((bf16[384,384]{1,0:T(8,128)(2,1)S(1)}, bf16[384,384]{1,0:T(8,128)(2,1)S(1)}, u32[]{:S(2)}, u32[]{:S(2)}) %collective-permute-start.9) | collective-permute-done | bytes 294944 | tf_op jit(solution)/shard_map/ppermute | solution.py:518
  60.4 0.0 collective-permute-done.12.late
  60.4 0.0 collective-permute-done.11.middle
  60.4 1.3 %shard_map.118 = (bf16[192,768]{1,0:T(8,128)(2,1)}, bf16[192,768]{1,0:T(8,128)(2,1)}, bf16[192,768]{1,0:T(8,128)(2,1)}, f32[1,192]{1,0:T(1,128)}) custom-call(s32[12,128]{1,0:T(8,128)S(1)} %bitcast.10, f32[1,192]{1,0:T(1,128)S(1)} %bitcast.12, f32[1,192]{1,0:T(1,128)S(1)} %get-tuple-element.50.dots, f32[1,192]{1,0:T(1,128)S(1)} %collective-permute-done.5.dots_far, ...), custom_call_target="tpu_custom_call" | custom-call | flops 1024 | bytes 1024 | tf_op jit(solution)/shard_map/pallas_call | solution.py:637
  (18 shorter events, 0.0 us)
Async XLA Ops:
  0.6 18.8 %copy-start.4 = (s32[1536]{0:T(1024)S(1)}, s32[1536]{0:T(1024)}, u32[]{:S(2)}) copy-start(s32[1536]{0:T(1024)} %param.15) | copy-start | bytes 18436
  4.6 22.0 %copy-start.3 = (bf16[800,384]{1,0:T(8,128)(2,1)S(1)}, bf16[800,384]{1,0:T(8,128)(2,1)}, u32[]{:S(2)}) copy-start(bf16[800,384]{1,0:T(8,128)(2,1)} %get-tuple-element.40.mine) | copy-start | bytes 1843204
  4.6 22.0 %collective-permute-start.2 = (bf16[800,384]{1,0:T(8,128)(2,1)}, bf16[800,384]{1,0:T(8,128)(2,1)S(1)}, u32[]{:S(2)}, u32[]{:S(2)}) collective-permute-start(bf16[800,384]{1,0:T(8,128)(2,1)} %get-tuple-element.41.own), channel_id=1, source_target_pairs={{0,4},{4,0},{8,12},{12,8},{16,20},{20,16},{24,28},{28,24},{1,5},{5... | collective-permute-start | bytes 1843208 | tf_op jit(solution)/shard_map/ppermute | solution.py:484
  7.6 1.0 %copy-start.5 = (bf16[400,384]{1,0:T(8,128)(2,1)S(1)}, bf16[400,384]{1,0:T(8,128)(2,1)}, u32[]{:S(2)}) copy-start(bf16[400,384]{1,0:T(8,128)(2,1)} %get-tuple-element.45.refs_1_) | copy-start | bytes 921604
  8.6 15.8 %collective-permute-start.1 = (bf16[400,384]{1,0:T(8,128)(2,1)}, bf16[400,384]{1,0:T(8,128)(2,1)S(1)}, u32[]{:S(2)}, u32[]{:S(2)}) collective-permute-start(bf16[400,384]{1,0:T(8,128)(2,1)} %get-tuple-element.46), channel_id=1, source_target_pairs={{0,12},{4,8},{24,20},{28,16},{1,13},{5,9},{25,21},{29,17},{2,14},{... | collective-permute-start | bytes 921608 | tf_op jit(solution)/shard_map/ppermute | solution.py:483
  12.0 14.6 %collective-permute-start = (bf16[400,384]{1,0:T(8,128)(2,1)}, bf16[400,384]{1,0:T(8,128)(2,1)S(1)}, u32[]{:S(2)}, u32[]{:S(2)}) collective-permute-start(bf16[400,384]{1,0:T(8,128)(2,1)} %get-tuple-element.46), channel_id=1, source_target_pairs={{0,8},{4,12},{8,0},{12,4},{16,24},{20,28},{24,16},{28,20},{1,9},{5... | collective-permute-start | bytes 921608 | tf_op jit(solution)/shard_map/ppermute | solution.py:482
  12.1 19.8 %collective-permute-start.4 = (bf16[400,384]{1,0:T(8,128)(2,1)S(1)}, bf16[400,384]{1,0:T(8,128)(2,1)S(1)}, u32[]{:S(2)}, u32[]{:S(2)}) collective-permute-start(bf16[400,384]{1,0:T(8,128)(2,1)S(1)} %get-tuple-element.49), channel_id=1, source_target_pairs={{8,16},{12,20},{16,8},{20,12},{9,17},{13,21},{17,9},{21,13},{10,18... | collective-permute-start | bytes 921608 | tf_op jit(solution)/shard_map/ppermute | solution.py:485
  12.8 21.7 %collective-permute-start.6 = (bf16[400,384]{1,0:T(8,128)(2,1)S(1)}, bf16[400,384]{1,0:T(8,128)(2,1)S(1)}, u32[]{:S(2)}, u32[]{:S(2)}) collective-permute-start(bf16[400,384]{1,0:T(8,128)(2,1)S(1)} %get-tuple-element.49), channel_id=1, source_target_pairs={{0,16},{4,20},{24,8},{28,12},{1,17},{5,21},{25,9},{29,13},{2,18},{... | collective-permute-start | bytes 921608 | tf_op jit(solution)/shard_map/ppermute | solution.py:486
  19.4 1.1 %copy-start = (bf16[800,384]{1,0:T(8,128)(2,1)S(1)}, bf16[800,384]{1,0:T(8,128)(2,1)}, u32[]{:S(2)}) copy-start(bf16[800,384]{1,0:T(8,128)(2,1)} %get-tuple-element.41.own) | copy-start | bytes 1843204
  20.5 1.1 %copy-start.2 = (bf16[800,384]{1,0:T(8,128)(2,1)S(1)}, bf16[800,384]{1,0:T(8,128)(2,1)}, u32[]{:S(2)}) copy-start(bf16[800,384]{1,0:T(8,128)(2,1)} %get-tuple-element.40.mine) | copy-start | bytes 1843204
  21.6 0.7 %copy-start.7 = (f32[1,192]{1,0:T(1,128)S(1)}, f32[1,192]{1,0:T(1,128)}, u32[]{:S(2)}) copy-start(f32[1,192]{1,0:T(1,128)} %get-tuple-element.42.dots_in) | copy-start | bytes 2308
  22.2 4.4 %copy-start.1 = (bf16[800,384]{1,0:T(8,128)(2,1)S(1)}, bf16[800,384]{1,0:T(8,128)(2,1)}, u32[]{:S(2)}) copy-start(bf16[800,384]{1,0:T(8,128)(2,1)} %get-tuple-element.41.own) | copy-start | bytes 1843204
  28.2 15.7 %collective-permute-start.7 = (bf16[384,384]{1,0:T(8,128)(2,1)S(1)}, bf16[384,384]{1,0:T(8,128)(2,1)S(1)}, u32[]{:S(2)}, u32[]{:S(2)}) collective-permute-start(bf16[384,384]{1,0:T(8,128)(2,1)S(1)} %get-tuple-element.66), channel_id=1, source_target_pairs={{0,4},{4,0},{8,12},{12,8},{16,20},{20,16},{24,28},{28,24},{1,5},{5... | collective-permute-start | bytes 884744 | tf_op jit(solution)/shard_map/ppermute | solution.py:503
  31.9 1.1 %collective-permute-start.3 = (f32[1,192]{1,0:T(1,128)S(1)}, f32[1,192]{1,0:T(1,128)S(1)}, u32[]{:S(2)}, u32[]{:S(2)}) collective-permute-start(f32[1,192]{1,0:T(1,128)S(1)} %get-tuple-element.47.after.dots), channel_id=1, source_target_pairs={{0,1},{1,0},{2,3},{3,2},{4,5},{5,4},{6,7},{7,6},{8,9},{9,8},{10,11... | collective-permute-start | bytes 2312 | tf_op jit(solution)/shard_map/ppermute | solution.py:502
  33.0 10.7 %collective-permute-start.5 = (f32[1,192]{1,0:T(1,128)S(1)}, f32[1,192]{1,0:T(1,128)S(1)}, u32[]{:S(2)}, u32[]{:S(2)}) collective-permute-start(f32[1,192]{1,0:T(1,128)S(1)} %get-tuple-element.50.dots), channel_id=1, source_target_pairs={{0,2},{1,3},{2,0},{3,1},{4,6},{5,7},{6,4},{7,5},{8,10},{9,11},{10,... | collective-permute-start | bytes 2312 | tf_op jit(solution)/shard_map/ppermute | solution.py:509
  34.5 25.9 %copy-start.6 = (f32[192]{0:T(256)S(1)}, f32[192]{0:T(256)}, u32[]{:S(2)}) copy-start(f32[192]{0:T(256)} %param.14) | copy-start | bytes 2308
  34.6 20.7 %collective-permute-start.8 = (bf16[384,384]{1,0:T(8,128)(2,1)S(1)}, bf16[384,384]{1,0:T(8,128)(2,1)S(1)}, u32[]{:S(2)}, u32[]{:S(2)}) collective-permute-start(bf16[384,384]{1,0:T(8,128)(2,1)S(1)} %get-tuple-element.67), channel_id=1, source_target_pairs={{0,8},{4,12},{8,0},{12,4},{16,24},{20,28},{24,16},{28,20},{1,9},{5... | collective-permute-start | bytes 884744 | tf_op jit(solution)/shard_map/ppermute | solution.py:517
  41.1 19.2 %collective-permute-start.9 = (bf16[384,384]{1,0:T(8,128)(2,1)S(1)}, bf16[384,384]{1,0:T(8,128)(2,1)S(1)}, u32[]{:S(2)}, u32[]{:S(2)}) collective-permute-start(bf16[384,384]{1,0:T(8,128)(2,1)S(1)} %get-tuple-element.68), channel_id=1, source_target_pairs={{8,4},{12,0},{16,28},{20,24},{9,5},{13,1},{17,29},{21,25},{10,6},{... | collective-permute-start | bytes 884744 | tf_op jit(solution)/shard_map/ppermute | solution.py:518
  42.4 18.0 %collective-permute-start.10 = (bf16[384,384]{1,0:T(8,128)(2,1)S(1)}, bf16[384,384]{1,0:T(8,128)(2,1)S(1)}, u32[]{:S(2)}, u32[]{:S(2)}) collective-permute-start(bf16[384,384]{1,0:T(8,128)(2,1)S(1)} %get-tuple-element.69), channel_id=1, source_target_pairs={{16,0},{20,4},{8,24},{12,28},{17,1},{21,5},{9,25},{13,29},{18,2},{... | collective-permute-start | bytes 884744 | tf_op jit(solution)/shard_map/ppermute | solution.py:519
  43.7 16.7 %collective-permute-start.12 = (bf16[384,384]{1,0:T(8,128)(2,1)S(1)}, bf16[384,384]{1,0:T(8,128)(2,1)S(1)}, u32[]{:S(2)}, u32[]{:S(2)}) collective-permute-start(bf16[384,384]{1,0:T(8,128)(2,1)S(1)} %get-tuple-element.71), channel_id=1, source_target_pairs={{0,4},{4,0},{8,12},{12,8},{16,20},{20,16},{24,28},{28,24},{1,5},{5... | collective-permute-start | bytes 884744 | tf_op jit(solution)/shard_map/ppermute | solution.py:521
  43.9 16.5 %collective-permute-start.11 = (bf16[384,384]{1,0:T(8,128)(2,1)S(1)}, bf16[384,384]{1,0:T(8,128)(2,1)S(1)}, u32[]{:S(2)}, u32[]{:S(2)}) collective-permute-start(bf16[384,384]{1,0:T(8,128)(2,1)S(1)} %get-tuple-element.70), channel_id=1, source_target_pairs={{8,16},{12,20},{16,8},{20,12},{9,17},{13,21},{17,9},{21,13},{10,18... | collective-permute-start | bytes 884744 | tf_op jit(solution)/shard_map/ppermute | solution.py:520

commit v3 on v2

--- a/solution.py
+++ b/solution.py
@@ -17,6 +17,7 @@
 TILE = 16
 BIG = 1e30
 VMEM = 24 * 1024 * 1024
+SUM_FLOPS = 5_000_000_000
 PREP_VMEM = 63 * 1024 * 1024
 F32 = jnp.float32
 BF16 = jnp.bfloat16
@@ -101,12 +102,35 @@
             )
     for copy in copies:
         copy.start()
+    for copy in copies[5:]:
+        copy.wait()
+    for at in range(2):
+        bank[pl.ds(at * rows + 2 * slots, TILE), :] = jnp.zeros((TILE, half), BF16)
+    level = lax.axis_index("seq") // 2
+    moves = []
+    for out, blocks in zip(outs, plan):
+        for place, block in enumerate(blocks(level)):
+            block = jnp.int32(block)
+            move = pltpu.make_async_copy(
+                bank.at[pl.ds(pl.multiple_of(block * rows, TILE), rows), :],
+                out.at[pl.ds(place * rows, rows), :],
+                done.at[len(moves)],
+            )
+            moves.append((block, move))
+
+    def each(some, early):
+        for block, move in some:
+
+            @pl.when((block < 2) == early)
+            def _():
+                move.start()
+
+    each(moves, True)
     for copy in copies[:5]:
         copy.wait()
     head_dim = width // heads
     root = math.sqrt(head_dim)
     shard = lax.axis_index("seq")
-    level = shard // 2
     count = used_slots(positions, shard, slots)
     lane = lax.broadcasted_iota(jnp.int32, (PIECE, slots), 1).astype(F32)
     used = lane < count
@@ -150,28 +174,13 @@
 
     per = heads // 2
     for at in range(2):
-        bank[pl.ds(at * rows + 2 * slots, TILE), :] = jnp.zeros((TILE, half), BF16)
         base = (2 + at) * rows
         bank[pl.ds(base + slots, slots), :] = jnp.concatenate(
             dout_parts[at * per:(at + 1) * per], axis=1
         )
         bank[pl.ds(base + 2 * slots, TILE), :] = pack(ext(at * per))
-    for copy in copies[5:]:
-        copy.wait()
-    moves = []
-    for out, blocks in zip(outs, plan):
-        for place, block in enumerate(blocks(level)):
-            start = pl.multiple_of(jnp.int32(block) * rows, TILE)
-            moves.append(
-                pltpu.make_async_copy(
-                    bank.at[pl.ds(start, rows), :],
-                    out.at[pl.ds(place * rows, rows), :],
-                    done.at[len(moves)],
-                )
-            )
-    for move in moves:
-        move.start()
-    for move in moves:
+    each(moves, False)
+    for _, move in moves:
         move.wait()
 
 
@@ -236,14 +245,15 @@
 
 
 class Store:
-    def __init__(self, slots, targets, fresh):
+    def __init__(self, slots, targets, fresh, olds=None):
         self.slots, self.targets, self.fresh = slots, targets, fresh
+        self.olds = olds or [ref for ref, _ in targets]
 
     def __call__(self, which, cols, term):
         for i, (ref, base) in enumerate(self.targets):
             rows = pl.ds(base + which * self.slots, self.slots)
             part = term[i * self.slots:(i + 1) * self.slots]
-            part = part if self.fresh else ref[rows, cols] + part
+            part = part if self.fresh else self.olds[i][rows, cols] + part
             ref[rows, cols] = part.astype(ref.dtype)
 
 
@@ -271,15 +281,11 @@
 )
 
 
-def gate_kernel(*refs):
-    pass
-
-
-def four_home_kernel(heads, positions, mine, own, dots_in, grads, own_total, dots):
+def four_home_kernel(heads, positions, mine, own, turn, grads, own_total):
     slots = grads.shape[0] // 4
     rows = 2 * slots + TILE
     shard = lax.axis_index("seq")
-    dots[...] = dots_in[...]
+    turn[...] = jnp.zeros(turn.shape, F32)
     for down in (True, False):
 
         @pl.when((shard < 4) == down)
@@ -294,39 +300,19 @@
                 )
 
 
-def four_guest_kernel(
-    heads, positions, after, mine, near, cross, turn, grads, near_total, cross_total
-):
-    turn[...] = after[...]
-    slots = grads.shape[0] // 2
-    rows = 2 * slots + TILE
-    shard = lax.axis_index("seq")
-    for level in (1, 2):
-
-        @pl.when(shard // 2 == level)
-        def _():
-            meet(
-                level == 1, [(mine, (level - 1) * rows, shard)],
-                [(near, 0, shard - 2), (cross, 0, (shard - 2) ^ 1)],
-                positions, heads, None,
-                Store(slots, [(grads, 0)], True),
-                Store(slots, [(near_total, 0), (cross_total, 0)], True),
-            )
-
-
 def meets_pair(shard):
     return (shard % 2 == 1) == (shard < 4)
 
 
 def four_pair_kernel(
     heads, positions, after, mine, own, other, near,
-    turn, grads, other_total, own_near, other_near, back, early
+    turn, grads_pair, other_total, own_near, other_near, back
 ):
+    slots = back.shape[0] // 2
+    rows = 2 * slots + TILE
+    shard = lax.axis_index("seq")
+    meets = meets_pair(shard)
     turn[...] = after[...]
-    slots = grads.shape[0] // 4
-    rows = 2 * slots + TILE
-    shard = lax.axis_index("seq")
-    meets = meets_pair(shard)
     for down in (True, False):
 
         @pl.when(meets & ((shard < 4) == down))
@@ -336,19 +322,9 @@
                 meet(
                     down, [(mine, at * rows, shard)], [(other, at * rows, shard ^ 1)],
                     positions, heads, None,
-                    Store(slots, [(grads, base)], True),
+                    Store(slots, [(grads_pair, base)], True),
                     Store(slots, [(other_total, base)], True),
                 )
-
-    for at in range(2):
-
-        @pl.when(meets & (shard // 2 % 2 == at))
-        def _():
-            early[...] = other_total[pl.ds(2 * slots * at, 2 * slots), :].astype(BF16)
-
-    @pl.when(jnp.logical_not(meets))
-    def _():
-        early[...] = jnp.zeros(early.shape, BF16)
 
     for level in (0, 3):
         at = 1 if level == 0 else 0
@@ -364,80 +340,106 @@
             )
 
 
-def four_far_meet(heads, level, block, reach, refs, positions, back, totals):
-    own, other, near, cross = refs
-    slots = back.shape[0] // 2
-    at = (level - 1) * (2 * slots + TILE)
-    shard = lax.axis_index("seq")
-    meet(
-        level == 1, [(block, 0, shard - 2 * reach)],
-        [
-            (own, at, shard), (other, at, shard ^ 1),
-            (near, 0, shard - 2), (cross, 0, (shard - 2) ^ 1),
-        ],
-        positions, heads, None,
-        Store(slots, [(back, 0)], True),
-        Store(slots, [(ref, 0) for ref in totals], reach == 1),
-    )
-
-
-def four_middle_kernel(
-    heads, positions, after, dots, dots_near, own, other, near, cross, middle, back, dots_sum, *totals
+def four_near_kernel(
+    heads, positions, after, dots, dots_near, mine, near, skip, middle, back,
+    dots_sum, near_low, grads_guest, skip_part, middle_part
 ):
+    slots = near_low.shape[0] // 2
+    rows = 2 * slots + TILE
+    shard = lax.axis_index("seq")
     dots_sum[...] = dots[...] + dots_near[...]
-    for level in (1, 2):
-
-        @pl.when(lax.axis_index("seq") // 2 == level)
+    for level in range(4):
+
+        @pl.when(shard // 2 == level)
         def _():
-            four_far_meet(
-                heads, level, middle, 1, (own, other, near, cross), positions, back, totals
+            if level in (0, 3):
+                near_low[...] = back[...]
+                return
+            meet(
+                level == 1,
+                [
+                    (mine, (level - 1) * rows, shard),
+                    (skip, 0, shard - 4), (middle, 0, shard - 2),
+                ],
+                [(near, 0, shard - 2)],
+                positions, heads, None,
+                Store(slots, [(grads_guest, 0), (skip_part, 0), (middle_part, 0)], True),
+                Store(slots, [(near_low, 0)], True),
             )
 
 
-def four_far_kernel(
-    heads, positions, own, other, near, cross, skip,
-    other_pair, other_near, near_in, cross_in, own_mid, other_mid, near_mid, cross_mid, step_back,
-    own_total, late, near_low, cross_low, skip_back, *totals
+def four_last_kernel(
+    heads, positions, dots_in, mine, own, other, cross, skip, middle,
+    grads_in, skip_in, middle_in, other_pair, own_in, other_in,
+    dots, grads_guest, skip_back, cross_low, middle_back, other_low, own_near,
+    skip_part, middle_part, other_near,
 ):
-    slots = near_in.shape[0] // 2
+    slots = grads_in.shape[0] // 2
+    rows = 2 * slots + TILE
+    shard = lax.axis_index("seq")
+    meets = meets_pair(shard)
+    dots[...] = dots_in[...]
+    for level in range(4):
+        at = (1, 0, 1, 0)[level]
+
+        @pl.when(shard // 2 == level)
+        def _():
+            if level in (0, 3):
+                own_near[...] = own_in[...]
+                other_near[...] = other_in[...]
+            else:
+                far = [(skip, 0, shard - 4), (middle, 0, shard - 2)]
+                parts = [(skip_part, 0), (middle_part, 0)]
+                meet(
+                    level == 1, far, [(own, at * rows, shard), (other, at * rows, shard ^ 1)],
+                    positions, heads, None,
+                    Store(slots, parts, False, [skip_in, middle_in]),
+                    Store(slots, [(own_near, 0), (other_near, 0)], True),
+                )
+                meet(
+                    level == 1, [(mine, at * rows, shard)] + far, [(cross, 0, (shard - 2) ^ 1)],
+                    positions, heads, None,
+                    Store(
+                        slots, [(grads_guest, 0), (skip_back, 0), (middle_back, 0)], False,
+                        [grads_in, skip_part, middle_part],
+                    ),
+                    Store(slots, [(cross_low, 0)], True),
+                )
+            for half in range(2):
+                part = pl.ds(2 * slots * half, 2 * slots)
+                total = jnp.where(meets, other_pair[part, :], 0.0)
+                total = total + other_near[...] if half == at else total
+                other_low[part, :] = total.astype(BF16)
+
+
+def four_sum_kernel(heads, grads, grads_pair, own, near, moving_sum, staying_sum):
+    slots = grads.shape[0] // 4
     shard = lax.axis_index("seq")
     meets = meets_pair(shard)
     for level in range(4):
-        part = pl.ds(2 * slots * (1 - level % 2), 2 * slots)
 
         @pl.when(shard // 2 == level)
         def _():
-            paired = jnp.where(meets, other_pair[part, :], 0.0)
-            if level in (0, 3):
-                late[...] = (paired + other_near[...]).astype(BF16)
-                near_low[...] = step_back[...]
-                return
-            own_total[...] = own_mid[...]
-            totals[0][...] = paired + other_mid[...]
-            totals[1][...] = near_in[...] + near_mid[...]
-            totals[2][...] = cross_in[...] + cross_mid[...]
-            four_far_meet(
-                heads, level, skip, 2, (own, other, near, cross), positions, skip_back,
-                (own_total, *totals),
-            )
-            late[...] = totals[0][...].astype(BF16)
-            near_low[...] = totals[1][...].astype(BF16)
-            cross_low[...] = totals[2][...].astype(BF16)
+            for at in range(2):
+                part = pl.ds(2 * slots * at, 2 * slots)
+                moving = grads[part, :] + jnp.where(meets, grads_pair[part, :], 0.0)
+                staying = own[part, :]
+                if at != (1, 0, 1, 0)[level]:
+                    if level in (1, 2):
+                        moving = moving + near[...].astype(F32)
+                    else:
+                        staying = staying + near[...].astype(F32)
+                moving_sum[part, :] = moving
+                staying_sum[part, :] = staying
 
 
 def four_join_kernel(
-    heads, positions, logit, dots, dots_far, grads, grads_guest, grads_pair, own, own_near, own_far,
-    early, near, cross, skip, middle, late,
-    query_grad, key_grad, value_grad, router
+    heads, positions, logit, dots, dots_far, moving_sum, staying_sum, grads_guest, own_near,
+    other, middle, skip, cross, query_grad, key_grad, value_grad, router
 ):
-    slots, half = grads.shape[0] // 4, grads.shape[1]
-    shard = lax.axis_index("seq")
-    meets = meets_pair(shard)
+    slots, half = moving_sum.shape[0] // 4, moving_sum.shape[1]
+    shard = lax.axis_index("seq")
     router[...] = router_part(positions, logit, dots[...] + dots_far[...], slots, shard)
-
-    def part(ref, which, at=0):
-        return ref[pl.ds((2 * at + which) * slots, slots), :].astype(F32)
-
     for level in range(4):
         inner = level in (1, 2)
 
@@ -449,81 +451,76 @@
                 moving, staying = [key_grad, value_grad], [query_grad]
             for at in range(2):
                 cols = pl.ds(at * half, half)
-                center = inner and at == level - 1
-                early_half = at == level % 2
-                for which, out in enumerate(moving):
-                    total = part(grads, which, at)
-                    total = total + jnp.where(meets, part(grads_pair, which, at), 0.0)
-                    if inner:
-                        total = total + part(grads_guest if center else near, which)
-                    out[:, cols] = total.astype(BF16)
+                met = at == (1, 0, 1, 0)[level]
+                plus = [grads_guest] if inner and met else []
                 if inner:
-                    extra = [own_far] if center else [middle]
+                    extra = [own_near] if met else [middle]
                 else:
-                    extra = [near, cross] if early_half else [own_near, skip]
-                extra.append(early if early_half else late)
-                for which, out in enumerate(staying):
-                    total = part(own, which, at) + sum(part(ref, which) for ref in extra)
-                    out[:, cols] = total.astype(BF16)
+                    extra = [own_near, skip] if met else [cross]
+                for outs, base, more in ((moving, moving_sum, plus), (staying, staying_sum, extra)):
+                    for which, out in enumerate(outs):
+                        rows = pl.ds((2 * at + which) * slots, slots)
+                        total = base[rows, :]
+                        for ref in more:
+                            total = total + ref[pl.ds(which * slots, slots), :].astype(F32)
+                        if outs is staying:
+                            total = total + other[rows, :].astype(F32)
+                        out[:, cols] = total.astype(BF16)
 
 
 def four_levels(prep, shape, positions, logit, slots, heads, width):
     double, block, total = shape(4 * slots + 2 * TILE), shape(2 * slots + TILE), shape(2 * slots, F32)
-    totals, low = shape(4 * slots, F32), shape(2 * slots)
+    totals, totals_low, low = shape(4 * slots, F32), shape(4 * slots), shape(2 * slots)
     own, mine, near_send, far_send, dots = prep(FOUR_PLAN, [double, double, block, block])
-    near_send, far_send = call(
-        gate_kernel, [block, block], near_send, far_send,
-        ins=[pltpu.HBM] * 2, outs=[pltpu.HBM] * 2, aliases={0: 0, 1: 1},
-    )
-
     def pairs(levels, flip=0):
         return [(2 * a + c, 2 * b + (c ^ flip)) for a, b in levels for c in range(2)]
 
     near = lax.ppermute(near_send, "seq", pairs([(0, 1), (1, 0), (2, 3), (3, 2)]))
-    cross = lax.ppermute(near_send, "seq", pairs([(0, 1), (3, 2)], 1))
+    cross = lax.ppermute(near, "seq", pairs([(1, 1), (2, 2)], 1))
     other = lax.ppermute(own, "seq", pairs([(i, i) for i in range(4)], 1))
+    skip = lax.ppermute(far_send, "seq", pairs([(0, 2), (3, 1)]))
     middle = lax.ppermute(far_send, "seq", pairs([(1, 2), (2, 1)]))
-    skip = lax.ppermute(far_send, "seq", pairs([(0, 2), (3, 1)]))
-    grads, own_total, dots = call(
+    row = shape(1, F32, slots)
+    turn, grads, own_total = call(
         functools.partial(four_home_kernel, heads),
-        [totals] * 2 + [shape(1, F32, slots)],
-        positions, mine, own, dots,
-    )
-    row = shape(1, F32, slots)
-    dots, grads_guest, near_total, cross_total = call(
-        functools.partial(four_guest_kernel, heads), [row] + [total] * 3,
-        positions, dots, mine, near, cross,
-    )
-    turn, grads_pair, other_total, own_near, other_near, step_back, early = call(
+        [row] + [totals] * 2,
+        positions, mine, own,
+    )
+    turn, grads_pair, other_total, own_near, other_near, step_back = call(
         functools.partial(four_pair_kernel, heads),
-        [row, totals, totals, total, total, low, low],
-        positions, dots, mine, own, other, near,
+        [row, totals, totals, total, total, low],
+        positions, turn, mine, own, other, near,
     )
     dots_near = lax.ppermute(dots, "tp", [(i, i ^ 1) for i in range(4)])
-    early = lax.ppermute(early, "seq", pairs([(i, i) for i in range(4)], 1))
-    middle_back, dots, *middles = call(
-        functools.partial(four_middle_kernel, heads),
-        [low, row] + [total] * 4,
-        positions, turn, dots, dots_near, own, other, near, cross, middle,
+    dots, near_low, grads_guest, skip_part, middle_part = call(
+        functools.partial(four_near_kernel, heads),
+        [row, low, total, total, total],
+        positions, turn, dots, dots_near, mine, near, skip, middle, step_back,
+    )
+    near = lax.ppermute(near_low, "seq", pairs([(0, 1), (1, 0), (2, 3), (3, 2)]))
+    dots, grads_guest, skip_back, cross_low, middle_back, other_low, own_near = call(
+        functools.partial(four_last_kernel, heads),
+        [row, total, low, low, low, totals_low, total],
+        positions, dots, mine, own, other, cross, skip, middle,
+        grads_guest, skip_part, middle_part, other_total, own_near, other_near,
+        scratch=[pltpu.VMEM(total.shape, F32)] * 3,
     )
     dots_far = lax.ppermute(dots, "tp", [(i, i ^ 2) for i in range(4)])
-    own_far, late, near_low, cross_low, skip_back = call(
-        functools.partial(four_far_kernel, heads),
-        [total, low, low, low, low],
-        positions, own, other, near, cross, skip,
-        other_total, other_near, near_total, cross_total, *middles, step_back,
-        scratch=[pltpu.VMEM(total.shape, F32)] * 3,
-    )
-    near = lax.ppermute(near_low, "seq", pairs([(0, 1), (1, 0), (2, 3), (3, 2)]))
+    skip = lax.ppermute(skip_back, "seq", pairs([(2, 0), (1, 3)]))
     cross = lax.ppermute(cross_low, "seq", pairs([(1, 0), (2, 3)], 1))
-    skip = lax.ppermute(skip_back, "seq", pairs([(2, 0), (1, 3)]))
     middle = lax.ppermute(middle_back, "seq", pairs([(1, 2), (2, 1)]))
-    late = lax.ppermute(late, "seq", pairs([(i, i) for i in range(4)], 1))
+    other = lax.ppermute(other_low, "seq", pairs([(i, i) for i in range(4)], 1))
+    moving_sum, staying_sum = call(
+        functools.partial(four_sum_kernel, heads),
+        [totals] * 2,
+        grads, grads_pair, own_total, near,
+        flops=SUM_FLOPS,
+    )
     return call(
         functools.partial(four_join_kernel, heads),
         [shape(slots, BF16, width)] * 3 + [row],
-        positions, logit, dots, dots_far, grads, grads_guest, grads_pair,
-        own_total, own_near, own_far, early, near, cross, skip, middle, late,
+        positions, logit, dots, dots_far, moving_sum, staying_sum, grads_guest, own_near,
+        other, middle, skip, cross,
     )
 
 

time: 62.1 us -> 54 us (0.87)
  starting transfers between devices: 28.9 us -> 23.5 us
  local copies, waits for them, and re-layouts: 3.8 us -> 2.16 us
  waiting for transfers between devices: 19.2 us -> 17.7 us
    ppermute x1, waiting for transfers between devices: 10.7 us -> 1.35 us  [four_levels(): lax.ppermute(near_low, 'seq', pairs([(0, 1), (1, 0), (2, 3), (3, 2)]))]
    ppermute x3 -> x2, starting transfers between devices: 7.27 us -> 1.74 us  [the longest x1 1.07 us: four_levels(): other = lax.ppermute(other_low, 'seq', pairs([(i, i) for i in range(4)], 1))]
    ppermute x1, waiting for transfers between devices: 0.01 us -> 5.07 us  [four_levels(): skip = lax.ppermute(skip_back, 'seq', pairs([(2, 0), (1, 3)]))]
    ppermute x1, starting transfers between devices: 6.61 us -> 4.6 us  [four_levels(): skip = lax.ppermute(far_send, 'seq', pairs([(0, 2), (3, 1)]))]
    ppermute x1, waiting for transfers between devices: 0.01 us -> 1.82 us  [four_levels(): dots_far = lax.ppermute(dots, 'tp', [(i, i ^ 2) for i in range(4)])]
    unnamed x16 -> x14, local copies, waits for them, and re-layouts: 3.8 us -> 2.16 us
    ppermute x1, starting transfers between devices: 0.07 us -> 1.7 us  [four_levels(): lax.ppermute(near_send, 'seq', pairs([(0, 1), (1, 0), (2, 3), (3, 2)]))]
    ppermute x1, waiting for transfers between devices: 5.1 us -> 6.27 us  [four_levels(): cross = lax.ppermute(cross_low, 'seq', pairs([(1, 0), (2, 3)], 1))]
  transfers between devices with their start and end apart: 13 -> 12, of which waited for: 4 -> 6; matrix products, arithmetic and copies ran while one was open for 0% -> 0% of each run, Pallas kernels for 6% -> 8%
where the time goes in v3:
time: 54 us; the launch traced here: 53.7 us
  starting transfers between devices  23.5 us (44%)
  waiting for transfers between devices  17.7 us (33%)
  Pallas kernels  9.39 us (17%)
  local copies, waits for them, and re-layouts  2.16 us (4%)
  between operations  0.84 us (2%)
    pallas_call x7, Pallas kernels, call(): pl.pallas_call(kernel, out_shape=out_shape, in_specs=[pl.BlockSpec(memory...  9.39 us
    ppermute x1, starting transfers between devices, four_levels(): lax.ppermute(near_low, 'seq', pairs([(0, 1), (1, 0), (2, 3), (3, 2)]))  6.97 us
    ppermute x1, waiting for transfers between devices, four_levels(): cross = lax.ppermute(cross_low, 'seq', pairs([(1, 0), (2, 3)], 1))  6.27 us
    ppermute x1, waiting for transfers between devices, four_levels(): skip = lax.ppermute(skip_back, 'seq', pairs([(2, 0), (1, 3)]))  5.07 us
    ppermute x1, starting transfers between devices, four_levels(): skip = lax.ppermute(far_send, 'seq', pairs([(0, 2), (3, 1)]))  4.6 us
    ppermute x1, starting transfers between devices, four_levels(): other = lax.ppermute(own, 'seq', pairs([(i, i) for i in range(4)], 1))  3.03 us
    ppermute x1, waiting for transfers between devices, four_levels(): lax.ppermute(near_send, 'seq', pairs([(0, 1), (1, 0), (2, 3), (3, 2)]))  2.74 us
    unnamed x14, local copies, waits for them, and re-layouts  2.16 us
  transfers between devices with their start and end apart: 12, of which 6 were waited for; matrix products, arithmetic and copies ran while one was open for 0% of the time, Pallas kernels for 8%

profile of v3, /device:TPU:0, one launch (start us, length us, event | category | flops | bytes accessed | tf_op | source)
XLA Modules:
  0.0 53.7 jit_solution(16947074644249364288)
XLA Ops:
  0.6 3.8 %shard_map.111 = (f32[1,192]{1,0:T(1,128)}, bf16[800,384]{1,0:T(8,128)(2,1)}, bf16[800,384]{1,0:T(8,128)(2,1)}, bf16[400,384]{1,0:T(8,128)(2,1)}, bf16[400,384]{1,0:T(8,128)(2,1)}) custom-call(bf16[192,768]{1,0:T(8,128)(2,1)} %refs_0_.1, bf16[192,768]{1,0:T(8,128)(2,1)} %refs_1_.1, f32[1,192]{1,0:T(1,128)} %bitcast.10, f32[6,192]{1,0:T(8,128)} %bitcast.12, ...), custom_call_target="tpu_custom_call" | custom-call | flops 1024 | bytes 1024 | tf_op jit(solution)/shard_map/pallas_call | solution.py:634
  4.4 3.0 %collective-permute-start = (bf16[800,384]{1,0:T(8,128)(2,1)}, bf16[800,384]{1,0:T(8,128)(2,1)S(1)}, u32[]{:S(2)}, u32[]{:S(2)}) collective-permute-start(bf16[800,384]{1,0:T(8,128)(2,1)} %get-tuple-element.37.own), channel_id=1, source_target_pairs={{0,4},{4,0},{8,12},{12,8},{16,20},{20,16},{24,28},{28,24},{1,5},{5... | collective-permute-start | bytes 1843208 | tf_op jit(solution)/shard_map/ppermute | solution.py:480
  7.5 1.7 %collective-permute-start.1 = (bf16[400,384]{1,0:T(8,128)(2,1)}, bf16[400,384]{1,0:T(8,128)(2,1)S(1)}, u32[]{:S(2)}, u32[]{:S(2)}) collective-permute-start(bf16[400,384]{1,0:T(8,128)(2,1)} %get-tuple-element.39), channel_id=1, source_target_pairs={{0,8},{4,12},{8,0},{12,4},{16,24},{20,28},{24,16},{28,20},{1,9},{5... | collective-permute-start | bytes 921608 | tf_op jit(solution)/shard_map/ppermute | solution.py:478
  9.2 4.6 %collective-permute-start.3 = (bf16[400,384]{1,0:T(8,128)(2,1)}, bf16[400,384]{1,0:T(8,128)(2,1)S(1)}, u32[]{:S(2)}, u32[]{:S(2)}) collective-permute-start(bf16[400,384]{1,0:T(8,128)(2,1)} %get-tuple-element.42), channel_id=1, source_target_pairs={{0,16},{4,20},{24,8},{28,12},{1,17},{5,21},{25,9},{29,13},{2,18},{... | collective-permute-start | bytes 921608 | tf_op jit(solution)/shard_map/ppermute | solution.py:481
  13.8 0.7 %collective-permute-start.4 = (bf16[400,384]{1,0:T(8,128)(2,1)}, bf16[400,384]{1,0:T(8,128)(2,1)S(1)}, u32[]{:S(2)}, u32[]{:S(2)}) collective-permute-start(bf16[400,384]{1,0:T(8,128)(2,1)} %get-tuple-element.42), channel_id=1, source_target_pairs={{8,16},{12,20},{16,8},{20,12},{9,17},{13,21},{17,9},{21,13},{10,18... | collective-permute-start | bytes 921608 | tf_op jit(solution)/shard_map/ppermute | solution.py:482
  14.5 2.7 %collective-permute-done.1.near = bf16[400,384]{1,0:T(8,128)(2,1)S(1)} collective-permute-done((bf16[400,384]{1,0:T(8,128)(2,1)}, bf16[400,384]{1,0:T(8,128)(2,1)S(1)}, u32[]{:S(2)}, u32[]{:S(2)}) %collective-permute-start.1) | collective-permute-done | bytes 307232 | tf_op jit(solution)/shard_map/ppermute | solution.py:478
  17.2 0.7 %collective-permute-start.5 = (bf16[400,384]{1,0:T(8,128)(2,1)S(1)}, bf16[400,384]{1,0:T(8,128)(2,1)S(1)}, u32[]{:S(2)}, u32[]{:S(2)}) collective-permute-start(bf16[400,384]{1,0:T(8,128)(2,1)S(1)} %collective-permute-done.1.near), channel_id=1, source_target_pairs={{8,12},{12,8},{16,20},{20,16},{9,13},{13,9},{17,21},{21,17},{10,14... | collective-permute-start | bytes 921608 | tf_op jit(solution)/shard_map/ppermute | solution.py:479
  17.9 0.1 collective-permute-start.2
  18.0 1.1 %copy-done = bf16[800,384]{1,0:T(8,128)(2,1)S(1)} copy-done((bf16[800,384]{1,0:T(8,128)(2,1)S(1)}, bf16[800,384]{1,0:T(8,128)(2,1)}, u32[]{:S(2)}) %copy-start) | copy-done | bytes 614424
  19.0 1.1 %copy-done.2 = bf16[800,384]{1,0:T(8,128)(2,1)S(1)} copy-done((bf16[800,384]{1,0:T(8,128)(2,1)S(1)}, bf16[800,384]{1,0:T(8,128)(2,1)}, u32[]{:S(2)}) %copy-start.2) | copy-done | bytes 614424
  20.1 2.1 %shard_map.112 = (f32[1,192]{1,0:T(1,128)S(1)}, f32[768,384]{1,0:T(8,128)S(1)}, f32[768,384]{1,0:T(8,128)S(1)}) custom-call(s32[12,128]{1,0:T(8,128)S(1)} %bitcast.5, bf16[800,384]{1,0:T(8,128)(2,1)S(1)} %copy-done, bf16[800,384]{1,0:T(8,128)(2,1)S(1)} %copy-done.2), custom_call_target="tpu_custom_call" | custom-call | flops 1024 | bytes 1024 | tf_op jit(solution)/shard_map/pallas_call | solution.py:634
  22.2 0.0 copy-start.6
  22.2 0.0 collective-permute-done.other
  22.3 1.5 %shard_map.113 = (f32[1,192]{1,0:T(1,128)S(1)}, f32[768,384]{1,0:T(8,128)S(1)}, f32[768,384]{1,0:T(8,128)S(1)}, f32[384,384]{1,0:T(8,128)S(1)}, f32[384,384]{1,0:T(8,128)S(1)}, /*index=5*/bf16[384,384]{1,0:T(8,128)(2,1)S(1)}) custom-call(s32[12,128]{1,0:T(8,128)S(1)} %bitcast.6, f32[1,192]{1,0:T(1,128)S(1)} %get-tuple-element.38.after, ...), custom_call_target="tpu_custom_call" | custom-call | flops 1024 | bytes 1024 | tf_op jit(solution)/shard_map/pallas_call | solution.py:634
  23.8 0.0 collective-permute-done.2.dots_near
  23.8 0.0 collective-permute-done.4.middle
  23.8 0.2 shard_map.114
  24.1 7.0 %collective-permute-start.7 = (bf16[384,384]{1,0:T(8,128)(2,1)S(1)}, bf16[384,384]{1,0:T(8,128)(2,1)S(1)}, u32[]{:S(2)}, u32[]{:S(2)}) collective-permute-start(bf16[384,384]{1,0:T(8,128)(2,1)S(1)} %get-tuple-element.55), channel_id=1, source_target_pairs={{0,8},{4,12},{8,0},{12,4},{16,24},{20,28},{24,16},{28,20},{1,9},{5... | collective-permute-start | bytes 884744 | tf_op jit(solution)/shard_map/ppermute | solution.py:500
  31.1 0.2 shard_map.115
  31.3 1.1 %collective-permute-start.8 = (bf16[768,384]{1,0:T(8,128)(2,1)S(1)}, bf16[768,384]{1,0:T(8,128)(2,1)S(1)}, u32[]{:S(2)}, u32[]{:S(2)}) collective-permute-start(bf16[768,384]{1,0:T(8,128)(2,1)S(1)} %get-tuple-element.60), channel_id=1, source_target_pairs={{0,4},{4,0},{8,12},{12,8},{16,20},{20,16},{24,28},{28,24},{1,5},{5... | collective-permute-start | bytes 1769480 | tf_op jit(solution)/shard_map/ppermute | solution.py:512
  32.4 1.3 %collective-permute-start.10 = (bf16[384,384]{1,0:T(8,128)(2,1)S(1)}, bf16[384,384]{1,0:T(8,128)(2,1)S(1)}, u32[]{:S(2)}, u32[]{:S(2)}) collective-permute-start(bf16[384,384]{1,0:T(8,128)(2,1)S(1)} %get-tuple-element.62), channel_id=1, source_target_pairs={{16,0},{20,4},{8,24},{12,28},{17,1},{21,5},{9,25},{13,29},{18,2},{... | collective-permute-start | bytes 884744 | tf_op jit(solution)/shard_map/ppermute | solution.py:509
  33.6 1.3 %collective-permute-start.11 = (bf16[384,384]{1,0:T(8,128)(2,1)S(1)}, bf16[384,384]{1,0:T(8,128)(2,1)S(1)}, u32[]{:S(2)}, u32[]{:S(2)}) collective-permute-start(bf16[384,384]{1,0:T(8,128)(2,1)S(1)} %get-tuple-element.63), channel_id=1, source_target_pairs={{8,4},{12,0},{16,28},{20,24},{9,5},{13,1},{17,29},{21,25},{10,6},{... | collective-permute-start | bytes 884744 | tf_op jit(solution)/shard_map/ppermute | solution.py:510
  34.9 0.7 %collective-permute-start.9 = (bf16[384,384]{1,0:T(8,128)(2,1)S(1)}, bf16[384,384]{1,0:T(8,128)(2,1)S(1)}, u32[]{:S(2)}, u32[]{:S(2)}) collective-permute-start(bf16[384,384]{1,0:T(8,128)(2,1)S(1)} %get-tuple-element.61), channel_id=1, source_target_pairs={{8,16},{12,20},{16,8},{20,12},{9,17},{13,21},{17,9},{21,13},{10,18... | collective-permute-start | bytes 884744 | tf_op jit(solution)/shard_map/ppermute | solution.py:511
  35.6 1.4 %collective-permute-done.7.near = bf16[384,384]{1,0:T(8,128)(2,1)S(1)} collective-permute-done((bf16[384,384]{1,0:T(8,128)(2,1)S(1)}, bf16[384,384]{1,0:T(8,128)(2,1)S(1)}, u32[]{:S(2)}, u32[]{:S(2)}) %collective-permute-start.7) | collective-permute-done | bytes 294944 | tf_op jit(solution)/shard_map/ppermute | solution.py:500
  37.0 1.5 %collective-permute-start.6 = (f32[1,192]{1,0:T(1,128)S(1)}, f32[1,192]{1,0:T(1,128)S(1)}, u32[]{:S(2)}, u32[]{:S(2)}) collective-permute-start(f32[1,192]{1,0:T(1,128)S(1)} %get-tuple-element.51.dots), channel_id=1, source_target_pairs={{0,2},{1,3},{2,0},{3,1},{4,6},{5,7},{6,4},{7,5},{8,10},{9,11},{10,... | collective-permute-start | bytes 2312 | tf_op jit(solution)/shard_map/ppermute | solution.py:508
  38.5 0.2 shard_map.116
  38.7 1.8 %collective-permute-done.6.dots_far = f32[1,192]{1,0:T(1,128)S(1)} collective-permute-done((f32[1,192]{1,0:T(1,128)S(1)}, f32[1,192]{1,0:T(1,128)S(1)}, u32[]{:S(2)}, u32[]{:S(2)}) %collective-permute-start.6) | collective-permute-done | bytes 800 | tf_op jit(solution)/shard_map/ppermute | solution.py:508
  40.6 5.1 %collective-permute-done.10.skip = bf16[384,384]{1,0:T(8,128)(2,1)S(1)} collective-permute-done((bf16[384,384]{1,0:T(8,128)(2,1)S(1)}, bf16[384,384]{1,0:T(8,128)(2,1)S(1)}, u32[]{:S(2)}, u32[]{:S(2)}) %collective-permute-start.10) | collective-permute-done | bytes 294944 | tf_op jit(solution)/shard_map/ppermute | solution.py:509
  45.6 6.3 %collective-permute-done.11.cross = bf16[384,384]{1,0:T(8,128)(2,1)S(1)} collective-permute-done((bf16[384,384]{1,0:T(8,128)(2,1)S(1)}, bf16[384,384]{1,0:T(8,128)(2,1)S(1)}, u32[]{:S(2)}, u32[]{:S(2)}) %collective-permute-start.11) | collective-permute-done | bytes 294944 | tf_op jit(solution)/shard_map/ppermute | solution.py:510
  51.9 0.0 collective-permute-done.9.middle
  51.9 0.5 collective-permute-done.8.other
  52.4 1.3 %shard_map.117 = (bf16[192,768]{1,0:T(8,128)(2,1)}, bf16[192,768]{1,0:T(8,128)(2,1)}, bf16[192,768]{1,0:T(8,128)(2,1)}, f32[1,192]{1,0:T(1,128)}) custom-call(s32[12,128]{1,0:T(8,128)S(1)} %bitcast.9, f32[1,192]{1,0:T(1,128)S(1)} %bitcast.11, f32[1,192]{1,0:T(1,128)S(1)} %get-tuple-element.51.dots, f32[1,192]{1,0:T(1,128)S(1)} %collective-permute-done.6.dots_far, ...), custom_call_target="tpu_custom_call" | custom-call | flops 1024 | bytes 1024 | tf_op jit(solution)/shard_map/pallas_call | solution.py:634
  (13 shorter events, 0.0 us)
Async XLA Ops:
  0.6 17.3 %copy-start.4 = (s32[1536]{0:T(1024)S(1)}, s32[1536]{0:T(1024)}, u32[]{:S(2)}) copy-start(s32[1536]{0:T(1024)} %param.15) | copy-start | bytes 18436
  4.4 17.8 %collective-permute-start = (bf16[800,384]{1,0:T(8,128)(2,1)}, bf16[800,384]{1,0:T(8,128)(2,1)S(1)}, u32[]{:S(2)}, u32[]{:S(2)}) collective-permute-start(bf16[800,384]{1,0:T(8,128)(2,1)} %get-tuple-element.37.own), channel_id=1, source_target_pairs={{0,4},{4,0},{8,12},{12,8},{16,20},{20,16},{24,28},{28,24},{1,5},{5... | collective-permute-start | bytes 1843208 | tf_op jit(solution)/shard_map/ppermute | solution.py:480
  7.5 9.7 %collective-permute-start.1 = (bf16[400,384]{1,0:T(8,128)(2,1)}, bf16[400,384]{1,0:T(8,128)(2,1)S(1)}, u32[]{:S(2)}, u32[]{:S(2)}) collective-permute-start(bf16[400,384]{1,0:T(8,128)(2,1)} %get-tuple-element.39), channel_id=1, source_target_pairs={{0,8},{4,12},{8,0},{12,4},{16,24},{20,28},{24,16},{28,20},{1,9},{5... | collective-permute-start | bytes 921608 | tf_op jit(solution)/shard_map/ppermute | solution.py:478
  9.2 14.6 %collective-permute-start.3 = (bf16[400,384]{1,0:T(8,128)(2,1)}, bf16[400,384]{1,0:T(8,128)(2,1)S(1)}, u32[]{:S(2)}, u32[]{:S(2)}) collective-permute-start(bf16[400,384]{1,0:T(8,128)(2,1)} %get-tuple-element.42), channel_id=1, source_target_pairs={{0,16},{4,20},{24,8},{28,12},{1,17},{5,21},{25,9},{29,13},{2,18},{... | collective-permute-start | bytes 921608 | tf_op jit(solution)/shard_map/ppermute | solution.py:481
  13.8 10.0 %collective-permute-start.4 = (bf16[400,384]{1,0:T(8,128)(2,1)}, bf16[400,384]{1,0:T(8,128)(2,1)S(1)}, u32[]{:S(2)}, u32[]{:S(2)}) collective-permute-start(bf16[400,384]{1,0:T(8,128)(2,1)} %get-tuple-element.42), channel_id=1, source_target_pairs={{8,16},{12,20},{16,8},{20,12},{9,17},{13,21},{17,9},{21,13},{10,18... | collective-permute-start | bytes 921608 | tf_op jit(solution)/shard_map/ppermute | solution.py:482
  17.2 13.8 %collective-permute-start.5 = (bf16[400,384]{1,0:T(8,128)(2,1)S(1)}, bf16[400,384]{1,0:T(8,128)(2,1)S(1)}, u32[]{:S(2)}, u32[]{:S(2)}) collective-permute-start(bf16[400,384]{1,0:T(8,128)(2,1)S(1)} %collective-permute-done.1.near), channel_id=1, source_target_pairs={{8,12},{12,8},{16,20},{20,16},{9,13},{13,9},{17,21},{21,17},{10,14... | collective-permute-start | bytes 921608 | tf_op jit(solution)/shard_map/ppermute | solution.py:479
  17.9 5.9 %collective-permute-start.2 = (f32[1,192]{1,0:T(1,128)}, f32[1,192]{1,0:T(1,128)S(1)}, u32[]{:S(2)}, u32[]{:S(2)}) collective-permute-start(f32[1,192]{1,0:T(1,128)} %get-tuple-element.41.dots), channel_id=1, source_target_pairs={{0,1},{1,0},{2,3},{3,2},{4,5},{5,4},{6,7},{7,6},{8,9},{9,8},{10,11... | collective-permute-start | bytes 2312 | tf_op jit(solution)/shard_map/ppermute | solution.py:494
  18.0 1.1 %copy-start = (bf16[800,384]{1,0:T(8,128)(2,1)S(1)}, bf16[800,384]{1,0:T(8,128)(2,1)}, u32[]{:S(2)}) copy-start(bf16[800,384]{1,0:T(8,128)(2,1)} %get-tuple-element.36.mine) | copy-start | bytes 1843204
  19.0 1.1 %copy-start.2 = (bf16[800,384]{1,0:T(8,128)(2,1)S(1)}, bf16[800,384]{1,0:T(8,128)(2,1)}, u32[]{:S(2)}) copy-start(bf16[800,384]{1,0:T(8,128)(2,1)} %get-tuple-element.37.own) | copy-start | bytes 1843204
  22.2 1.6 %copy-start.1 = (bf16[800,384]{1,0:T(8,128)(2,1)S(1)}, bf16[800,384]{1,0:T(8,128)(2,1)}, u32[]{:S(2)}) copy-start(bf16[800,384]{1,0:T(8,128)(2,1)} %get-tuple-element.36.mine) | copy-start | bytes 1843204
  22.2 1.6 %copy-start.6 = (f32[1,192]{1,0:T(1,128)S(1)}, f32[1,192]{1,0:T(1,128)}, u32[]{:S(2)}) copy-start(f32[1,192]{1,0:T(1,128)} %get-tuple-element.41.dots) | copy-start | bytes 2308
  23.8 7.3 %copy-start.3 = (bf16[800,384]{1,0:T(8,128)(2,1)S(1)}, bf16[800,384]{1,0:T(8,128)(2,1)}, u32[]{:S(2)}) copy-start(bf16[800,384]{1,0:T(8,128)(2,1)} %get-tuple-element.37.own) | copy-start | bytes 1843204
  24.1 12.9 %collective-permute-start.7 = (bf16[384,384]{1,0:T(8,128)(2,1)S(1)}, bf16[384,384]{1,0:T(8,128)(2,1)S(1)}, u32[]{:S(2)}, u32[]{:S(2)}) collective-permute-start(bf16[384,384]{1,0:T(8,128)(2,1)S(1)} %get-tuple-element.55), channel_id=1, source_target_pairs={{0,8},{4,12},{8,0},{12,4},{16,24},{20,28},{24,16},{28,20},{1,9},{5... | collective-permute-start | bytes 884744 | tf_op jit(solution)/shard_map/ppermute | solution.py:500
  31.3 21.1 %collective-permute-start.8 = (bf16[768,384]{1,0:T(8,128)(2,1)S(1)}, bf16[768,384]{1,0:T(8,128)(2,1)S(1)}, u32[]{:S(2)}, u32[]{:S(2)}) collective-permute-start(bf16[768,384]{1,0:T(8,128)(2,1)S(1)} %get-tuple-element.60), channel_id=1, source_target_pairs={{0,4},{4,0},{8,12},{12,8},{16,20},{20,16},{24,28},{28,24},{1,5},{5... | collective-permute-start | bytes 1769480 | tf_op jit(solution)/shard_map/ppermute | solution.py:512
  32.4 13.3 %collective-permute-start.10 = (bf16[384,384]{1,0:T(8,128)(2,1)S(1)}, bf16[384,384]{1,0:T(8,128)(2,1)S(1)}, u32[]{:S(2)}, u32[]{:S(2)}) collective-permute-start(bf16[384,384]{1,0:T(8,128)(2,1)S(1)} %get-tuple-element.62), channel_id=1, source_target_pairs={{16,0},{20,4},{8,24},{12,28},{17,1},{21,5},{9,25},{13,29},{18,2},{... | collective-permute-start | bytes 884744 | tf_op jit(solution)/shard_map/ppermute | solution.py:509
  33.6 18.2 %collective-permute-start.11 = (bf16[384,384]{1,0:T(8,128)(2,1)S(1)}, bf16[384,384]{1,0:T(8,128)(2,1)S(1)}, u32[]{:S(2)}, u32[]{:S(2)}) collective-permute-start(bf16[384,384]{1,0:T(8,128)(2,1)S(1)} %get-tuple-element.63), channel_id=1, source_target_pairs={{8,4},{12,0},{16,28},{20,24},{9,5},{13,1},{17,29},{21,25},{10,6},{... | collective-permute-start | bytes 884744 | tf_op jit(solution)/shard_map/ppermute | solution.py:510
  34.9 16.9 %collective-permute-start.9 = (bf16[384,384]{1,0:T(8,128)(2,1)S(1)}, bf16[384,384]{1,0:T(8,128)(2,1)S(1)}, u32[]{:S(2)}, u32[]{:S(2)}) collective-permute-start(bf16[384,384]{1,0:T(8,128)(2,1)S(1)} %get-tuple-element.61), channel_id=1, source_target_pairs={{8,16},{12,20},{16,8},{20,12},{9,17},{13,21},{17,9},{21,13},{10,18... | collective-permute-start | bytes 884744 | tf_op jit(solution)/shard_map/ppermute | solution.py:511
  37.0 3.6 %collective-permute-start.6 = (f32[1,192]{1,0:T(1,128)S(1)}, f32[1,192]{1,0:T(1,128)S(1)}, u32[]{:S(2)}, u32[]{:S(2)}) collective-permute-start(f32[1,192]{1,0:T(1,128)S(1)} %get-tuple-element.51.dots), channel_id=1, source_target_pairs={{0,2},{1,3},{2,0},{3,1},{4,6},{5,7},{6,4},{7,5},{8,10},{9,11},{10,... | collective-permute-start | bytes 2312 | tf_op jit(solution)/shard_map/ppermute | solution.py:508
  38.5 13.9 %copy-start.5 = (f32[192]{0:T(256)S(1)}, f32[192]{0:T(256)}, u32[]{:S(2)}) copy-start(f32[192]{0:T(256)} %param.14) | copy-start | bytes 2308

commit v4 on v3

--- a/solution.py
+++ b/solution.py
@@ -304,48 +304,76 @@
     return (shard % 2 == 1) == (shard < 4)
 
 
+def follow_kernel(block, after, out):
+    pass
+
+
 def four_pair_kernel(
-    heads, positions, after, mine, own, other, near,
-    turn, grads_pair, other_total, own_near, other_near, back
+    heads, positions, after, mine, other, turn, grads_pair, met_total, early, early_total
+):
+    slots = early.shape[0] // 2
+    rows = 2 * slots + TILE
+    shard = lax.axis_index("seq")
+    meets = meets_pair(shard)
+    turn[...] = after[...]
+    for level in range(4):
+
+        @pl.when(meets & (shard // 2 == level))
+        def _():
+            for at in range(2):
+                met = at == (1, 0, 1, 0)[level]
+                meet(
+                    level < 2, [(mine, at * rows, shard)], [(other, at * rows, shard ^ 1)],
+                    positions, heads, None,
+                    Store(slots, [(grads_pair, 2 * slots * at)], True),
+                    Store(slots, [(met_total if met else early_total, 0)], True),
+                )
+            early[...] = early_total[...].astype(BF16)
+
+    @pl.when(jnp.logical_not(meets))
+    def _():
+        early[...] = jnp.zeros(early.shape, BF16)
+
+
+def four_skip_kernel(
+    heads, positions, after, mine, own, other, near, skip,
+    turn, own_near, other_near, back, near_total, grads_guest, skip_part
 ):
     slots = back.shape[0] // 2
     rows = 2 * slots + TILE
     shard = lax.axis_index("seq")
-    meets = meets_pair(shard)
     turn[...] = after[...]
-    for down in (True, False):
-
-        @pl.when(meets & ((shard < 4) == down))
-        def _():
-            for at in range(2):
-                base = 2 * slots * at
-                meet(
-                    down, [(mine, at * rows, shard)], [(other, at * rows, shard ^ 1)],
-                    positions, heads, None,
-                    Store(slots, [(grads_pair, base)], True),
-                    Store(slots, [(other_total, base)], True),
-                )
-
-    for level in (0, 3):
-        at = 1 if level == 0 else 0
+    for level in range(4):
+        at = (1, 0, 1, 0)[level]
 
         @pl.when(shard // 2 == level)
         def _():
+            pair = [(own, at * rows, shard), (other, at * rows, shard ^ 1)]
+            totals = Store(slots, [(own_near, 0), (other_near, 0)], True)
+            guest = [(near, 0, shard - 2)]
+            if level in (0, 3):
+                meet(
+                    level == 0, guest, pair, positions, heads, None,
+                    Store(slots, [(back, 0)], True), totals,
+                )
+                return
+            far = [(skip, 0, shard - 4)]
             meet(
-                level == 0, [(near, 0, shard - 2)],
-                [(own, at * rows, shard), (other, at * rows, shard ^ 1)],
-                positions, heads, None,
-                Store(slots, [(back, 0)], True),
-                Store(slots, [(own_near, 0), (other_near, 0)], True),
+                level == 1, [(mine, at * rows, shard)] + far, guest, positions, heads, None,
+                Store(slots, [(grads_guest, 0), (skip_part, 0)], True),
+                Store(slots, [(near_total, 0)], True),
             )
+            meet(
+                level == 1, far, pair, positions, heads, None,
+                Store(slots, [(skip_part, 0)], False), totals,
+            )
 
 
 def four_near_kernel(
-    heads, positions, after, dots, dots_near, mine, near, skip, middle, back,
-    dots_sum, near_low, grads_guest, skip_part, middle_part
+    heads, positions, after, dots, dots_near, near, middle, back, near_total,
+    dots_sum, near_low, middle_part
 ):
     slots = near_low.shape[0] // 2
-    rows = 2 * slots + TILE
     shard = lax.axis_index("seq")
     dots_sum[...] = dots[...] + dots_near[...]
     for level in range(4):
@@ -356,23 +384,18 @@
                 near_low[...] = back[...]
                 return
             meet(
-                level == 1,
-                [
-                    (mine, (level - 1) * rows, shard),
-                    (skip, 0, shard - 4), (middle, 0, shard - 2),
-                ],
-                [(near, 0, shard - 2)],
+                level == 1, [(middle, 0, shard - 2)], [(near, 0, shard - 2)],
                 positions, heads, None,
-                Store(slots, [(grads_guest, 0), (skip_part, 0), (middle_part, 0)], True),
-                Store(slots, [(near_low, 0)], True),
+                Store(slots, [(middle_part, 0)], True),
+                Store(slots, [(near_low, 0)], False, [near_total]),
             )
 
 
 def four_last_kernel(
     heads, positions, dots_in, mine, own, other, cross, skip, middle,
-    grads_in, skip_in, middle_in, other_pair, own_in, other_in,
-    dots, grads_guest, skip_back, cross_low, middle_back, other_low, own_near,
-    skip_part, middle_part, other_near,
+    grads_in, skip_in, middle_in, met_pair, own_in, other_in,
+    dots, grads_guest, skip_back, cross_low, middle_back, late, own_near,
+    middle_part, other_near,
 ):
     slots = grads_in.shape[0] // 2
     rows = 2 * slots + TILE
@@ -389,30 +412,26 @@
                 other_near[...] = other_in[...]
             else:
                 far = [(skip, 0, shard - 4), (middle, 0, shard - 2)]
-                parts = [(skip_part, 0), (middle_part, 0)]
                 meet(
-                    level == 1, far, [(own, at * rows, shard), (other, at * rows, shard ^ 1)],
+                    level == 1, far[1:], [(own, at * rows, shard), (other, at * rows, shard ^ 1)],
                     positions, heads, None,
-                    Store(slots, parts, False, [skip_in, middle_in]),
-                    Store(slots, [(own_near, 0), (other_near, 0)], True),
+                    Store(slots, [(middle_part, 0)], False, [middle_in]),
+                    Store(slots, [(own_near, 0), (other_near, 0)], False, [own_in, other_in]),
                 )
                 meet(
                     level == 1, [(mine, at * rows, shard)] + far, [(cross, 0, (shard - 2) ^ 1)],
                     positions, heads, None,
                     Store(
                         slots, [(grads_guest, 0), (skip_back, 0), (middle_back, 0)], False,
-                        [grads_in, skip_part, middle_part],
+                        [grads_in, skip_in, middle_part],
                     ),
                     Store(slots, [(cross_low, 0)], True),
                 )
-            for half in range(2):
-                part = pl.ds(2 * slots * half, 2 * slots)
-                total = jnp.where(meets, other_pair[part, :], 0.0)
-                total = total + other_near[...] if half == at else total
-                other_low[part, :] = total.astype(BF16)
-
-
-def four_sum_kernel(heads, grads, grads_pair, own, near, moving_sum, staying_sum):
+
+    late[...] = (other_near[...] + jnp.where(meets, met_pair[...], 0.0)).astype(BF16)
+
+
+def four_sum_kernel(heads, grads, grads_pair, own, near, early, moving_sum, staying_sum):
     slots = grads.shape[0] // 4
     shard = lax.axis_index("seq")
     meets = meets_pair(shard)
@@ -425,6 +444,7 @@
                 moving = grads[part, :] + jnp.where(meets, grads_pair[part, :], 0.0)
                 staying = own[part, :]
                 if at != (1, 0, 1, 0)[level]:
+                    staying = staying + early[...].astype(F32)
                     if level in (1, 2):
                         moving = moving + near[...].astype(F32)
                     else:
@@ -435,7 +455,7 @@
 
 def four_join_kernel(
     heads, positions, logit, dots, dots_far, moving_sum, staying_sum, grads_guest, own_near,
-    other, middle, skip, cross, query_grad, key_grad, value_grad, router
+    late, skip, cross, middle, query_grad, key_grad, value_grad, router
 ):
     slots, half = moving_sum.shape[0] // 4, moving_sum.shape[1]
     shard = lax.axis_index("seq")
@@ -454,29 +474,26 @@
                 met = at == (1, 0, 1, 0)[level]
                 plus = [grads_guest] if inner and met else []
                 if inner:
-                    extra = [own_near] if met else [middle]
+                    extra = [own_near, late] if met else [middle]
                 else:
-                    extra = [own_near, skip] if met else [cross]
+                    extra = [own_near, skip, late] if met else [cross]
                 for outs, base, more in ((moving, moving_sum, plus), (staying, staying_sum, extra)):
                     for which, out in enumerate(outs):
                         rows = pl.ds((2 * at + which) * slots, slots)
                         total = base[rows, :]
                         for ref in more:
                             total = total + ref[pl.ds(which * slots, slots), :].astype(F32)
-                        if outs is staying:
-                            total = total + other[rows, :].astype(F32)
                         out[:, cols] = total.astype(BF16)
 
 
 def four_levels(prep, shape, positions, logit, slots, heads, width):
     double, block, total = shape(4 * slots + 2 * TILE), shape(2 * slots + TILE), shape(2 * slots, F32)
-    totals, totals_low, low = shape(4 * slots, F32), shape(4 * slots), shape(2 * slots)
+    totals, low = shape(4 * slots, F32), shape(2 * slots)
     own, mine, near_send, far_send, dots = prep(FOUR_PLAN, [double, double, block, block])
     def pairs(levels, flip=0):
         return [(2 * a + c, 2 * b + (c ^ flip)) for a, b in levels for c in range(2)]
 
     near = lax.ppermute(near_send, "seq", pairs([(0, 1), (1, 0), (2, 3), (3, 2)]))
-    cross = lax.ppermute(near, "seq", pairs([(1, 1), (2, 2)], 1))
     other = lax.ppermute(own, "seq", pairs([(i, i) for i in range(4)], 1))
     skip = lax.ppermute(far_send, "seq", pairs([(0, 2), (3, 1)]))
     middle = lax.ppermute(far_send, "seq", pairs([(1, 2), (2, 1)]))
@@ -486,41 +503,52 @@
         [row] + [totals] * 2,
         positions, mine, own,
     )
-    turn, grads_pair, other_total, own_near, other_near, step_back = call(
+    (near,) = call(
+        follow_kernel, [block], near, turn, ins=[pl.ANY, pltpu.VMEM], outs=[pl.ANY], aliases={0: 0}
+    )
+    cross = lax.ppermute(near, "seq", pairs([(1, 1), (2, 2)], 1))
+    turn, grads_pair, met_pair, early = call(
         functools.partial(four_pair_kernel, heads),
-        [row, totals, totals, total, total, low],
-        positions, turn, mine, own, other, near,
+        [row, totals, total, low],
+        positions, turn, mine, other,
+        scratch=[pltpu.VMEM(total.shape, F32)],
+    )
+    early = lax.ppermute(early, "seq", pairs([(i, i) for i in range(4)], 1))
+    turn, own_near, other_near, step_back, near_total, grads_guest, skip_part = call(
+        functools.partial(four_skip_kernel, heads),
+        [row, total, total, low, total, total, total],
+        positions, turn, mine, own, other, near, skip,
     )
     dots_near = lax.ppermute(dots, "tp", [(i, i ^ 1) for i in range(4)])
-    dots, near_low, grads_guest, skip_part, middle_part = call(
+    dots, near_low, middle_part = call(
         functools.partial(four_near_kernel, heads),
-        [row, low, total, total, total],
-        positions, turn, dots, dots_near, mine, near, skip, middle, step_back,
+        [row, low, total],
+        positions, turn, dots, dots_near, near, middle, step_back, near_total,
     )
     near = lax.ppermute(near_low, "seq", pairs([(0, 1), (1, 0), (2, 3), (3, 2)]))
-    dots, grads_guest, skip_back, cross_low, middle_back, other_low, own_near = call(
+    dots, grads_guest, skip_back, cross_low, middle_back, late, own_near = call(
         functools.partial(four_last_kernel, heads),
-        [row, total, low, low, low, totals_low, total],
+        [row, total, low, low, low, low, total],
         positions, dots, mine, own, other, cross, skip, middle,
-        grads_guest, skip_part, middle_part, other_total, own_near, other_near,
-        scratch=[pltpu.VMEM(total.shape, F32)] * 3,
+        grads_guest, skip_part, middle_part, met_pair, own_near, other_near,
+        scratch=[pltpu.VMEM(total.shape, F32)] * 2,
     )
     dots_far = lax.ppermute(dots, "tp", [(i, i ^ 2) for i in range(4)])
     skip = lax.ppermute(skip_back, "seq", pairs([(2, 0), (1, 3)]))
     cross = lax.ppermute(cross_low, "seq", pairs([(1, 0), (2, 3)], 1))
     middle = lax.ppermute(middle_back, "seq", pairs([(1, 2), (2, 1)]))
-    other = lax.ppermute(other_low, "seq", pairs([(i, i) for i in range(4)], 1))
+    late = lax.ppermute(late, "seq", pairs([(i, i) for i in range(4)], 1))
     moving_sum, staying_sum = call(
         functools.partial(four_sum_kernel, heads),
         [totals] * 2,
-        grads, grads_pair, own_total, near,
+        grads, grads_pair, own_total, near, early,
         flops=SUM_FLOPS,
     )
     return call(
         functools.partial(four_join_kernel, heads),
         [shape(slots, BF16, width)] * 3 + [row],
         positions, logit, dots, dots_far, moving_sum, staying_sum, grads_guest, own_near,
-        other, middle, skip, cross,
+        late, skip, cross, middle,
     )
 
 

time: 54 us -> 54.8 us (1.015)
  starting transfers between devices: 23.5 us -> 26.9 us
  waiting for transfers between devices: 17.7 us -> 15 us
    ppermute x1, waiting for transfers between devices: 5.07 us -> 0.01 us  [four_levels(): skip = lax.ppermute(skip_back, 'seq', pairs([(2, 0), (1, 3)]))]
    ppermute x1 -> x2, starting transfers between devices: 1.07 us -> 5.04 us  [the longest x1 3.27 us: four_levels(): late = lax.ppermute(late, 'seq', pairs([(i, i) for i in range(4)], 1))]
    ppermute x1, waiting for transfers between devices: 6.27 us -> 2.66 us  [four_levels(): cross = lax.ppermute(cross_low, 'seq', pairs([(1, 0), (2, 3)], 1))]
    ppermute x1, waiting for transfers between devices: 1.35 us -> 4.85 us  [four_levels(): lax.ppermute(near_low, 'seq', pairs([(0, 1), (1, 0), (2, 3), (3, 2)]))]
    ppermute x1, waiting for transfers between devices: 2.74 us -> 0.01 us  [four_levels(): lax.ppermute(near_send, 'seq', pairs([(0, 1), (1, 0), (2, 3), (3, 2)]))]
    ppermute x1 -> x2, waiting for transfers between devices: 0.49 us -> 3.05 us  [the longest x1 3.05 us: four_levels(): late = lax.ppermute(late, 'seq', pairs([(i, i) for i in range(4)], 1))]
    ppermute x1, waiting for transfers between devices: 0.01 us -> 1.88 us  [four_levels(): other = lax.ppermute(own, 'seq', pairs([(i, i) for i in range(4)], 1))]
    ppermute x1, waiting for transfers between devices: 0.01 us -> 0.81 us  [four_levels(): skip = lax.ppermute(far_send, 'seq', pairs([(0, 2), (3, 1)]))]
  transfers between devices with their start and end apart: 12 -> 13, of which waited for: 6 -> 6; matrix products, arithmetic and copies ran while one was open for 0% -> 0% of each run, Pallas kernels for 8% -> 8%
where the time goes in v4:
time: 54.8 us; the launch traced here: 54.5 us
  starting transfers between devices  26.9 us (49%)
  waiting for transfers between devices  15 us (27%)
  Pallas kernels  9.52 us (17%)
  local copies, waits for them, and re-layouts  2.16 us (4%)
  between operations  0.83 us (2%)
    pallas_call x9, Pallas kernels, call(): pl.pallas_call(kernel, out_shape=out_shape, in_specs=[pl.BlockSpec(memory...  9.52 us
    ppermute x1, starting transfers between devices, four_levels(): lax.ppermute(near_low, 'seq', pairs([(0, 1), (1, 0), (2, 3), (3, 2)]))  6.23 us
    ppermute x1, waiting for transfers between devices, four_levels(): lax.ppermute(near_low, 'seq', pairs([(0, 1), (1, 0), (2, 3), (3, 2)]))  4.85 us
    ppermute x1, starting transfers between devices, four_levels(): skip = lax.ppermute(far_send, 'seq', pairs([(0, 2), (3, 1)]))  4.56 us
    ppermute x1, starting transfers between devices, four_levels(): late = lax.ppermute(late, 'seq', pairs([(i, i) for i in range(4)], 1))  3.27 us
    ppermute x1, waiting for transfers between devices, four_levels(): late = lax.ppermute(late, 'seq', pairs([(i, i) for i in range(4)], 1))  3.05 us
    ppermute x1, starting transfers between devices, four_levels(): other = lax.ppermute(own, 'seq', pairs([(i, i) for i in range(4)], 1))  3.03 us
    ppermute x1, waiting for transfers between devices, four_levels(): cross = lax.ppermute(cross_low, 'seq', pairs([(1, 0), (2, 3)], 1))  2.66 us
  transfers between devices with their start and end apart: 13, of which 6 were waited for; matrix products, arithmetic and copies ran while one was open for 0% of the time, Pallas kernels for 8%

profile of v4, /device:TPU:0, one launch (start us, length us, event | category | flops | bytes accessed | tf_op | source)
XLA Modules:
  0.0 54.5 jit_solution(14758379867246972186)
XLA Ops:
  0.6 3.8 %shard_map.111 = (f32[1,192]{1,0:T(1,128)}, bf16[800,384]{1,0:T(8,128)(2,1)}, bf16[800,384]{1,0:T(8,128)(2,1)}, bf16[400,384]{1,0:T(8,128)(2,1)}, bf16[400,384]{1,0:T(8,128)(2,1)}) custom-call(bf16[192,768]{1,0:T(8,128)(2,1)} %refs_0_.1, bf16[192,768]{1,0:T(8,128)(2,1)} %refs_1_.1, f32[1,192]{1,0:T(1,128)} %bitcast.11, f32[6,192]{1,0:T(8,128)} %bitcast.13, ...), custom_call_target="tpu_custom_call" | custom-call | flops 1024 | bytes 1024 | tf_op jit(solution)/shard_map/pallas_call | solution.py:662
  4.4 0.0 copy-start.6
  4.4 3.0 %collective-permute-start = (bf16[800,384]{1,0:T(8,128)(2,1)}, bf16[800,384]{1,0:T(8,128)(2,1)S(1)}, u32[]{:S(2)}, u32[]{:S(2)}) collective-permute-start(bf16[800,384]{1,0:T(8,128)(2,1)} %get-tuple-element.40.own), channel_id=1, source_target_pairs={{0,4},{4,0},{8,12},{12,8},{16,20},{20,16},{24,28},{28,24},{1,5},{5... | collective-permute-start | bytes 1843208 | tf_op jit(solution)/shard_map/ppermute | solution.py:497
  7.5 1.7 %collective-permute-start.1 = (bf16[400,384]{1,0:T(8,128)(2,1)}, bf16[400,384]{1,0:T(8,128)(2,1)S(1)}, u32[]{:S(2)}, u32[]{:S(2)}) collective-permute-start(bf16[400,384]{1,0:T(8,128)(2,1)} %get-tuple-element.43), channel_id=1, source_target_pairs={{0,8},{4,12},{8,0},{12,4},{16,24},{20,28},{24,16},{28,20},{1,9},{5... | collective-permute-start | bytes 921608 | tf_op jit(solution)/shard_map/ppermute | solution.py:496
  9.2 4.6 %collective-permute-start.2 = (bf16[400,384]{1,0:T(8,128)(2,1)}, bf16[400,384]{1,0:T(8,128)(2,1)S(1)}, u32[]{:S(2)}, u32[]{:S(2)}) collective-permute-start(bf16[400,384]{1,0:T(8,128)(2,1)} %get-tuple-element.44), channel_id=1, source_target_pairs={{0,16},{4,20},{24,8},{28,12},{1,17},{5,21},{25,9},{29,13},{2,18},{... | collective-permute-start | bytes 921608 | tf_op jit(solution)/shard_map/ppermute | solution.py:498
  13.8 0.7 %collective-permute-start.4 = (bf16[400,384]{1,0:T(8,128)(2,1)}, bf16[400,384]{1,0:T(8,128)(2,1)S(1)}, u32[]{:S(2)}, u32[]{:S(2)}) collective-permute-start(bf16[400,384]{1,0:T(8,128)(2,1)} %get-tuple-element.44), channel_id=1, source_target_pairs={{8,16},{12,20},{16,8},{20,12},{9,17},{13,21},{17,9},{21,13},{10,18... | collective-permute-start | bytes 921608 | tf_op jit(solution)/shard_map/ppermute | solution.py:499
  14.5 1.1 %copy-done = bf16[800,384]{1,0:T(8,128)(2,1)S(1)} copy-done((bf16[800,384]{1,0:T(8,128)(2,1)S(1)}, bf16[800,384]{1,0:T(8,128)(2,1)}, u32[]{:S(2)}) %copy-start) | copy-done | bytes 614424
  15.5 1.1 %copy-done.2 = bf16[800,384]{1,0:T(8,128)(2,1)S(1)} copy-done((bf16[800,384]{1,0:T(8,128)(2,1)S(1)}, bf16[800,384]{1,0:T(8,128)(2,1)}, u32[]{:S(2)}) %copy-start.2) | copy-done | bytes 614424
  16.6 2.1 %shard_map.112 = (f32[1,192]{1,0:T(1,128)S(1)}, f32[768,384]{1,0:T(8,128)S(1)}, f32[768,384]{1,0:T(8,128)S(1)}) custom-call(s32[12,128]{1,0:T(8,128)S(1)} %bitcast.5, bf16[800,384]{1,0:T(8,128)(2,1)S(1)} %copy-done, bf16[800,384]{1,0:T(8,128)(2,1)S(1)} %copy-done.2), custom_call_target="tpu_custom_call" | custom-call | flops 1024 | bytes 1024 | tf_op jit(solution)/shard_map/pallas_call | solution.py:662
  18.7 0.0 collective-permute-done.1.block
  18.8 0.8 %collective-permute-start.5 = (bf16[400,384]{1,0:T(8,128)(2,1)S(1)}, bf16[400,384]{1,0:T(8,128)(2,1)S(1)}, u32[]{:S(2)}, u32[]{:S(2)}) collective-permute-start(bf16[400,384]{1,0:T(8,128)(2,1)S(1)} %shard_map.114.near), channel_id=1, source_target_pairs={{8,12},{12,8},{16,20},{20,16},{9,13},{13,9},{17,21},{21,17},{10,14... | collective-permute-start | bytes 921608 | tf_op jit(solution)/shard_map/ppermute | solution.py:509
  19.6 0.1 collective-permute-start.3
  19.7 1.9 %collective-permute-done.other = bf16[800,384]{1,0:T(8,128)(2,1)S(1)} collective-permute-done((bf16[800,384]{1,0:T(8,128)(2,1)}, bf16[800,384]{1,0:T(8,128)(2,1)S(1)}, u32[]{:S(2)}, u32[]{:S(2)}) %collective-permute-start) | collective-permute-done | bytes 614432 | tf_op jit(solution)/shard_map/ppermute | solution.py:497
  21.6 0.8 %collective-permute-done.2.skip = bf16[400,384]{1,0:T(8,128)(2,1)S(1)} collective-permute-done((bf16[400,384]{1,0:T(8,128)(2,1)}, bf16[400,384]{1,0:T(8,128)(2,1)S(1)}, u32[]{:S(2)}, u32[]{:S(2)}) %collective-permute-start.2) | collective-permute-done | bytes 307232 | tf_op jit(solution)/shard_map/ppermute | solution.py:498
  22.4 1.7 %shard_map.115 = (f32[1,192]{1,0:T(1,128)S(1)}, f32[384,384]{1,0:T(8,128)S(1)}, f32[384,384]{1,0:T(8,128)S(1)}, bf16[384,384]{1,0:T(8,128)(2,1)S(1)}, f32[384,38...) custom-call(s32[12,128]{1,0:T(8,128)S(1)} %bitcast.7, f32[1,192]{1,0:T(1,128)S(1)} %get-tuple-element.42.after, ...), custom_call_target="tpu_custom_call" | custom-call | flops 1024 | bytes 1024 | tf_op jit(solution)/shard_map/pallas_call | solution.py:662
  24.1 0.0 collective-permute-done.3.dots_near
  24.1 0.1 shard_map.116
  24.2 6.2 %collective-permute-start.7 = (bf16[384,384]{1,0:T(8,128)(2,1)S(1)}, bf16[384,384]{1,0:T(8,128)(2,1)S(1)}, u32[]{:S(2)}, u32[]{:S(2)}) collective-permute-start(bf16[384,384]{1,0:T(8,128)(2,1)S(1)} %get-tuple-element.60), channel_id=1, source_target_pairs={{0,8},{4,12},{8,0},{12,4},{16,24},{20,28},{24,16},{28,20},{1,9},{5... | collective-permute-start | bytes 884744 | tf_op jit(solution)/shard_map/ppermute | solution.py:528
  30.4 1.8 %collective-permute-start.8 = (bf16[384,384]{1,0:T(8,128)(2,1)S(1)}, bf16[384,384]{1,0:T(8,128)(2,1)S(1)}, u32[]{:S(2)}, u32[]{:S(2)}) collective-permute-start(bf16[384,384]{1,0:T(8,128)(2,1)S(1)} %get-tuple-element.61), channel_id=1, source_target_pairs={{0,4},{4,0},{8,12},{12,8},{16,20},{20,16},{24,28},{28,24},{1,5},{5... | collective-permute-start | bytes 884744 | tf_op jit(solution)/shard_map/ppermute | solution.py:516
  32.2 0.0 collective-permute-done.5.cross
  32.2 0.4 shard_map.117
  32.6 1.3 %collective-permute-start.10 = (bf16[384,384]{1,0:T(8,128)(2,1)S(1)}, bf16[384,384]{1,0:T(8,128)(2,1)S(1)}, u32[]{:S(2)}, u32[]{:S(2)}) collective-permute-start(bf16[384,384]{1,0:T(8,128)(2,1)S(1)} %get-tuple-element.67), channel_id=1, source_target_pairs={{16,0},{20,4},{8,24},{12,28},{17,1},{21,5},{9,25},{13,29},{18,2},{... | collective-permute-start | bytes 884744 | tf_op jit(solution)/shard_map/ppermute | solution.py:537
  33.9 1.3 %collective-permute-start.11 = (bf16[384,384]{1,0:T(8,128)(2,1)S(1)}, bf16[384,384]{1,0:T(8,128)(2,1)S(1)}, u32[]{:S(2)}, u32[]{:S(2)}) collective-permute-start(bf16[384,384]{1,0:T(8,128)(2,1)S(1)} %get-tuple-element.68), channel_id=1, source_target_pairs={{8,4},{12,0},{16,28},{20,24},{9,5},{13,1},{17,29},{21,25},{10,6},{... | collective-permute-start | bytes 884744 | tf_op jit(solution)/shard_map/ppermute | solution.py:538
  35.2 0.7 %collective-permute-start.12 = (bf16[384,384]{1,0:T(8,128)(2,1)S(1)}, bf16[384,384]{1,0:T(8,128)(2,1)S(1)}, u32[]{:S(2)}, u32[]{:S(2)}) collective-permute-start(bf16[384,384]{1,0:T(8,128)(2,1)S(1)} %get-tuple-element.69), channel_id=1, source_target_pairs={{8,16},{12,20},{16,8},{20,12},{9,17},{13,21},{17,9},{21,13},{10,18... | collective-permute-start | bytes 884744 | tf_op jit(solution)/shard_map/ppermute | solution.py:539
  35.8 4.8 %collective-permute-done.7.near = bf16[384,384]{1,0:T(8,128)(2,1)S(1)} collective-permute-done((bf16[384,384]{1,0:T(8,128)(2,1)S(1)}, bf16[384,384]{1,0:T(8,128)(2,1)S(1)}, u32[]{:S(2)}, u32[]{:S(2)}) %collective-permute-start.7) | collective-permute-done | bytes 294944 | tf_op jit(solution)/shard_map/ppermute | solution.py:528
  40.7 3.3 %collective-permute-start.9 = (bf16[384,384]{1,0:T(8,128)(2,1)S(1)}, bf16[384,384]{1,0:T(8,128)(2,1)S(1)}, u32[]{:S(2)}, u32[]{:S(2)}) collective-permute-start(bf16[384,384]{1,0:T(8,128)(2,1)S(1)} %get-tuple-element.66), channel_id=1, source_target_pairs={{0,4},{4,0},{8,12},{12,8},{16,20},{20,16},{24,28},{28,24},{1,5},{5... | collective-permute-start | bytes 884744 | tf_op jit(solution)/shard_map/ppermute | solution.py:540
  44.0 1.5 %collective-permute-start.6 = (f32[1,192]{1,0:T(1,128)S(1)}, f32[1,192]{1,0:T(1,128)S(1)}, u32[]{:S(2)}, u32[]{:S(2)}) collective-permute-start(f32[1,192]{1,0:T(1,128)S(1)} %get-tuple-element.56.dots), channel_id=1, source_target_pairs={{0,2},{1,3},{2,0},{3,1},{4,6},{5,7},{6,4},{7,5},{8,10},{9,11},{10,... | collective-permute-start | bytes 2312 | tf_op jit(solution)/shard_map/ppermute | solution.py:536
  45.5 0.3 shard_map.118
  45.8 1.7 %collective-permute-done.6.dots_far = f32[1,192]{1,0:T(1,128)S(1)} collective-permute-done((f32[1,192]{1,0:T(1,128)S(1)}, f32[1,192]{1,0:T(1,128)S(1)}, u32[]{:S(2)}, u32[]{:S(2)}) %collective-permute-start.6) | collective-permute-done | bytes 800 | tf_op jit(solution)/shard_map/ppermute | solution.py:536
  47.5 2.7 %collective-permute-done.11.cross = bf16[384,384]{1,0:T(8,128)(2,1)S(1)} collective-permute-done((bf16[384,384]{1,0:T(8,128)(2,1)S(1)}, bf16[384,384]{1,0:T(8,128)(2,1)S(1)}, u32[]{:S(2)}, u32[]{:S(2)}) %collective-permute-start.11) | collective-permute-done | bytes 294944 | tf_op jit(solution)/shard_map/ppermute | solution.py:538
  50.2 3.1 %collective-permute-done.9.late = bf16[384,384]{1,0:T(8,128)(2,1)S(1)} collective-permute-done((bf16[384,384]{1,0:T(8,128)(2,1)S(1)}, bf16[384,384]{1,0:T(8,128)(2,1)S(1)}, u32[]{:S(2)}, u32[]{:S(2)}) %collective-permute-start.9) | collective-permute-done | bytes 294944 | tf_op jit(solution)/shard_map/ppermute | solution.py:540
  53.2 1.2 %shard_map.119 = (bf16[192,768]{1,0:T(8,128)(2,1)}, bf16[192,768]{1,0:T(8,128)(2,1)}, bf16[192,768]{1,0:T(8,128)(2,1)}, f32[1,192]{1,0:T(1,128)}) custom-call(s32[12,128]{1,0:T(8,128)S(1)} %bitcast.10, f32[1,192]{1,0:T(1,128)S(1)} %bitcast.12, f32[1,192]{1,0:T(1,128)S(1)} %get-tuple-element.56.dots, f32[1,192]{1,0:T(1,128)S(1)} %collective-permute-done.6.dots_far, ...), custom_call_target="tpu_custom_call" | custom-call | flops 1024 | bytes 1024 | tf_op jit(solution)/shard_map/pallas_call | solution.py:662
  (17 shorter events, 0.1 us)
Async XLA Ops:
  0.6 13.8 %copy-start.4 = (s32[1536]{0:T(1024)S(1)}, s32[1536]{0:T(1024)}, u32[]{:S(2)}) copy-start(s32[1536]{0:T(1024)} %param.15) | copy-start | bytes 18436
  4.4 15.1 %copy-start.6 = (f32[1,192]{1,0:T(1,128)S(1)}, f32[1,192]{1,0:T(1,128)}, u32[]{:S(2)}) copy-start(f32[1,192]{1,0:T(1,128)} %get-tuple-element.46.dots) | copy-start | bytes 2308
  4.4 17.1 %collective-permute-start = (bf16[800,384]{1,0:T(8,128)(2,1)}, bf16[800,384]{1,0:T(8,128)(2,1)S(1)}, u32[]{:S(2)}, u32[]{:S(2)}) collective-permute-start(bf16[800,384]{1,0:T(8,128)(2,1)} %get-tuple-element.40.own), channel_id=1, source_target_pairs={{0,4},{4,0},{8,12},{12,8},{16,20},{20,16},{24,28},{28,24},{1,5},{5... | collective-permute-start | bytes 1843208 | tf_op jit(solution)/shard_map/ppermute | solution.py:497
  7.5 11.3 %collective-permute-start.1 = (bf16[400,384]{1,0:T(8,128)(2,1)}, bf16[400,384]{1,0:T(8,128)(2,1)S(1)}, u32[]{:S(2)}, u32[]{:S(2)}) collective-permute-start(bf16[400,384]{1,0:T(8,128)(2,1)} %get-tuple-element.43), channel_id=1, source_target_pairs={{0,8},{4,12},{8,0},{12,4},{16,24},{20,28},{24,16},{28,20},{1,9},{5... | collective-permute-start | bytes 921608 | tf_op jit(solution)/shard_map/ppermute | solution.py:496
  9.2 13.2 %collective-permute-start.2 = (bf16[400,384]{1,0:T(8,128)(2,1)}, bf16[400,384]{1,0:T(8,128)(2,1)S(1)}, u32[]{:S(2)}, u32[]{:S(2)}) collective-permute-start(bf16[400,384]{1,0:T(8,128)(2,1)} %get-tuple-element.44), channel_id=1, source_target_pairs={{0,16},{4,20},{24,8},{28,12},{1,17},{5,21},{25,9},{29,13},{2,18},{... | collective-permute-start | bytes 921608 | tf_op jit(solution)/shard_map/ppermute | solution.py:498
  13.8 10.3 %collective-permute-start.4 = (bf16[400,384]{1,0:T(8,128)(2,1)}, bf16[400,384]{1,0:T(8,128)(2,1)S(1)}, u32[]{:S(2)}, u32[]{:S(2)}) collective-permute-start(bf16[400,384]{1,0:T(8,128)(2,1)} %get-tuple-element.44), channel_id=1, source_target_pairs={{8,16},{12,20},{16,8},{20,12},{9,17},{13,21},{17,9},{21,13},{10,18... | collective-permute-start | bytes 921608 | tf_op jit(solution)/shard_map/ppermute | solution.py:499
  14.5 1.1 %copy-start = (bf16[800,384]{1,0:T(8,128)(2,1)S(1)}, bf16[800,384]{1,0:T(8,128)(2,1)}, u32[]{:S(2)}) copy-start(bf16[800,384]{1,0:T(8,128)(2,1)} %get-tuple-element.39.mine) | copy-start | bytes 1843204
  15.5 1.1 %copy-start.2 = (bf16[800,384]{1,0:T(8,128)(2,1)S(1)}, bf16[800,384]{1,0:T(8,128)(2,1)}, u32[]{:S(2)}) copy-start(bf16[800,384]{1,0:T(8,128)(2,1)} %get-tuple-element.40.own) | copy-start | bytes 1843204
  16.6 4.9 %copy-start.1 = (bf16[800,384]{1,0:T(8,128)(2,1)S(1)}, bf16[800,384]{1,0:T(8,128)(2,1)}, u32[]{:S(2)}) copy-start(bf16[800,384]{1,0:T(8,128)(2,1)} %get-tuple-element.39.mine) | copy-start | bytes 1843204
  18.7 3.7 %copy-start.3 = (bf16[800,384]{1,0:T(8,128)(2,1)S(1)}, bf16[800,384]{1,0:T(8,128)(2,1)}, u32[]{:S(2)}) copy-start(bf16[800,384]{1,0:T(8,128)(2,1)} %get-tuple-element.40.own) | copy-start | bytes 1843204
  18.8 13.4 %collective-permute-start.5 = (bf16[400,384]{1,0:T(8,128)(2,1)S(1)}, bf16[400,384]{1,0:T(8,128)(2,1)S(1)}, u32[]{:S(2)}, u32[]{:S(2)}) collective-permute-start(bf16[400,384]{1,0:T(8,128)(2,1)S(1)} %shard_map.114.near), channel_id=1, source_target_pairs={{8,12},{12,8},{16,20},{20,16},{9,13},{13,9},{17,21},{21,17},{10,14... | collective-permute-start | bytes 921608 | tf_op jit(solution)/shard_map/ppermute | solution.py:509
  19.6 4.5 %collective-permute-start.3 = (f32[1,192]{1,0:T(1,128)S(1)}, f32[1,192]{1,0:T(1,128)S(1)}, u32[]{:S(2)}, u32[]{:S(2)}) collective-permute-start(f32[1,192]{1,0:T(1,128)S(1)} %copy-done.6), channel_id=1, source_target_pairs={{0,1},{1,0},{2,3},{3,2},{4,5},{5,4},{6,7},{7,6},{8,9},{9,8},{10,11... | collective-permute-start | bytes 2312 | tf_op jit(solution)/shard_map/ppermute | solution.py:522
  24.2 16.5 %collective-permute-start.7 = (bf16[384,384]{1,0:T(8,128)(2,1)S(1)}, bf16[384,384]{1,0:T(8,128)(2,1)S(1)}, u32[]{:S(2)}, u32[]{:S(2)}) collective-permute-start(bf16[384,384]{1,0:T(8,128)(2,1)S(1)} %get-tuple-element.60), channel_id=1, source_target_pairs={{0,8},{4,12},{8,0},{12,4},{16,24},{20,28},{24,16},{28,20},{1,9},{5... | collective-permute-start | bytes 884744 | tf_op jit(solution)/shard_map/ppermute | solution.py:528
  30.4 13.6 %collective-permute-start.8 = (bf16[384,384]{1,0:T(8,128)(2,1)S(1)}, bf16[384,384]{1,0:T(8,128)(2,1)S(1)}, u32[]{:S(2)}, u32[]{:S(2)}) collective-permute-start(bf16[384,384]{1,0:T(8,128)(2,1)S(1)} %get-tuple-element.61), channel_id=1, source_target_pairs={{0,4},{4,0},{8,12},{12,8},{16,20},{20,16},{24,28},{28,24},{1,5},{5... | collective-permute-start | bytes 884744 | tf_op jit(solution)/shard_map/ppermute | solution.py:516
  32.6 15.0 %collective-permute-start.10 = (bf16[384,384]{1,0:T(8,128)(2,1)S(1)}, bf16[384,384]{1,0:T(8,128)(2,1)S(1)}, u32[]{:S(2)}, u32[]{:S(2)}) collective-permute-start(bf16[384,384]{1,0:T(8,128)(2,1)S(1)} %get-tuple-element.67), channel_id=1, source_target_pairs={{16,0},{20,4},{8,24},{12,28},{17,1},{21,5},{9,25},{13,29},{18,2},{... | collective-permute-start | bytes 884744 | tf_op jit(solution)/shard_map/ppermute | solution.py:537
  33.9 16.3 %collective-permute-start.11 = (bf16[384,384]{1,0:T(8,128)(2,1)S(1)}, bf16[384,384]{1,0:T(8,128)(2,1)S(1)}, u32[]{:S(2)}, u32[]{:S(2)}) collective-permute-start(bf16[384,384]{1,0:T(8,128)(2,1)S(1)} %get-tuple-element.68), channel_id=1, source_target_pairs={{8,4},{12,0},{16,28},{20,24},{9,5},{13,1},{17,29},{21,25},{10,6},{... | collective-permute-start | bytes 884744 | tf_op jit(solution)/shard_map/ppermute | solution.py:538
  35.2 15.0 %collective-permute-start.12 = (bf16[384,384]{1,0:T(8,128)(2,1)S(1)}, bf16[384,384]{1,0:T(8,128)(2,1)S(1)}, u32[]{:S(2)}, u32[]{:S(2)}) collective-permute-start(bf16[384,384]{1,0:T(8,128)(2,1)S(1)} %get-tuple-element.69), channel_id=1, source_target_pairs={{8,16},{12,20},{16,8},{20,12},{9,17},{13,21},{17,9},{21,13},{10,18... | collective-permute-start | bytes 884744 | tf_op jit(solution)/shard_map/ppermute | solution.py:539
  40.7 12.6 %collective-permute-start.9 = (bf16[384,384]{1,0:T(8,128)(2,1)S(1)}, bf16[384,384]{1,0:T(8,128)(2,1)S(1)}, u32[]{:S(2)}, u32[]{:S(2)}) collective-permute-start(bf16[384,384]{1,0:T(8,128)(2,1)S(1)} %get-tuple-element.66), channel_id=1, source_target_pairs={{0,4},{4,0},{8,12},{12,8},{16,20},{20,16},{24,28},{28,24},{1,5},{5... | collective-permute-start | bytes 884744 | tf_op jit(solution)/shard_map/ppermute | solution.py:540
  44.0 3.6 %collective-permute-start.6 = (f32[1,192]{1,0:T(1,128)S(1)}, f32[1,192]{1,0:T(1,128)S(1)}, u32[]{:S(2)}, u32[]{:S(2)}) collective-permute-start(f32[1,192]{1,0:T(1,128)S(1)} %get-tuple-element.56.dots), channel_id=1, source_target_pairs={{0,2},{1,3},{2,0},{3,1},{4,6},{5,7},{6,4},{7,5},{8,10},{9,11},{10,... | collective-permute-start | bytes 2312 | tf_op jit(solution)/shard_map/ppermute | solution.py:536
  45.5 7.8 %copy-start.5 = (f32[192]{0:T(256)S(1)}, f32[192]{0:T(256)}, u32[]{:S(2)}) copy-start(f32[192]{0:T(256)} %param.14) | copy-start | bytes 2308

commit v5 on v4

--- a/solution.py
+++ b/solution.py
@@ -455,7 +455,7 @@
 
 def four_join_kernel(
     heads, positions, logit, dots, dots_far, moving_sum, staying_sum, grads_guest, own_near,
-    late, skip, cross, middle, query_grad, key_grad, value_grad, router
+    middle, skip, cross, late, query_grad, key_grad, value_grad, router
 ):
     slots, half = moving_sum.shape[0] // 4, moving_sum.shape[1]
     shard = lax.axis_index("seq")
@@ -548,7 +548,7 @@
         functools.partial(four_join_kernel, heads),
         [shape(slots, BF16, width)] * 3 + [row],
         positions, logit, dots, dots_far, moving_sum, staying_sum, grads_guest, own_near,
-        late, skip, cross, middle,
+        middle, skip, cross, late,
     )
 
 

time: 54.8 us -> 51.9 us (0.947)
  starting transfers between devices: 26.9 us -> 24 us
    ppermute x1, starting transfers between devices: 3.27 us -> 0.36 us  [four_levels(): late = lax.ppermute(late, 'seq', pairs([(i, i) for i in range(4)], 1))]
    ppermute x1, waiting for transfers between devices: 3.05 us -> 0.18 us  [four_levels(): late = lax.ppermute(late, 'seq', pairs([(i, i) for i in range(4)], 1))]
    ppermute x1, waiting for transfers between devices: 2.66 us -> 4.79 us  [four_levels(): cross = lax.ppermute(cross_low, 'seq', pairs([(1, 0), (2, 3)], 1))]
    ppermute x1, waiting for transfers between devices: 4.85 us -> 5.57 us  [four_levels(): lax.ppermute(near_low, 'seq', pairs([(0, 1), (1, 0), (2, 3), (3, 2)]))]
  transfers between devices with their start and end apart: 13 -> 13, of which waited for: 6 -> 6; matrix products, arithmetic and copies ran while one was open for 0% -> 0% of each run, Pallas kernels for 8% -> 9%
where the time goes in v5:
time: 51.9 us; the launch traced here: 51.6 us
  starting transfers between devices  24 us (46%)
  waiting for transfers between devices  15 us (29%)
  Pallas kernels  9.52 us (18%)
  local copies, waits for them, and re-layouts  2.16 us (4%)
  between operations  0.84 us (2%)
    pallas_call x9, Pallas kernels, call(): pl.pallas_call(kernel, out_shape=out_shape, in_specs=[pl.BlockSpec(memory...  9.52 us
    ppermute x1, starting transfers between devices, four_levels(): lax.ppermute(near_low, 'seq', pairs([(0, 1), (1, 0), (2, 3), (3, 2)]))  6.23 us
    ppermute x1, waiting for transfers between devices, four_levels(): lax.ppermute(near_low, 'seq', pairs([(0, 1), (1, 0), (2, 3), (3, 2)]))  5.57 us
    ppermute x1, waiting for transfers between devices, four_levels(): cross = lax.ppermute(cross_low, 'seq', pairs([(1, 0), (2, 3)], 1))  4.79 us
    ppermute x1, starting transfers between devices, four_levels(): skip = lax.ppermute(far_send, 'seq', pairs([(0, 2), (3, 1)]))  4.56 us
    ppermute x1, starting transfers between devices, four_levels(): other = lax.ppermute(own, 'seq', pairs([(i, i) for i in range(4)], 1))  3.03 us
    unnamed x14, local copies, waits for them, and re-layouts  2.16 us
    ppermute x1, waiting for transfers between devices, four_levels(): other = lax.ppermute(own, 'seq', pairs([(i, i) for i in range(4)], 1))  1.88 us
  transfers between devices with their start and end apart: 13, of which 6 were waited for; matrix products, arithmetic and copies ran while one was open for 0% of the time, Pallas kernels for 9%

profile of v5, /device:TPU:0, one launch (start us, length us, event | category | flops | bytes accessed | tf_op | source)
XLA Modules:
  0.0 51.6 jit_solution(12508257800265189690)
XLA Ops:
  0.6 3.8 %shard_map.111 = (f32[1,192]{1,0:T(1,128)}, bf16[800,384]{1,0:T(8,128)(2,1)}, bf16[800,384]{1,0:T(8,128)(2,1)}, bf16[400,384]{1,0:T(8,128)(2,1)}, bf16[400,384]{1,0:T(8,128)(2,1)}) custom-call(bf16[192,768]{1,0:T(8,128)(2,1)} %refs_0_.1, bf16[192,768]{1,0:T(8,128)(2,1)} %refs_1_.1, f32[1,192]{1,0:T(1,128)} %bitcast.11, f32[6,192]{1,0:T(8,128)} %bitcast.13, ...), custom_call_target="tpu_custom_call" | custom-call | flops 1024 | bytes 1024 | tf_op jit(solution)/shard_map/pallas_call | solution.py:662
  4.4 0.0 copy-start.6
  4.4 3.0 %collective-permute-start = (bf16[800,384]{1,0:T(8,128)(2,1)}, bf16[800,384]{1,0:T(8,128)(2,1)S(1)}, u32[]{:S(2)}, u32[]{:S(2)}) collective-permute-start(bf16[800,384]{1,0:T(8,128)(2,1)} %get-tuple-element.40.own), channel_id=1, source_target_pairs={{0,4},{4,0},{8,12},{12,8},{16,20},{20,16},{24,28},{28,24},{1,5},{5... | collective-permute-start | bytes 1843208 | tf_op jit(solution)/shard_map/ppermute | solution.py:497
  7.5 1.7 %collective-permute-start.1 = (bf16[400,384]{1,0:T(8,128)(2,1)}, bf16[400,384]{1,0:T(8,128)(2,1)S(1)}, u32[]{:S(2)}, u32[]{:S(2)}) collective-permute-start(bf16[400,384]{1,0:T(8,128)(2,1)} %get-tuple-element.43), channel_id=1, source_target_pairs={{0,8},{4,12},{8,0},{12,4},{16,24},{20,28},{24,16},{28,20},{1,9},{5... | collective-permute-start | bytes 921608 | tf_op jit(solution)/shard_map/ppermute | solution.py:496
  9.2 4.6 %collective-permute-start.2 = (bf16[400,384]{1,0:T(8,128)(2,1)}, bf16[400,384]{1,0:T(8,128)(2,1)S(1)}, u32[]{:S(2)}, u32[]{:S(2)}) collective-permute-start(bf16[400,384]{1,0:T(8,128)(2,1)} %get-tuple-element.44), channel_id=1, source_target_pairs={{0,16},{4,20},{24,8},{28,12},{1,17},{5,21},{25,9},{29,13},{2,18},{... | collective-permute-start | bytes 921608 | tf_op jit(solution)/shard_map/ppermute | solution.py:498
  13.8 0.7 %collective-permute-start.4 = (bf16[400,384]{1,0:T(8,128)(2,1)}, bf16[400,384]{1,0:T(8,128)(2,1)S(1)}, u32[]{:S(2)}, u32[]{:S(2)}) collective-permute-start(bf16[400,384]{1,0:T(8,128)(2,1)} %get-tuple-element.44), channel_id=1, source_target_pairs={{8,16},{12,20},{16,8},{20,12},{9,17},{13,21},{17,9},{21,13},{10,18... | collective-permute-start | bytes 921608 | tf_op jit(solution)/shard_map/ppermute | solution.py:499
  14.5 1.1 %copy-done = bf16[800,384]{1,0:T(8,128)(2,1)S(1)} copy-done((bf16[800,384]{1,0:T(8,128)(2,1)S(1)}, bf16[800,384]{1,0:T(8,128)(2,1)}, u32[]{:S(2)}) %copy-start) | copy-done | bytes 614424
  15.5 1.1 %copy-done.2 = bf16[800,384]{1,0:T(8,128)(2,1)S(1)} copy-done((bf16[800,384]{1,0:T(8,128)(2,1)S(1)}, bf16[800,384]{1,0:T(8,128)(2,1)}, u32[]{:S(2)}) %copy-start.2) | copy-done | bytes 614424
  16.6 2.1 %shard_map.112 = (f32[1,192]{1,0:T(1,128)S(1)}, f32[768,384]{1,0:T(8,128)S(1)}, f32[768,384]{1,0:T(8,128)S(1)}) custom-call(s32[12,128]{1,0:T(8,128)S(1)} %bitcast.5, bf16[800,384]{1,0:T(8,128)(2,1)S(1)} %copy-done, bf16[800,384]{1,0:T(8,128)(2,1)S(1)} %copy-done.2), custom_call_target="tpu_custom_call" | custom-call | flops 1024 | bytes 1024 | tf_op jit(solution)/shard_map/pallas_call | solution.py:662
  18.7 0.0 collective-permute-done.1.block
  18.8 0.8 %collective-permute-start.5 = (bf16[400,384]{1,0:T(8,128)(2,1)S(1)}, bf16[400,384]{1,0:T(8,128)(2,1)S(1)}, u32[]{:S(2)}, u32[]{:S(2)}) collective-permute-start(bf16[400,384]{1,0:T(8,128)(2,1)S(1)} %shard_map.114.near), channel_id=1, source_target_pairs={{8,12},{12,8},{16,20},{20,16},{9,13},{13,9},{17,21},{21,17},{10,14... | collective-permute-start | bytes 921608 | tf_op jit(solution)/shard_map/ppermute | solution.py:509
  19.6 0.1 collective-permute-start.3
  19.7 1.9 %collective-permute-done.other = bf16[800,384]{1,0:T(8,128)(2,1)S(1)} collective-permute-done((bf16[800,384]{1,0:T(8,128)(2,1)}, bf16[800,384]{1,0:T(8,128)(2,1)S(1)}, u32[]{:S(2)}, u32[]{:S(2)}) %collective-permute-start) | collective-permute-done | bytes 614432 | tf_op jit(solution)/shard_map/ppermute | solution.py:497
  21.6 0.8 %collective-permute-done.2.skip = bf16[400,384]{1,0:T(8,128)(2,1)S(1)} collective-permute-done((bf16[400,384]{1,0:T(8,128)(2,1)}, bf16[400,384]{1,0:T(8,128)(2,1)S(1)}, u32[]{:S(2)}, u32[]{:S(2)}) %collective-permute-start.2) | collective-permute-done | bytes 307232 | tf_op jit(solution)/shard_map/ppermute | solution.py:498
  22.4 1.7 %shard_map.115 = (f32[1,192]{1,0:T(1,128)S(1)}, f32[384,384]{1,0:T(8,128)S(1)}, f32[384,384]{1,0:T(8,128)S(1)}, bf16[384,384]{1,0:T(8,128)(2,1)S(1)}, f32[384,38...) custom-call(s32[12,128]{1,0:T(8,128)S(1)} %bitcast.7, f32[1,192]{1,0:T(1,128)S(1)} %get-tuple-element.42.after, ...), custom_call_target="tpu_custom_call" | custom-call | flops 1024 | bytes 1024 | tf_op jit(solution)/shard_map/pallas_call | solution.py:662
  24.1 0.0 collective-permute-done.3.dots_near
  24.1 0.1 shard_map.116
  24.2 6.2 %collective-permute-start.7 = (bf16[384,384]{1,0:T(8,128)(2,1)S(1)}, bf16[384,384]{1,0:T(8,128)(2,1)S(1)}, u32[]{:S(2)}, u32[]{:S(2)}) collective-permute-start(bf16[384,384]{1,0:T(8,128)(2,1)S(1)} %get-tuple-element.60), channel_id=1, source_target_pairs={{0,8},{4,12},{8,0},{12,4},{16,24},{20,28},{24,16},{28,20},{1,9},{5... | collective-permute-start | bytes 884744 | tf_op jit(solution)/shard_map/ppermute | solution.py:528
  30.4 1.8 %collective-permute-start.8 = (bf16[384,384]{1,0:T(8,128)(2,1)S(1)}, bf16[384,384]{1,0:T(8,128)(2,1)S(1)}, u32[]{:S(2)}, u32[]{:S(2)}) collective-permute-start(bf16[384,384]{1,0:T(8,128)(2,1)S(1)} %get-tuple-element.61), channel_id=1, source_target_pairs={{0,4},{4,0},{8,12},{12,8},{16,20},{20,16},{24,28},{28,24},{1,5},{5... | collective-permute-start | bytes 884744 | tf_op jit(solution)/shard_map/ppermute | solution.py:516
  32.2 0.0 collective-permute-done.5.cross
  32.2 0.4 shard_map.117
  32.6 1.3 %collective-permute-start.10 = (bf16[384,384]{1,0:T(8,128)(2,1)S(1)}, bf16[384,384]{1,0:T(8,128)(2,1)S(1)}, u32[]{:S(2)}, u32[]{:S(2)}) collective-permute-start(bf16[384,384]{1,0:T(8,128)(2,1)S(1)} %get-tuple-element.67), channel_id=1, source_target_pairs={{16,0},{20,4},{8,24},{12,28},{17,1},{21,5},{9,25},{13,29},{18,2},{... | collective-permute-start | bytes 884744 | tf_op jit(solution)/shard_map/ppermute | solution.py:537
  33.9 1.3 %collective-permute-start.11 = (bf16[384,384]{1,0:T(8,128)(2,1)S(1)}, bf16[384,384]{1,0:T(8,128)(2,1)S(1)}, u32[]{:S(2)}, u32[]{:S(2)}) collective-permute-start(bf16[384,384]{1,0:T(8,128)(2,1)S(1)} %get-tuple-element.68), channel_id=1, source_target_pairs={{8,4},{12,0},{16,28},{20,24},{9,5},{13,1},{17,29},{21,25},{10,6},{... | collective-permute-start | bytes 884744 | tf_op jit(solution)/shard_map/ppermute | solution.py:538
  35.2 0.4 collective-permute-start.12
  35.5 5.6 %collective-permute-done.7.near = bf16[384,384]{1,0:T(8,128)(2,1)S(1)} collective-permute-done((bf16[384,384]{1,0:T(8,128)(2,1)S(1)}, bf16[384,384]{1,0:T(8,128)(2,1)S(1)}, u32[]{:S(2)}, u32[]{:S(2)}) %collective-permute-start.7) | collective-permute-done | bytes 294944 | tf_op jit(solution)/shard_map/ppermute | solution.py:528
  41.1 0.7 %collective-permute-start.9 = (bf16[384,384]{1,0:T(8,128)(2,1)S(1)}, bf16[384,384]{1,0:T(8,128)(2,1)S(1)}, u32[]{:S(2)}, u32[]{:S(2)}) collective-permute-start(bf16[384,384]{1,0:T(8,128)(2,1)S(1)} %get-tuple-element.66), channel_id=1, source_target_pairs={{8,16},{12,20},{16,8},{20,12},{9,17},{13,21},{17,9},{21,13},{10,18... | collective-permute-start | bytes 884744 | tf_op jit(solution)/shard_map/ppermute | solution.py:539
  41.8 1.6 %collective-permute-start.6 = (f32[1,192]{1,0:T(1,128)S(1)}, f32[1,192]{1,0:T(1,128)S(1)}, u32[]{:S(2)}, u32[]{:S(2)}) collective-permute-start(f32[1,192]{1,0:T(1,128)S(1)} %get-tuple-element.56.dots), channel_id=1, source_target_pairs={{0,2},{1,3},{2,0},{3,1},{4,6},{5,7},{6,4},{7,5},{8,10},{9,11},{10,... | collective-permute-start | bytes 2312 | tf_op jit(solution)/shard_map/ppermute | solution.py:536
  43.3 0.3 shard_map.118
  43.6 1.8 %collective-permute-done.6.dots_far = f32[1,192]{1,0:T(1,128)S(1)} collective-permute-done((f32[1,192]{1,0:T(1,128)S(1)}, f32[1,192]{1,0:T(1,128)S(1)}, u32[]{:S(2)}, u32[]{:S(2)}) %collective-permute-start.6) | collective-permute-done | bytes 800 | tf_op jit(solution)/shard_map/ppermute | solution.py:536
  45.4 4.8 %collective-permute-done.11.cross = bf16[384,384]{1,0:T(8,128)(2,1)S(1)} collective-permute-done((bf16[384,384]{1,0:T(8,128)(2,1)S(1)}, bf16[384,384]{1,0:T(8,128)(2,1)S(1)}, u32[]{:S(2)}, u32[]{:S(2)}) %collective-permute-start.11) | collective-permute-done | bytes 294944 | tf_op jit(solution)/shard_map/ppermute | solution.py:538
  50.2 0.2 collective-permute-done.12.late
  50.4 1.2 %shard_map.119 = (bf16[192,768]{1,0:T(8,128)(2,1)}, bf16[192,768]{1,0:T(8,128)(2,1)}, bf16[192,768]{1,0:T(8,128)(2,1)}, f32[1,192]{1,0:T(1,128)}) custom-call(s32[12,128]{1,0:T(8,128)S(1)} %bitcast.10, f32[1,192]{1,0:T(1,128)S(1)} %bitcast.12, f32[1,192]{1,0:T(1,128)S(1)} %get-tuple-element.56.dots, f32[1,192]{1,0:T(1,128)S(1)} %collective-permute-done.6.dots_far, ...), custom_call_target="tpu_custom_call" | custom-call | flops 1024 | bytes 1024 | tf_op jit(solution)/shard_map/pallas_call | solution.py:662
  (17 shorter events, 0.1 us)
Async XLA Ops:
  0.6 13.8 %copy-start.4 = (s32[1536]{0:T(1024)S(1)}, s32[1536]{0:T(1024)}, u32[]{:S(2)}) copy-start(s32[1536]{0:T(1024)} %param.15) | copy-start | bytes 18436
  4.4 15.1 %copy-start.6 = (f32[1,192]{1,0:T(1,128)S(1)}, f32[1,192]{1,0:T(1,128)}, u32[]{:S(2)}) copy-start(f32[1,192]{1,0:T(1,128)} %get-tuple-element.46.dots) | copy-start | bytes 2308
  4.4 17.1 %collective-permute-start = (bf16[800,384]{1,0:T(8,128)(2,1)}, bf16[800,384]{1,0:T(8,128)(2,1)S(1)}, u32[]{:S(2)}, u32[]{:S(2)}) collective-permute-start(bf16[800,384]{1,0:T(8,128)(2,1)} %get-tuple-element.40.own), channel_id=1, source_target_pairs={{0,4},{4,0},{8,12},{12,8},{16,20},{20,16},{24,28},{28,24},{1,5},{5... | collective-permute-start | bytes 1843208 | tf_op jit(solution)/shard_map/ppermute | solution.py:497
  7.5 11.3 %collective-permute-start.1 = (bf16[400,384]{1,0:T(8,128)(2,1)}, bf16[400,384]{1,0:T(8,128)(2,1)S(1)}, u32[]{:S(2)}, u32[]{:S(2)}) collective-permute-start(bf16[400,384]{1,0:T(8,128)(2,1)} %get-tuple-element.43), channel_id=1, source_target_pairs={{0,8},{4,12},{8,0},{12,4},{16,24},{20,28},{24,16},{28,20},{1,9},{5... | collective-permute-start | bytes 921608 | tf_op jit(solution)/shard_map/ppermute | solution.py:496
  9.2 13.2 %collective-permute-start.2 = (bf16[400,384]{1,0:T(8,128)(2,1)}, bf16[400,384]{1,0:T(8,128)(2,1)S(1)}, u32[]{:S(2)}, u32[]{:S(2)}) collective-permute-start(bf16[400,384]{1,0:T(8,128)(2,1)} %get-tuple-element.44), channel_id=1, source_target_pairs={{0,16},{4,20},{24,8},{28,12},{1,17},{5,21},{25,9},{29,13},{2,18},{... | collective-permute-start | bytes 921608 | tf_op jit(solution)/shard_map/ppermute | solution.py:498
  13.8 10.3 %collective-permute-start.4 = (bf16[400,384]{1,0:T(8,128)(2,1)}, bf16[400,384]{1,0:T(8,128)(2,1)S(1)}, u32[]{:S(2)}, u32[]{:S(2)}) collective-permute-start(bf16[400,384]{1,0:T(8,128)(2,1)} %get-tuple-element.44), channel_id=1, source_target_pairs={{8,16},{12,20},{16,8},{20,12},{9,17},{13,21},{17,9},{21,13},{10,18... | collective-permute-start | bytes 921608 | tf_op jit(solution)/shard_map/ppermute | solution.py:499
  14.5 1.1 %copy-start = (bf16[800,384]{1,0:T(8,128)(2,1)S(1)}, bf16[800,384]{1,0:T(8,128)(2,1)}, u32[]{:S(2)}) copy-start(bf16[800,384]{1,0:T(8,128)(2,1)} %get-tuple-element.39.mine) | copy-start | bytes 1843204
  15.5 1.1 %copy-start.2 = (bf16[800,384]{1,0:T(8,128)(2,1)S(1)}, bf16[800,384]{1,0:T(8,128)(2,1)}, u32[]{:S(2)}) copy-start(bf16[800,384]{1,0:T(8,128)(2,1)} %get-tuple-element.40.own) | copy-start | bytes 1843204
  16.6 4.9 %copy-start.1 = (bf16[800,384]{1,0:T(8,128)(2,1)S(1)}, bf16[800,384]{1,0:T(8,128)(2,1)}, u32[]{:S(2)}) copy-start(bf16[800,384]{1,0:T(8,128)(2,1)} %get-tuple-element.39.mine) | copy-start | bytes 1843204
  18.7 3.7 %copy-start.3 = (bf16[800,384]{1,0:T(8,128)(2,1)S(1)}, bf16[800,384]{1,0:T(8,128)(2,1)}, u32[]{:S(2)}) copy-start(bf16[800,384]{1,0:T(8,128)(2,1)} %get-tuple-element.40.own) | copy-start | bytes 1843204
  18.8 13.4 %collective-permute-start.5 = (bf16[400,384]{1,0:T(8,128)(2,1)S(1)}, bf16[400,384]{1,0:T(8,128)(2,1)S(1)}, u32[]{:S(2)}, u32[]{:S(2)}) collective-permute-start(bf16[400,384]{1,0:T(8,128)(2,1)S(1)} %shard_map.114.near), channel_id=1, source_target_pairs={{8,12},{12,8},{16,20},{20,16},{9,13},{13,9},{17,21},{21,17},{10,14... | collective-permute-start | bytes 921608 | tf_op jit(solution)/shard_map/ppermute | solution.py:509
  19.6 4.5 %collective-permute-start.3 = (f32[1,192]{1,0:T(1,128)S(1)}, f32[1,192]{1,0:T(1,128)S(1)}, u32[]{:S(2)}, u32[]{:S(2)}) collective-permute-start(f32[1,192]{1,0:T(1,128)S(1)} %copy-done.6), channel_id=1, source_target_pairs={{0,1},{1,0},{2,3},{3,2},{4,5},{5,4},{6,7},{7,6},{8,9},{9,8},{10,11... | collective-permute-start | bytes 2312 | tf_op jit(solution)/shard_map/ppermute | solution.py:522
  24.2 16.9 %collective-permute-start.7 = (bf16[384,384]{1,0:T(8,128)(2,1)S(1)}, bf16[384,384]{1,0:T(8,128)(2,1)S(1)}, u32[]{:S(2)}, u32[]{:S(2)}) collective-permute-start(bf16[384,384]{1,0:T(8,128)(2,1)S(1)} %get-tuple-element.60), channel_id=1, source_target_pairs={{0,8},{4,12},{8,0},{12,4},{16,24},{20,28},{24,16},{28,20},{1,9},{5... | collective-permute-start | bytes 884744 | tf_op jit(solution)/shard_map/ppermute | solution.py:528
  30.4 11.4 %collective-permute-start.8 = (bf16[384,384]{1,0:T(8,128)(2,1)S(1)}, bf16[384,384]{1,0:T(8,128)(2,1)S(1)}, u32[]{:S(2)}, u32[]{:S(2)}) collective-permute-start(bf16[384,384]{1,0:T(8,128)(2,1)S(1)} %get-tuple-element.61), channel_id=1, source_target_pairs={{0,4},{4,0},{8,12},{12,8},{16,20},{20,16},{24,28},{28,24},{1,5},{5... | collective-permute-start | bytes 884744 | tf_op jit(solution)/shard_map/ppermute | solution.py:516
  32.6 12.8 %collective-permute-start.10 = (bf16[384,384]{1,0:T(8,128)(2,1)S(1)}, bf16[384,384]{1,0:T(8,128)(2,1)S(1)}, u32[]{:S(2)}, u32[]{:S(2)}) collective-permute-start(bf16[384,384]{1,0:T(8,128)(2,1)S(1)} %get-tuple-element.67), channel_id=1, source_target_pairs={{16,0},{20,4},{8,24},{12,28},{17,1},{21,5},{9,25},{13,29},{18,2},{... | collective-permute-start | bytes 884744 | tf_op jit(solution)/shard_map/ppermute | solution.py:537
  33.9 16.3 %collective-permute-start.11 = (bf16[384,384]{1,0:T(8,128)(2,1)S(1)}, bf16[384,384]{1,0:T(8,128)(2,1)S(1)}, u32[]{:S(2)}, u32[]{:S(2)}) collective-permute-start(bf16[384,384]{1,0:T(8,128)(2,1)S(1)} %get-tuple-element.68), channel_id=1, source_target_pairs={{8,4},{12,0},{16,28},{20,24},{9,5},{13,1},{17,29},{21,25},{10,6},{... | collective-permute-start | bytes 884744 | tf_op jit(solution)/shard_map/ppermute | solution.py:538
  35.2 15.2 %collective-permute-start.12 = (bf16[384,384]{1,0:T(8,128)(2,1)S(1)}, bf16[384,384]{1,0:T(8,128)(2,1)S(1)}, u32[]{:S(2)}, u32[]{:S(2)}) collective-permute-start(bf16[384,384]{1,0:T(8,128)(2,1)S(1)} %get-tuple-element.69), channel_id=1, source_target_pairs={{0,4},{4,0},{8,12},{12,8},{16,20},{20,16},{24,28},{28,24},{1,5},{5... | collective-permute-start | bytes 884744 | tf_op jit(solution)/shard_map/ppermute | solution.py:540
  41.1 9.3 %collective-permute-start.9 = (bf16[384,384]{1,0:T(8,128)(2,1)S(1)}, bf16[384,384]{1,0:T(8,128)(2,1)S(1)}, u32[]{:S(2)}, u32[]{:S(2)}) collective-permute-start(bf16[384,384]{1,0:T(8,128)(2,1)S(1)} %get-tuple-element.66), channel_id=1, source_target_pairs={{8,16},{12,20},{16,8},{20,12},{9,17},{13,21},{17,9},{21,13},{10,18... | collective-permute-start | bytes 884744 | tf_op jit(solution)/shard_map/ppermute | solution.py:539
  41.8 3.6 %collective-permute-start.6 = (f32[1,192]{1,0:T(1,128)S(1)}, f32[1,192]{1,0:T(1,128)S(1)}, u32[]{:S(2)}, u32[]{:S(2)}) collective-permute-start(f32[1,192]{1,0:T(1,128)S(1)} %get-tuple-element.56.dots), channel_id=1, source_target_pairs={{0,2},{1,3},{2,0},{3,1},{4,6},{5,7},{6,4},{7,5},{8,10},{9,11},{10,... | collective-permute-start | bytes 2312 | tf_op jit(solution)/shard_map/ppermute | solution.py:536
  43.3 7.1 %copy-start.5 = (f32[192]{0:T(256)S(1)}, f32[192]{0:T(256)}, u32[]{:S(2)}) copy-start(f32[192]{0:T(256)} %param.14) | copy-start | bytes 2308

commit v6 on v5

--- a/solution.py
+++ b/solution.py
@@ -102,30 +102,6 @@
             )
     for copy in copies:
         copy.start()
-    for copy in copies[5:]:
-        copy.wait()
-    for at in range(2):
-        bank[pl.ds(at * rows + 2 * slots, TILE), :] = jnp.zeros((TILE, half), BF16)
-    level = lax.axis_index("seq") // 2
-    moves = []
-    for out, blocks in zip(outs, plan):
-        for place, block in enumerate(blocks(level)):
-            block = jnp.int32(block)
-            move = pltpu.make_async_copy(
-                bank.at[pl.ds(pl.multiple_of(block * rows, TILE), rows), :],
-                out.at[pl.ds(place * rows, rows), :],
-                done.at[len(moves)],
-            )
-            moves.append((block, move))
-
-    def each(some, early):
-        for block, move in some:
-
-            @pl.when((block < 2) == early)
-            def _():
-                move.start()
-
-    each(moves, True)
     for copy in copies[:5]:
         copy.wait()
     head_dim = width // heads
@@ -149,6 +125,30 @@
         dout_parts.append(dout)
         delta_parts.append(dout.astype(F32) * out)
         dot_parts.append(wide * out)
+    for copy in copies[5:]:
+        copy.wait()
+    for at in range(2):
+        bank[pl.ds(at * rows + 2 * slots, TILE), :] = jnp.zeros((TILE, half), BF16)
+    level = lax.axis_index("seq") // 2
+    moves = []
+    for out, blocks in zip(outs, plan):
+        for place, block in enumerate(blocks(level)):
+            block = jnp.int32(block)
+            move = pltpu.make_async_copy(
+                bank.at[pl.ds(pl.multiple_of(block * rows, TILE), rows), :],
+                out.at[pl.ds(place * rows, rows), :],
+                done.at[len(moves)],
+            )
+            moves.append((block, move))
+
+    def each(some, early):
+        for block, move in some:
+
+            @pl.when((block < 2) == early)
+            def _():
+                move.start()
+
+    each(moves, True)
     delta_high, delta_low = split_exact(jnp.concatenate(delta_parts, axis=1))
     delta = dot(pick, delta_high, NT) + dot(pick, delta_low, NT)
     dot_high, dot_low = split_exact(jnp.concatenate(dot_parts, axis=1))

time: 51.9 us -> 51.8 us (level)
  no operation moved by 1% of the time
where the time goes in v6:
time: 51.8 us; the launch traced here: 51.5 us
  starting transfers between devices  23.9 us (46%)
  waiting for transfers between devices  15.1 us (29%)
  Pallas kernels  9.53 us (18%)
  local copies, waits for them, and re-layouts  2.16 us (4%)
  between operations  0.84 us (2%)
    pallas_call x9, Pallas kernels, call(): pl.pallas_call(kernel, out_shape=out_shape, in_specs=[pl.BlockSpec(memory...  9.53 us
    ppermute x1, starting transfers between devices, four_levels(): lax.ppermute(near_low, 'seq', pairs([(0, 1), (1, 0), (2, 3), (3, 2)]))  6.21 us
    ppermute x1, waiting for transfers between devices, four_levels(): lax.ppermute(near_low, 'seq', pairs([(0, 1), (1, 0), (2, 3), (3, 2)]))  5.57 us
    ppermute x1, waiting for transfers between devices, four_levels(): cross = lax.ppermute(cross_low, 'seq', pairs([(1, 0), (2, 3)], 1))  4.79 us
    ppermute x1, starting transfers between devices, four_levels(): skip = lax.ppermute(far_send, 'seq', pairs([(0, 2), (3, 1)]))  4.54 us
    ppermute x1, starting transfers between devices, four_levels(): other = lax.ppermute(own, 'seq', pairs([(i, i) for i in range(4)], 1))  3.03 us
    unnamed x14, local copies, waits for them, and re-layouts  2.16 us
    ppermute x1, waiting for transfers between devices, four_levels(): other = lax.ppermute(own, 'seq', pairs([(i, i) for i in range(4)], 1))  2.04 us
  transfers between devices with their start and end apart: 13, of which 6 were waited for; matrix products, arithmetic and copies ran while one was open for 0% of the time, Pallas kernels for 9%

profile of v6, /device:TPU:0, one launch (start us, length us, event | category | flops | bytes accessed | tf_op | source)
XLA Modules:
  0.0 51.5 jit_solution(12265710092519269704)
XLA Ops:
  0.6 3.8 %shard_map.111 = (f32[1,192]{1,0:T(1,128)}, bf16[800,384]{1,0:T(8,128)(2,1)}, bf16[800,384]{1,0:T(8,128)(2,1)}, bf16[400,384]{1,0:T(8,128)(2,1)}, bf16[400,384]{1,0:T(8,128)(2,1)}) custom-call(bf16[192,768]{1,0:T(8,128)(2,1)} %refs_0_.1, bf16[192,768]{1,0:T(8,128)(2,1)} %refs_1_.1, f32[1,192]{1,0:T(1,128)} %bitcast.11, f32[6,192]{1,0:T(8,128)} %bitcast.13, ...), custom_call_target="tpu_custom_call" | custom-call | flops 1024 | bytes 1024 | tf_op jit(solution)/shard_map/pallas_call | solution.py:662
  4.4 0.0 copy-start.6
  4.5 3.0 %collective-permute-start = (bf16[800,384]{1,0:T(8,128)(2,1)}, bf16[800,384]{1,0:T(8,128)(2,1)S(1)}, u32[]{:S(2)}, u32[]{:S(2)}) collective-permute-start(bf16[800,384]{1,0:T(8,128)(2,1)} %get-tuple-element.40.own), channel_id=1, source_target_pairs={{0,4},{4,0},{8,12},{12,8},{16,20},{20,16},{24,28},{28,24},{1,5},{5... | collective-permute-start | bytes 1843208 | tf_op jit(solution)/shard_map/ppermute | solution.py:497
  7.5 1.6 %collective-permute-start.1 = (bf16[400,384]{1,0:T(8,128)(2,1)}, bf16[400,384]{1,0:T(8,128)(2,1)S(1)}, u32[]{:S(2)}, u32[]{:S(2)}) collective-permute-start(bf16[400,384]{1,0:T(8,128)(2,1)} %get-tuple-element.43), channel_id=1, source_target_pairs={{0,8},{4,12},{8,0},{12,4},{16,24},{20,28},{24,16},{28,20},{1,9},{5... | collective-permute-start | bytes 921608 | tf_op jit(solution)/shard_map/ppermute | solution.py:496
  9.1 4.5 %collective-permute-start.2 = (bf16[400,384]{1,0:T(8,128)(2,1)}, bf16[400,384]{1,0:T(8,128)(2,1)S(1)}, u32[]{:S(2)}, u32[]{:S(2)}) collective-permute-start(bf16[400,384]{1,0:T(8,128)(2,1)} %get-tuple-element.44), channel_id=1, source_target_pairs={{0,16},{4,20},{24,8},{28,12},{1,17},{5,21},{25,9},{29,13},{2,18},{... | collective-permute-start | bytes 921608 | tf_op jit(solution)/shard_map/ppermute | solution.py:498
  13.6 0.7 %collective-permute-start.4 = (bf16[400,384]{1,0:T(8,128)(2,1)}, bf16[400,384]{1,0:T(8,128)(2,1)S(1)}, u32[]{:S(2)}, u32[]{:S(2)}) collective-permute-start(bf16[400,384]{1,0:T(8,128)(2,1)} %get-tuple-element.44), channel_id=1, source_target_pairs={{8,16},{12,20},{16,8},{20,12},{9,17},{13,21},{17,9},{21,13},{10,18... | collective-permute-start | bytes 921608 | tf_op jit(solution)/shard_map/ppermute | solution.py:499
  14.3 1.1 %copy-done = bf16[800,384]{1,0:T(8,128)(2,1)S(1)} copy-done((bf16[800,384]{1,0:T(8,128)(2,1)S(1)}, bf16[800,384]{1,0:T(8,128)(2,1)}, u32[]{:S(2)}) %copy-start) | copy-done | bytes 614424
  15.4 1.1 %copy-done.2 = bf16[800,384]{1,0:T(8,128)(2,1)S(1)} copy-done((bf16[800,384]{1,0:T(8,128)(2,1)S(1)}, bf16[800,384]{1,0:T(8,128)(2,1)}, u32[]{:S(2)}) %copy-start.2) | copy-done | bytes 614424
  16.5 2.1 %shard_map.112 = (f32[1,192]{1,0:T(1,128)S(1)}, f32[768,384]{1,0:T(8,128)S(1)}, f32[768,384]{1,0:T(8,128)S(1)}) custom-call(s32[12,128]{1,0:T(8,128)S(1)} %bitcast.5, bf16[800,384]{1,0:T(8,128)(2,1)S(1)} %copy-done, bf16[800,384]{1,0:T(8,128)(2,1)S(1)} %copy-done.2), custom_call_target="tpu_custom_call" | custom-call | flops 1024 | bytes 1024 | tf_op jit(solution)/shard_map/pallas_call | solution.py:662
  18.6 0.0 collective-permute-done.1.block
  18.6 0.8 %collective-permute-start.5 = (bf16[400,384]{1,0:T(8,128)(2,1)S(1)}, bf16[400,384]{1,0:T(8,128)(2,1)S(1)}, u32[]{:S(2)}, u32[]{:S(2)}) collective-permute-start(bf16[400,384]{1,0:T(8,128)(2,1)S(1)} %shard_map.114.near), channel_id=1, source_target_pairs={{8,12},{12,8},{16,20},{20,16},{9,13},{13,9},{17,21},{21,17},{10,14... | collective-permute-start | bytes 921608 | tf_op jit(solution)/shard_map/ppermute | solution.py:509
  19.4 0.1 collective-permute-start.3
  19.5 2.0 %collective-permute-done.other = bf16[800,384]{1,0:T(8,128)(2,1)S(1)} collective-permute-done((bf16[800,384]{1,0:T(8,128)(2,1)}, bf16[800,384]{1,0:T(8,128)(2,1)S(1)}, u32[]{:S(2)}, u32[]{:S(2)}) %collective-permute-start) | collective-permute-done | bytes 614432 | tf_op jit(solution)/shard_map/ppermute | solution.py:497
  21.6 0.7 %collective-permute-done.2.skip = bf16[400,384]{1,0:T(8,128)(2,1)S(1)} collective-permute-done((bf16[400,384]{1,0:T(8,128)(2,1)}, bf16[400,384]{1,0:T(8,128)(2,1)S(1)}, u32[]{:S(2)}, u32[]{:S(2)}) %collective-permute-start.2) | collective-permute-done | bytes 307232 | tf_op jit(solution)/shard_map/ppermute | solution.py:498
  22.3 1.7 %shard_map.115 = (f32[1,192]{1,0:T(1,128)S(1)}, f32[384,384]{1,0:T(8,128)S(1)}, f32[384,384]{1,0:T(8,128)S(1)}, bf16[384,384]{1,0:T(8,128)(2,1)S(1)}, f32[384,38...) custom-call(s32[12,128]{1,0:T(8,128)S(1)} %bitcast.7, f32[1,192]{1,0:T(1,128)S(1)} %get-tuple-element.42.after, ...), custom_call_target="tpu_custom_call" | custom-call | flops 1024 | bytes 1024 | tf_op jit(solution)/shard_map/pallas_call | solution.py:662
  24.0 0.1 shard_map.116
  24.0 6.2 %collective-permute-start.7 = (bf16[384,384]{1,0:T(8,128)(2,1)S(1)}, bf16[384,384]{1,0:T(8,128)(2,1)S(1)}, u32[]{:S(2)}, u32[]{:S(2)}) collective-permute-start(bf16[384,384]{1,0:T(8,128)(2,1)S(1)} %get-tuple-element.60), channel_id=1, source_target_pairs={{0,8},{4,12},{8,0},{12,4},{16,24},{20,28},{24,16},{28,20},{1,9},{5... | collective-permute-start | bytes 884744 | tf_op jit(solution)/shard_map/ppermute | solution.py:528
  30.2 1.8 %collective-permute-start.8 = (bf16[384,384]{1,0:T(8,128)(2,1)S(1)}, bf16[384,384]{1,0:T(8,128)(2,1)S(1)}, u32[]{:S(2)}, u32[]{:S(2)}) collective-permute-start(bf16[384,384]{1,0:T(8,128)(2,1)S(1)} %get-tuple-element.61), channel_id=1, source_target_pairs={{0,4},{4,0},{8,12},{12,8},{16,20},{20,16},{24,28},{28,24},{1,5},{5... | collective-permute-start | bytes 884744 | tf_op jit(solution)/shard_map/ppermute | solution.py:516
  32.1 0.4 shard_map.117
  32.5 1.3 %collective-permute-start.10 = (bf16[384,384]{1,0:T(8,128)(2,1)S(1)}, bf16[384,384]{1,0:T(8,128)(2,1)S(1)}, u32[]{:S(2)}, u32[]{:S(2)}) collective-permute-start(bf16[384,384]{1,0:T(8,128)(2,1)S(1)} %get-tuple-element.67), channel_id=1, source_target_pairs={{16,0},{20,4},{8,24},{12,28},{17,1},{21,5},{9,25},{13,29},{18,2},{... | collective-permute-start | bytes 884744 | tf_op jit(solution)/shard_map/ppermute | solution.py:537
  33.8 1.3 %collective-permute-start.11 = (bf16[384,384]{1,0:T(8,128)(2,1)S(1)}, bf16[384,384]{1,0:T(8,128)(2,1)S(1)}, u32[]{:S(2)}, u32[]{:S(2)}) collective-permute-start(bf16[384,384]{1,0:T(8,128)(2,1)S(1)} %get-tuple-element.68), channel_id=1, source_target_pairs={{8,4},{12,0},{16,28},{20,24},{9,5},{13,1},{17,29},{21,25},{10,6},{... | collective-permute-start | bytes 884744 | tf_op jit(solution)/shard_map/ppermute | solution.py:538
  35.0 0.3 collective-permute-start.12
  35.4 5.6 %collective-permute-done.7.near = bf16[384,384]{1,0:T(8,128)(2,1)S(1)} collective-permute-done((bf16[384,384]{1,0:T(8,128)(2,1)S(1)}, bf16[384,384]{1,0:T(8,128)(2,1)S(1)}, u32[]{:S(2)}, u32[]{:S(2)}) %collective-permute-start.7) | collective-permute-done | bytes 294944 | tf_op jit(solution)/shard_map/ppermute | solution.py:528
  40.9 0.7 %collective-permute-start.9 = (bf16[384,384]{1,0:T(8,128)(2,1)S(1)}, bf16[384,384]{1,0:T(8,128)(2,1)S(1)}, u32[]{:S(2)}, u32[]{:S(2)}) collective-permute-start(bf16[384,384]{1,0:T(8,128)(2,1)S(1)} %get-tuple-element.66), channel_id=1, source_target_pairs={{8,16},{12,20},{16,8},{20,12},{9,17},{13,21},{17,9},{21,13},{10,18... | collective-permute-start | bytes 884744 | tf_op jit(solution)/shard_map/ppermute | solution.py:539
  41.6 0.0 collective-permute-done.8.early
  41.6 1.6 %collective-permute-start.6 = (f32[1,192]{1,0:T(1,128)S(1)}, f32[1,192]{1,0:T(1,128)S(1)}, u32[]{:S(2)}, u32[]{:S(2)}) collective-permute-start(f32[1,192]{1,0:T(1,128)S(1)} %get-tuple-element.56.dots), channel_id=1, source_target_pairs={{0,2},{1,3},{2,0},{3,1},{4,6},{5,7},{6,4},{7,5},{8,10},{9,11},{10,... | collective-permute-start | bytes 2312 | tf_op jit(solution)/shard_map/ppermute | solution.py:536
  43.2 0.3 shard_map.118
  43.5 1.8 %collective-permute-done.6.dots_far = f32[1,192]{1,0:T(1,128)S(1)} collective-permute-done((f32[1,192]{1,0:T(1,128)S(1)}, f32[1,192]{1,0:T(1,128)S(1)}, u32[]{:S(2)}, u32[]{:S(2)}) %collective-permute-start.6) | collective-permute-done | bytes 800 | tf_op jit(solution)/shard_map/ppermute | solution.py:536
  45.3 0.0 collective-permute-done.10.skip
  45.3 4.8 %collective-permute-done.11.cross = bf16[384,384]{1,0:T(8,128)(2,1)S(1)} collective-permute-done((bf16[384,384]{1,0:T(8,128)(2,1)S(1)}, bf16[384,384]{1,0:T(8,128)(2,1)S(1)}, u32[]{:S(2)}, u32[]{:S(2)}) %collective-permute-start.11) | collective-permute-done | bytes 294944 | tf_op jit(solution)/shard_map/ppermute | solution.py:538
  50.0 0.2 collective-permute-done.12.late
  50.2 1.2 %shard_map.119 = (bf16[192,768]{1,0:T(8,128)(2,1)}, bf16[192,768]{1,0:T(8,128)(2,1)}, bf16[192,768]{1,0:T(8,128)(2,1)}, f32[1,192]{1,0:T(1,128)}) custom-call(s32[12,128]{1,0:T(8,128)S(1)} %bitcast.10, f32[1,192]{1,0:T(1,128)S(1)} %bitcast.12, f32[1,192]{1,0:T(1,128)S(1)} %get-tuple-element.56.dots, f32[1,192]{1,0:T(1,128)S(1)} %collective-permute-done.6.dots_far, ...), custom_call_target="tpu_custom_call" | custom-call | flops 1024 | bytes 1024 | tf_op jit(solution)/shard_map/pallas_call | solution.py:662
  (17 shorter events, 0.1 us)
Async XLA Ops:
  0.6 13.7 %copy-start.4 = (s32[1536]{0:T(1024)S(1)}, s32[1536]{0:T(1024)}, u32[]{:S(2)}) copy-start(s32[1536]{0:T(1024)} %param.15) | copy-start | bytes 18436
  4.4 15.0 %copy-start.6 = (f32[1,192]{1,0:T(1,128)S(1)}, f32[1,192]{1,0:T(1,128)}, u32[]{:S(2)}) copy-start(f32[1,192]{1,0:T(1,128)} %get-tuple-element.46.dots) | copy-start | bytes 2308
  4.5 17.1 %collective-permute-start = (bf16[800,384]{1,0:T(8,128)(2,1)}, bf16[800,384]{1,0:T(8,128)(2,1)S(1)}, u32[]{:S(2)}, u32[]{:S(2)}) collective-permute-start(bf16[800,384]{1,0:T(8,128)(2,1)} %get-tuple-element.40.own), channel_id=1, source_target_pairs={{0,4},{4,0},{8,12},{12,8},{16,20},{20,16},{24,28},{28,24},{1,5},{5... | collective-permute-start | bytes 1843208 | tf_op jit(solution)/shard_map/ppermute | solution.py:497
  7.5 11.1 %collective-permute-start.1 = (bf16[400,384]{1,0:T(8,128)(2,1)}, bf16[400,384]{1,0:T(8,128)(2,1)S(1)}, u32[]{:S(2)}, u32[]{:S(2)}) collective-permute-start(bf16[400,384]{1,0:T(8,128)(2,1)} %get-tuple-element.43), channel_id=1, source_target_pairs={{0,8},{4,12},{8,0},{12,4},{16,24},{20,28},{24,16},{28,20},{1,9},{5... | collective-permute-start | bytes 921608 | tf_op jit(solution)/shard_map/ppermute | solution.py:496
  9.1 13.2 %collective-permute-start.2 = (bf16[400,384]{1,0:T(8,128)(2,1)}, bf16[400,384]{1,0:T(8,128)(2,1)S(1)}, u32[]{:S(2)}, u32[]{:S(2)}) collective-permute-start(bf16[400,384]{1,0:T(8,128)(2,1)} %get-tuple-element.44), channel_id=1, source_target_pairs={{0,16},{4,20},{24,8},{28,12},{1,17},{5,21},{25,9},{29,13},{2,18},{... | collective-permute-start | bytes 921608 | tf_op jit(solution)/shard_map/ppermute | solution.py:498
  13.6 10.3 %collective-permute-start.4 = (bf16[400,384]{1,0:T(8,128)(2,1)}, bf16[400,384]{1,0:T(8,128)(2,1)S(1)}, u32[]{:S(2)}, u32[]{:S(2)}) collective-permute-start(bf16[400,384]{1,0:T(8,128)(2,1)} %get-tuple-element.44), channel_id=1, source_target_pairs={{8,16},{12,20},{16,8},{20,12},{9,17},{13,21},{17,9},{21,13},{10,18... | collective-permute-start | bytes 921608 | tf_op jit(solution)/shard_map/ppermute | solution.py:499
  14.3 1.1 %copy-start = (bf16[800,384]{1,0:T(8,128)(2,1)S(1)}, bf16[800,384]{1,0:T(8,128)(2,1)}, u32[]{:S(2)}) copy-start(bf16[800,384]{1,0:T(8,128)(2,1)} %get-tuple-element.39.mine) | copy-start | bytes 1843204
  15.4 1.1 %copy-start.2 = (bf16[800,384]{1,0:T(8,128)(2,1)S(1)}, bf16[800,384]{1,0:T(8,128)(2,1)}, u32[]{:S(2)}) copy-start(bf16[800,384]{1,0:T(8,128)(2,1)} %get-tuple-element.40.own) | copy-start | bytes 1843204
  16.5 5.1 %copy-start.1 = (bf16[800,384]{1,0:T(8,128)(2,1)S(1)}, bf16[800,384]{1,0:T(8,128)(2,1)}, u32[]{:S(2)}) copy-start(bf16[800,384]{1,0:T(8,128)(2,1)} %get-tuple-element.39.mine) | copy-start | bytes 1843204
  18.6 3.7 %copy-start.3 = (bf16[800,384]{1,0:T(8,128)(2,1)S(1)}, bf16[800,384]{1,0:T(8,128)(2,1)}, u32[]{:S(2)}) copy-start(bf16[800,384]{1,0:T(8,128)(2,1)} %get-tuple-element.40.own) | copy-start | bytes 1843204
  18.6 13.5 %collective-permute-start.5 = (bf16[400,384]{1,0:T(8,128)(2,1)S(1)}, bf16[400,384]{1,0:T(8,128)(2,1)S(1)}, u32[]{:S(2)}, u32[]{:S(2)}) collective-permute-start(bf16[400,384]{1,0:T(8,128)(2,1)S(1)} %shard_map.114.near), channel_id=1, source_target_pairs={{8,12},{12,8},{16,20},{20,16},{9,13},{13,9},{17,21},{21,17},{10,14... | collective-permute-start | bytes 921608 | tf_op jit(solution)/shard_map/ppermute | solution.py:509
  19.4 4.5 %collective-permute-start.3 = (f32[1,192]{1,0:T(1,128)S(1)}, f32[1,192]{1,0:T(1,128)S(1)}, u32[]{:S(2)}, u32[]{:S(2)}) collective-permute-start(f32[1,192]{1,0:T(1,128)S(1)} %copy-done.6), channel_id=1, source_target_pairs={{0,1},{1,0},{2,3},{3,2},{4,5},{5,4},{6,7},{7,6},{8,9},{9,8},{10,11... | collective-permute-start | bytes 2312 | tf_op jit(solution)/shard_map/ppermute | solution.py:522
  24.0 16.9 %collective-permute-start.7 = (bf16[384,384]{1,0:T(8,128)(2,1)S(1)}, bf16[384,384]{1,0:T(8,128)(2,1)S(1)}, u32[]{:S(2)}, u32[]{:S(2)}) collective-permute-start(bf16[384,384]{1,0:T(8,128)(2,1)S(1)} %get-tuple-element.60), channel_id=1, source_target_pairs={{0,8},{4,12},{8,0},{12,4},{16,24},{20,28},{24,16},{28,20},{1,9},{5... | collective-permute-start | bytes 884744 | tf_op jit(solution)/shard_map/ppermute | solution.py:528
  30.2 11.4 %collective-permute-start.8 = (bf16[384,384]{1,0:T(8,128)(2,1)S(1)}, bf16[384,384]{1,0:T(8,128)(2,1)S(1)}, u32[]{:S(2)}, u32[]{:S(2)}) collective-permute-start(bf16[384,384]{1,0:T(8,128)(2,1)S(1)} %get-tuple-element.61), channel_id=1, source_target_pairs={{0,4},{4,0},{8,12},{12,8},{16,20},{20,16},{24,28},{28,24},{1,5},{5... | collective-permute-start | bytes 884744 | tf_op jit(solution)/shard_map/ppermute | solution.py:516
  32.5 12.8 %collective-permute-start.10 = (bf16[384,384]{1,0:T(8,128)(2,1)S(1)}, bf16[384,384]{1,0:T(8,128)(2,1)S(1)}, u32[]{:S(2)}, u32[]{:S(2)}) collective-permute-start(bf16[384,384]{1,0:T(8,128)(2,1)S(1)} %get-tuple-element.67), channel_id=1, source_target_pairs={{16,0},{20,4},{8,24},{12,28},{17,1},{21,5},{9,25},{13,29},{18,2},{... | collective-permute-start | bytes 884744 | tf_op jit(solution)/shard_map/ppermute | solution.py:537
  33.8 16.3 %collective-permute-start.11 = (bf16[384,384]{1,0:T(8,128)(2,1)S(1)}, bf16[384,384]{1,0:T(8,128)(2,1)S(1)}, u32[]{:S(2)}, u32[]{:S(2)}) collective-permute-start(bf16[384,384]{1,0:T(8,128)(2,1)S(1)} %get-tuple-element.68), channel_id=1, source_target_pairs={{8,4},{12,0},{16,28},{20,24},{9,5},{13,1},{17,29},{21,25},{10,6},{... | collective-permute-start | bytes 884744 | tf_op jit(solution)/shard_map/ppermute | solution.py:538
  35.0 15.2 %collective-permute-start.12 = (bf16[384,384]{1,0:T(8,128)(2,1)S(1)}, bf16[384,384]{1,0:T(8,128)(2,1)S(1)}, u32[]{:S(2)}, u32[]{:S(2)}) collective-permute-start(bf16[384,384]{1,0:T(8,128)(2,1)S(1)} %get-tuple-element.69), channel_id=1, source_target_pairs={{0,4},{4,0},{8,12},{12,8},{16,20},{20,16},{24,28},{28,24},{1,5},{5... | collective-permute-start | bytes 884744 | tf_op jit(solution)/shard_map/ppermute | solution.py:540
  40.9 9.3 %collective-permute-start.9 = (bf16[384,384]{1,0:T(8,128)(2,1)S(1)}, bf16[384,384]{1,0:T(8,128)(2,1)S(1)}, u32[]{:S(2)}, u32[]{:S(2)}) collective-permute-start(bf16[384,384]{1,0:T(8,128)(2,1)S(1)} %get-tuple-element.66), channel_id=1, source_target_pairs={{8,16},{12,20},{16,8},{20,12},{9,17},{13,21},{17,9},{21,13},{10,18... | collective-permute-start | bytes 884744 | tf_op jit(solution)/shard_map/ppermute | solution.py:539
  41.6 3.6 %collective-permute-start.6 = (f32[1,192]{1,0:T(1,128)S(1)}, f32[1,192]{1,0:T(1,128)S(1)}, u32[]{:S(2)}, u32[]{:S(2)}) collective-permute-start(f32[1,192]{1,0:T(1,128)S(1)} %get-tuple-element.56.dots), channel_id=1, source_target_pairs={{0,2},{1,3},{2,0},{3,1},{4,6},{5,7},{6,4},{7,5},{8,10},{9,11},{10,... | collective-permute-start | bytes 2312 | tf_op jit(solution)/shard_map/ppermute | solution.py:536
  43.2 7.0 %copy-start.5 = (f32[192]{0:T(256)S(1)}, f32[192]{0:T(256)}, u32[]{:S(2)}) copy-start(f32[192]{0:T(256)} %param.14) | copy-start | bytes 2308

commit v7 on v6

--- a/solution.py
+++ b/solution.py
@@ -455,7 +455,7 @@
 
 def four_join_kernel(
     heads, positions, logit, dots, dots_far, moving_sum, staying_sum, grads_guest, own_near,
-    middle, skip, cross, late, query_grad, key_grad, value_grad, router
+    middle, cross, skip, late, query_grad, key_grad, value_grad, router
 ):
     slots, half = moving_sum.shape[0] // 4, moving_sum.shape[1]
     shard = lax.axis_index("seq")
@@ -514,6 +514,10 @@
         scratch=[pltpu.VMEM(total.shape, F32)],
     )
     early = lax.ppermute(early, "seq", pairs([(i, i) for i in range(4)], 1))
+    (early,) = call(
+        follow_kernel, [low], early, turn, ins=[pl.ANY, pltpu.VMEM], outs=[pl.ANY],
+        aliases={0: 0}, flops=SUM_FLOPS,
+    )
     turn, own_near, other_near, step_back, near_total, grads_guest, skip_part = call(
         functools.partial(four_skip_kernel, heads),
         [row, total, total, low, total, total, total],
@@ -548,7 +552,7 @@
         functools.partial(four_join_kernel, heads),
         [shape(slots, BF16, width)] * 3 + [row],
         positions, logit, dots, dots_far, moving_sum, staying_sum, grads_guest, own_near,
-        middle, skip, cross, late,
+        middle, cross, skip, late,
     )
 
 

time: 51.8 us -> 53.5 us (1.033)
  waiting for transfers between devices: 15.1 us -> 16.3 us
    ppermute x1, waiting for transfers between devices: 5.57 us -> 10.1 us  [four_levels(): lax.ppermute(near_low, 'seq', pairs([(0, 1), (1, 0), (2, 3), (3, 2)]))]
    ppermute x1, waiting for transfers between devices: 4.79 us -> 2.27 us  [four_levels(): cross = lax.ppermute(cross_low, 'seq', pairs([(1, 0), (2, 3)], 1))]
    ppermute x1, starting transfers between devices: 1.82 us -> 3.92 us  [four_levels(): early = lax.ppermute(early, 'seq', pairs([(i, i) for i in range(4)], 1))]
    ppermute x1, starting transfers between devices: 6.21 us -> 4.8 us  [four_levels(): lax.ppermute(near_low, 'seq', pairs([(0, 1), (1, 0), (2, 3), (3, 2)]))]
    ppermute x1, waiting for transfers between devices: 0.68 us -> 0.01 us  [four_levels(): skip = lax.ppermute(far_send, 'seq', pairs([(0, 2), (3, 1)]))]
    pallas_call x9 -> x10, Pallas kernels: 9.53 us -> 9.56 us  [call(): pl.pallas_call(kernel, out_shape=out_shape, in_specs=[pl.BlockSpec(memory...]
  transfers between devices with their start and end apart: 13 -> 13, of which waited for: 6 -> 4; matrix products, arithmetic and copies ran while one was open for 0% -> 0% of each run, Pallas kernels for 9% -> 9%
where the time goes in v7:
time: 53.5 us; the launch traced here: 53.2 us
  starting transfers between devices  24.3 us (45%)
  waiting for transfers between devices  16.3 us (30%)
  Pallas kernels  9.56 us (18%)
  local copies, waits for them, and re-layouts  2.16 us (4%)
  between operations  0.85 us (2%)
    ppermute x1, waiting for transfers between devices, four_levels(): lax.ppermute(near_low, 'seq', pairs([(0, 1), (1, 0), (2, 3), (3, 2)]))  10.1 us
    pallas_call x10, Pallas kernels, call(): pl.pallas_call(kernel, out_shape=out_shape, in_specs=[pl.BlockSpec(memory...  9.56 us
    ppermute x1, starting transfers between devices, four_levels(): lax.ppermute(near_low, 'seq', pairs([(0, 1), (1, 0), (2, 3), (3, 2)]))  4.8 us
    ppermute x1, starting transfers between devices, four_levels(): skip = lax.ppermute(far_send, 'seq', pairs([(0, 2), (3, 1)]))  4.54 us
    ppermute x1, starting transfers between devices, four_levels(): early = lax.ppermute(early, 'seq', pairs([(i, i) for i in range(4)], 1))  3.92 us
    ppermute x1, starting transfers between devices, four_levels(): other = lax.ppermute(own, 'seq', pairs([(i, i) for i in range(4)], 1))  3.03 us
    ppermute x1, waiting for transfers between devices, four_levels(): cross = lax.ppermute(cross_low, 'seq', pairs([(1, 0), (2, 3)], 1))  2.27 us
    unnamed x14, local copies, waits for them, and re-layouts  2.16 us
  transfers between devices with their start and end apart: 13, of which 4 were waited for; matrix products, arithmetic and copies ran while one was open for 0% of the time, Pallas kernels for 9%

profile of v7, /device:TPU:0, one launch (start us, length us, event | category | flops | bytes accessed | tf_op | source)
XLA Modules:
  0.0 53.2 jit_solution(11652140357210786752)
XLA Ops:
  0.6 3.8 %shard_map.111 = (f32[1,192]{1,0:T(1,128)}, bf16[800,384]{1,0:T(8,128)(2,1)}, bf16[800,384]{1,0:T(8,128)(2,1)}, bf16[400,384]{1,0:T(8,128)(2,1)}, bf16[400,384]{1,0:T(8,128)(2,1)}) custom-call(bf16[192,768]{1,0:T(8,128)(2,1)} %refs_0_.1, bf16[192,768]{1,0:T(8,128)(2,1)} %refs_1_.1, f32[1,192]{1,0:T(1,128)} %bitcast.11, f32[6,192]{1,0:T(8,128)} %bitcast.13, ...), custom_call_target="tpu_custom_call" | custom-call | flops 1024 | bytes 1024 | tf_op jit(solution)/shard_map/pallas_call | solution.py:666
  4.4 3.0 %collective-permute-start = (bf16[800,384]{1,0:T(8,128)(2,1)}, bf16[800,384]{1,0:T(8,128)(2,1)S(1)}, u32[]{:S(2)}, u32[]{:S(2)}) collective-permute-start(bf16[800,384]{1,0:T(8,128)(2,1)} %get-tuple-element.40.own), channel_id=1, source_target_pairs={{0,4},{4,0},{8,12},{12,8},{16,20},{20,16},{24,28},{28,24},{1,5},{5... | collective-permute-start | bytes 1843208 | tf_op jit(solution)/shard_map/ppermute | solution.py:497
  7.5 1.6 %collective-permute-start.1 = (bf16[400,384]{1,0:T(8,128)(2,1)}, bf16[400,384]{1,0:T(8,128)(2,1)S(1)}, u32[]{:S(2)}, u32[]{:S(2)}) collective-permute-start(bf16[400,384]{1,0:T(8,128)(2,1)} %get-tuple-element.43), channel_id=1, source_target_pairs={{0,8},{4,12},{8,0},{12,4},{16,24},{20,28},{24,16},{28,20},{1,9},{5... | collective-permute-start | bytes 921608 | tf_op jit(solution)/shard_map/ppermute | solution.py:496
  9.1 4.5 %collective-permute-start.2 = (bf16[400,384]{1,0:T(8,128)(2,1)}, bf16[400,384]{1,0:T(8,128)(2,1)S(1)}, u32[]{:S(2)}, u32[]{:S(2)}) collective-permute-start(bf16[400,384]{1,0:T(8,128)(2,1)} %get-tuple-element.44), channel_id=1, source_target_pairs={{0,16},{4,20},{24,8},{28,12},{1,17},{5,21},{25,9},{29,13},{2,18},{... | collective-permute-start | bytes 921608 | tf_op jit(solution)/shard_map/ppermute | solution.py:498
  13.6 0.7 %collective-permute-start.4 = (bf16[400,384]{1,0:T(8,128)(2,1)}, bf16[400,384]{1,0:T(8,128)(2,1)S(1)}, u32[]{:S(2)}, u32[]{:S(2)}) collective-permute-start(bf16[400,384]{1,0:T(8,128)(2,1)} %get-tuple-element.44), channel_id=1, source_target_pairs={{8,16},{12,20},{16,8},{20,12},{9,17},{13,21},{17,9},{21,13},{10,18... | collective-permute-start | bytes 921608 | tf_op jit(solution)/shard_map/ppermute | solution.py:499
  14.3 1.1 %copy-done = bf16[800,384]{1,0:T(8,128)(2,1)S(1)} copy-done((bf16[800,384]{1,0:T(8,128)(2,1)S(1)}, bf16[800,384]{1,0:T(8,128)(2,1)}, u32[]{:S(2)}) %copy-start) | copy-done | bytes 614424
  15.4 1.1 %copy-done.2 = bf16[800,384]{1,0:T(8,128)(2,1)S(1)} copy-done((bf16[800,384]{1,0:T(8,128)(2,1)S(1)}, bf16[800,384]{1,0:T(8,128)(2,1)}, u32[]{:S(2)}) %copy-start.2) | copy-done | bytes 614424
  16.5 2.1 %shard_map.112 = (f32[1,192]{1,0:T(1,128)S(1)}, f32[768,384]{1,0:T(8,128)S(1)}, f32[768,384]{1,0:T(8,128)S(1)}) custom-call(s32[12,128]{1,0:T(8,128)S(1)} %bitcast.5, bf16[800,384]{1,0:T(8,128)(2,1)S(1)} %copy-done, bf16[800,384]{1,0:T(8,128)(2,1)S(1)} %copy-done.2), custom_call_target="tpu_custom_call" | custom-call | flops 1024 | bytes 1024 | tf_op jit(solution)/shard_map/pallas_call | solution.py:666
  18.6 0.0 copy-start.6
  18.6 0.0 collective-permute-done.1.block
  18.6 0.8 %collective-permute-start.5 = (bf16[400,384]{1,0:T(8,128)(2,1)S(1)}, bf16[400,384]{1,0:T(8,128)(2,1)S(1)}, u32[]{:S(2)}, u32[]{:S(2)}) collective-permute-start(bf16[400,384]{1,0:T(8,128)(2,1)S(1)} %shard_map.114.near), channel_id=1, source_target_pairs={{8,12},{12,8},{16,20},{20,16},{9,13},{13,9},{17,21},{21,17},{10,14... | collective-permute-start | bytes 921608 | tf_op jit(solution)/shard_map/ppermute | solution.py:509
  19.4 2.1 %collective-permute-done.other = bf16[800,384]{1,0:T(8,128)(2,1)S(1)} collective-permute-done((bf16[800,384]{1,0:T(8,128)(2,1)}, bf16[800,384]{1,0:T(8,128)(2,1)S(1)}, u32[]{:S(2)}, u32[]{:S(2)}) %collective-permute-start) | collective-permute-done | bytes 614432 | tf_op jit(solution)/shard_map/ppermute | solution.py:497
  21.6 3.9 %collective-permute-start.8 = (bf16[384,384]{1,0:T(8,128)(2,1)S(1)}, bf16[384,384]{1,0:T(8,128)(2,1)S(1)}, u32[]{:S(2)}, u32[]{:S(2)}) collective-permute-start(bf16[384,384]{1,0:T(8,128)(2,1)S(1)} %get-tuple-element.61), channel_id=1, source_target_pairs={{0,4},{4,0},{8,12},{12,8},{16,20},{20,16},{24,28},{28,24},{1,5},{5... | collective-permute-start | bytes 884744 | tf_op jit(solution)/shard_map/ppermute | solution.py:516
  25.5 0.0 collective-permute-start.3
  25.5 0.0 collective-permute-done.2.skip
  25.5 1.7 %shard_map.115 = (f32[1,192]{1,0:T(1,128)S(1)}, f32[384,384]{1,0:T(8,128)S(1)}, f32[384,384]{1,0:T(8,128)S(1)}, bf16[384,384]{1,0:T(8,128)(2,1)S(1)}, f32[384,38...) custom-call(s32[12,128]{1,0:T(8,128)S(1)} %bitcast.7, f32[1,192]{1,0:T(1,128)S(1)} %get-tuple-element.42.after, ...), custom_call_target="tpu_custom_call" | custom-call | flops 1024 | bytes 1024 | tf_op jit(solution)/shard_map/pallas_call | solution.py:666
  27.2 0.0 collective-permute-done.4.middle
  27.2 0.1 shard_map.116
  27.3 4.8 %collective-permute-start.7 = (bf16[384,384]{1,0:T(8,128)(2,1)S(1)}, bf16[384,384]{1,0:T(8,128)(2,1)S(1)}, u32[]{:S(2)}, u32[]{:S(2)}) collective-permute-start(bf16[384,384]{1,0:T(8,128)(2,1)S(1)} %get-tuple-element.60), channel_id=1, source_target_pairs={{0,8},{4,12},{8,0},{12,4},{16,24},{20,28},{24,16},{28,20},{1,9},{5... | collective-permute-start | bytes 884744 | tf_op jit(solution)/shard_map/ppermute | solution.py:532
  32.1 0.4 shard_map.117
  32.5 1.3 %collective-permute-start.10 = (bf16[384,384]{1,0:T(8,128)(2,1)S(1)}, bf16[384,384]{1,0:T(8,128)(2,1)S(1)}, u32[]{:S(2)}, u32[]{:S(2)}) collective-permute-start(bf16[384,384]{1,0:T(8,128)(2,1)S(1)} %get-tuple-element.67), channel_id=1, source_target_pairs={{8,4},{12,0},{16,28},{20,24},{9,5},{13,1},{17,29},{21,25},{10,6},{... | collective-permute-start | bytes 884744 | tf_op jit(solution)/shard_map/ppermute | solution.py:542
  33.8 1.3 %collective-permute-start.11 = (bf16[384,384]{1,0:T(8,128)(2,1)S(1)}, bf16[384,384]{1,0:T(8,128)(2,1)S(1)}, u32[]{:S(2)}, u32[]{:S(2)}) collective-permute-start(bf16[384,384]{1,0:T(8,128)(2,1)S(1)} %get-tuple-element.68), channel_id=1, source_target_pairs={{16,0},{20,4},{8,24},{12,28},{17,1},{21,5},{9,25},{13,29},{18,2},{... | collective-permute-start | bytes 884744 | tf_op jit(solution)/shard_map/ppermute | solution.py:541
  35.1 0.2 collective-permute-start.12
  35.3 0.0 collective-permute-done.8.block
  35.3 0.7 %collective-permute-start.9 = (bf16[384,384]{1,0:T(8,128)(2,1)S(1)}, bf16[384,384]{1,0:T(8,128)(2,1)S(1)}, u32[]{:S(2)}, u32[]{:S(2)}) collective-permute-start(bf16[384,384]{1,0:T(8,128)(2,1)S(1)} %get-tuple-element.66), channel_id=1, source_target_pairs={{8,16},{12,20},{16,8},{20,12},{9,17},{13,21},{17,9},{21,13},{10,18... | collective-permute-start | bytes 884744 | tf_op jit(solution)/shard_map/ppermute | solution.py:543
  36.0 10.1 %collective-permute-done.7.near = bf16[384,384]{1,0:T(8,128)(2,1)S(1)} collective-permute-done((bf16[384,384]{1,0:T(8,128)(2,1)S(1)}, bf16[384,384]{1,0:T(8,128)(2,1)S(1)}, u32[]{:S(2)}, u32[]{:S(2)}) %collective-permute-start.7) | collective-permute-done | bytes 294944 | tf_op jit(solution)/shard_map/ppermute | solution.py:532
  46.1 1.5 %collective-permute-start.6 = (f32[1,192]{1,0:T(1,128)S(1)}, f32[1,192]{1,0:T(1,128)S(1)}, u32[]{:S(2)}, u32[]{:S(2)}) collective-permute-start(f32[1,192]{1,0:T(1,128)S(1)} %get-tuple-element.56.dots), channel_id=1, source_target_pairs={{0,2},{1,3},{2,0},{3,1},{4,6},{5,7},{6,4},{7,5},{8,10},{9,11},{10,... | collective-permute-start | bytes 2312 | tf_op jit(solution)/shard_map/ppermute | solution.py:540
  47.6 0.3 shard_map.119
  47.8 1.8 %collective-permute-done.6.dots_far = f32[1,192]{1,0:T(1,128)S(1)} collective-permute-done((f32[1,192]{1,0:T(1,128)S(1)}, f32[1,192]{1,0:T(1,128)S(1)}, u32[]{:S(2)}, u32[]{:S(2)}) %collective-permute-start.6) | collective-permute-done | bytes 800 | tf_op jit(solution)/shard_map/ppermute | solution.py:540
  49.7 2.3 %collective-permute-done.10.cross = bf16[384,384]{1,0:T(8,128)(2,1)S(1)} collective-permute-done((bf16[384,384]{1,0:T(8,128)(2,1)S(1)}, bf16[384,384]{1,0:T(8,128)(2,1)S(1)}, u32[]{:S(2)}, u32[]{:S(2)}) %collective-permute-start.10) | collective-permute-done | bytes 294944 | tf_op jit(solution)/shard_map/ppermute | solution.py:542
  51.9 0.0 collective-permute-done.11.skip
  52.0 1.2 %shard_map.120 = (bf16[192,768]{1,0:T(8,128)(2,1)}, bf16[192,768]{1,0:T(8,128)(2,1)}, bf16[192,768]{1,0:T(8,128)(2,1)}, f32[1,192]{1,0:T(1,128)}) custom-call(s32[12,128]{1,0:T(8,128)S(1)} %bitcast.10, f32[1,192]{1,0:T(1,128)S(1)} %bitcast.12, f32[1,192]{1,0:T(1,128)S(1)} %get-tuple-element.56.dots, f32[1,192]{1,0:T(1,128)S(1)} %collective-permute-done.6.dots_far, ...), custom_call_target="tpu_custom_call" | custom-call | flops 1024 | bytes 1024 | tf_op jit(solution)/shard_map/pallas_call | solution.py:666
  (18 shorter events, 0.1 us)
Async XLA Ops:
  0.6 13.7 %copy-start.4 = (s32[1536]{0:T(1024)S(1)}, s32[1536]{0:T(1024)}, u32[]{:S(2)}) copy-start(s32[1536]{0:T(1024)} %param.15) | copy-start | bytes 18436
  4.4 17.1 %collective-permute-start = (bf16[800,384]{1,0:T(8,128)(2,1)}, bf16[800,384]{1,0:T(8,128)(2,1)S(1)}, u32[]{:S(2)}, u32[]{:S(2)}) collective-permute-start(bf16[800,384]{1,0:T(8,128)(2,1)} %get-tuple-element.40.own), channel_id=1, source_target_pairs={{0,4},{4,0},{8,12},{12,8},{16,20},{20,16},{24,28},{28,24},{1,5},{5... | collective-permute-start | bytes 1843208 | tf_op jit(solution)/shard_map/ppermute | solution.py:497
  7.5 11.1 %collective-permute-start.1 = (bf16[400,384]{1,0:T(8,128)(2,1)}, bf16[400,384]{1,0:T(8,128)(2,1)S(1)}, u32[]{:S(2)}, u32[]{:S(2)}) collective-permute-start(bf16[400,384]{1,0:T(8,128)(2,1)} %get-tuple-element.43), channel_id=1, source_target_pairs={{0,8},{4,12},{8,0},{12,4},{16,24},{20,28},{24,16},{28,20},{1,9},{5... | collective-permute-start | bytes 921608 | tf_op jit(solution)/shard_map/ppermute | solution.py:496
  9.1 16.4 %collective-permute-start.2 = (bf16[400,384]{1,0:T(8,128)(2,1)}, bf16[400,384]{1,0:T(8,128)(2,1)S(1)}, u32[]{:S(2)}, u32[]{:S(2)}) collective-permute-start(bf16[400,384]{1,0:T(8,128)(2,1)} %get-tuple-element.44), channel_id=1, source_target_pairs={{0,16},{4,20},{24,8},{28,12},{1,17},{5,21},{25,9},{29,13},{2,18},{... | collective-permute-start | bytes 921608 | tf_op jit(solution)/shard_map/ppermute | solution.py:498
  13.6 13.6 %collective-permute-start.4 = (bf16[400,384]{1,0:T(8,128)(2,1)}, bf16[400,384]{1,0:T(8,128)(2,1)S(1)}, u32[]{:S(2)}, u32[]{:S(2)}) collective-permute-start(bf16[400,384]{1,0:T(8,128)(2,1)} %get-tuple-element.44), channel_id=1, source_target_pairs={{8,16},{12,20},{16,8},{20,12},{9,17},{13,21},{17,9},{21,13},{10,18... | collective-permute-start | bytes 921608 | tf_op jit(solution)/shard_map/ppermute | solution.py:499
  14.3 1.1 %copy-start = (bf16[800,384]{1,0:T(8,128)(2,1)S(1)}, bf16[800,384]{1,0:T(8,128)(2,1)}, u32[]{:S(2)}) copy-start(bf16[800,384]{1,0:T(8,128)(2,1)} %get-tuple-element.39.mine) | copy-start | bytes 1843204
  15.4 1.1 %copy-start.2 = (bf16[800,384]{1,0:T(8,128)(2,1)S(1)}, bf16[800,384]{1,0:T(8,128)(2,1)}, u32[]{:S(2)}) copy-start(bf16[800,384]{1,0:T(8,128)(2,1)} %get-tuple-element.40.own) | copy-start | bytes 1843204
  16.5 5.1 %copy-start.1 = (bf16[800,384]{1,0:T(8,128)(2,1)S(1)}, bf16[800,384]{1,0:T(8,128)(2,1)}, u32[]{:S(2)}) copy-start(bf16[800,384]{1,0:T(8,128)(2,1)} %get-tuple-element.39.mine) | copy-start | bytes 1843204
  18.6 6.9 %copy-start.6 = (f32[1,192]{1,0:T(1,128)S(1)}, f32[1,192]{1,0:T(1,128)}, u32[]{:S(2)}) copy-start(f32[1,192]{1,0:T(1,128)} %get-tuple-element.46.dots) | copy-start | bytes 2308
  18.6 6.9 %copy-start.3 = (bf16[800,384]{1,0:T(8,128)(2,1)S(1)}, bf16[800,384]{1,0:T(8,128)(2,1)}, u32[]{:S(2)}) copy-start(bf16[800,384]{1,0:T(8,128)(2,1)} %get-tuple-element.40.own) | copy-start | bytes 1843204
  18.6 13.5 %collective-permute-start.5 = (bf16[400,384]{1,0:T(8,128)(2,1)S(1)}, bf16[400,384]{1,0:T(8,128)(2,1)S(1)}, u32[]{:S(2)}, u32[]{:S(2)}) collective-permute-start(bf16[400,384]{1,0:T(8,128)(2,1)S(1)} %shard_map.114.near), channel_id=1, source_target_pairs={{8,12},{12,8},{16,20},{20,16},{9,13},{13,9},{17,21},{21,17},{10,14... | collective-permute-start | bytes 921608 | tf_op jit(solution)/shard_map/ppermute | solution.py:509
  21.6 13.7 %collective-permute-start.8 = (bf16[384,384]{1,0:T(8,128)(2,1)S(1)}, bf16[384,384]{1,0:T(8,128)(2,1)S(1)}, u32[]{:S(2)}, u32[]{:S(2)}) collective-permute-start(bf16[384,384]{1,0:T(8,128)(2,1)S(1)} %get-tuple-element.61), channel_id=1, source_target_pairs={{0,4},{4,0},{8,12},{12,8},{16,20},{20,16},{24,28},{28,24},{1,5},{5... | collective-permute-start | bytes 884744 | tf_op jit(solution)/shard_map/ppermute | solution.py:516
  25.5 1.7 %collective-permute-start.3 = (f32[1,192]{1,0:T(1,128)S(1)}, f32[1,192]{1,0:T(1,128)S(1)}, u32[]{:S(2)}, u32[]{:S(2)}) collective-permute-start(f32[1,192]{1,0:T(1,128)S(1)} %copy-done.6), channel_id=1, source_target_pairs={{0,1},{1,0},{2,3},{3,2},{4,5},{5,4},{6,7},{7,6},{8,9},{9,8},{10,11... | collective-permute-start | bytes 2312 | tf_op jit(solution)/shard_map/ppermute | solution.py:526
  27.3 18.8 %collective-permute-start.7 = (bf16[384,384]{1,0:T(8,128)(2,1)S(1)}, bf16[384,384]{1,0:T(8,128)(2,1)S(1)}, u32[]{:S(2)}, u32[]{:S(2)}) collective-permute-start(bf16[384,384]{1,0:T(8,128)(2,1)S(1)} %get-tuple-element.60), channel_id=1, source_target_pairs={{0,8},{4,12},{8,0},{12,4},{16,24},{20,28},{24,16},{28,20},{1,9},{5... | collective-permute-start | bytes 884744 | tf_op jit(solution)/shard_map/ppermute | solution.py:532
  32.5 19.4 %collective-permute-start.10 = (bf16[384,384]{1,0:T(8,128)(2,1)S(1)}, bf16[384,384]{1,0:T(8,128)(2,1)S(1)}, u32[]{:S(2)}, u32[]{:S(2)}) collective-permute-start(bf16[384,384]{1,0:T(8,128)(2,1)S(1)} %get-tuple-element.67), channel_id=1, source_target_pairs={{8,4},{12,0},{16,28},{20,24},{9,5},{13,1},{17,29},{21,25},{10,6},{... | collective-permute-start | bytes 884744 | tf_op jit(solution)/shard_map/ppermute | solution.py:542
  33.8 18.1 %collective-permute-start.11 = (bf16[384,384]{1,0:T(8,128)(2,1)S(1)}, bf16[384,384]{1,0:T(8,128)(2,1)S(1)}, u32[]{:S(2)}, u32[]{:S(2)}) collective-permute-start(bf16[384,384]{1,0:T(8,128)(2,1)S(1)} %get-tuple-element.68), channel_id=1, source_target_pairs={{16,0},{20,4},{8,24},{12,28},{17,1},{21,5},{9,25},{13,29},{18,2},{... | collective-permute-start | bytes 884744 | tf_op jit(solution)/shard_map/ppermute | solution.py:541
  35.1 16.8 %collective-permute-start.12 = (bf16[384,384]{1,0:T(8,128)(2,1)S(1)}, bf16[384,384]{1,0:T(8,128)(2,1)S(1)}, u32[]{:S(2)}, u32[]{:S(2)}) collective-permute-start(bf16[384,384]{1,0:T(8,128)(2,1)S(1)} %get-tuple-element.69), channel_id=1, source_target_pairs={{0,4},{4,0},{8,12},{12,8},{16,20},{20,16},{24,28},{28,24},{1,5},{5... | collective-permute-start | bytes 884744 | tf_op jit(solution)/shard_map/ppermute | solution.py:544
  35.3 16.6 %collective-permute-start.9 = (bf16[384,384]{1,0:T(8,128)(2,1)S(1)}, bf16[384,384]{1,0:T(8,128)(2,1)S(1)}, u32[]{:S(2)}, u32[]{:S(2)}) collective-permute-start(bf16[384,384]{1,0:T(8,128)(2,1)S(1)} %get-tuple-element.66), channel_id=1, source_target_pairs={{8,16},{12,20},{16,8},{20,12},{9,17},{13,21},{17,9},{21,13},{10,18... | collective-permute-start | bytes 884744 | tf_op jit(solution)/shard_map/ppermute | solution.py:543
  46.1 3.6 %collective-permute-start.6 = (f32[1,192]{1,0:T(1,128)S(1)}, f32[1,192]{1,0:T(1,128)S(1)}, u32[]{:S(2)}, u32[]{:S(2)}) collective-permute-start(f32[1,192]{1,0:T(1,128)S(1)} %get-tuple-element.56.dots), channel_id=1, source_target_pairs={{0,2},{1,3},{2,0},{3,1},{4,6},{5,7},{6,4},{7,5},{8,10},{9,11},{10,... | collective-permute-start | bytes 2312 | tf_op jit(solution)/shard_map/ppermute | solution.py:540
  47.6 4.4 %copy-start.5 = (f32[192]{0:T(256)S(1)}, f32[192]{0:T(256)}, u32[]{:S(2)}) copy-start(f32[192]{0:T(256)} %param.14) | copy-start | bytes 2308

commit v8 on v7

--- a/solution.py
+++ b/solution.py
@@ -514,10 +514,6 @@
         scratch=[pltpu.VMEM(total.shape, F32)],
     )
     early = lax.ppermute(early, "seq", pairs([(i, i) for i in range(4)], 1))
-    (early,) = call(
-        follow_kernel, [low], early, turn, ins=[pl.ANY, pltpu.VMEM], outs=[pl.ANY],
-        aliases={0: 0}, flops=SUM_FLOPS,
-    )
     turn, own_near, other_near, step_back, near_total, grads_guest, skip_part = call(
         functools.partial(four_skip_kernel, heads),
         [row, total, total, low, total, total, total],

time: 53.5 us -> 51.8 us (0.968)
  waiting for transfers between devices: 16.3 us -> 15.1 us
    ppermute x1, waiting for transfers between devices: 10.1 us -> 0.85 us  [four_levels(): lax.ppermute(near_low, 'seq', pairs([(0, 1), (1, 0), (2, 3), (3, 2)]))]
    ppermute x1, waiting for transfers between devices: 0.01 us -> 4.33 us  [four_levels(): early = lax.ppermute(early, 'seq', pairs([(i, i) for i in range(4)], 1))]
    ppermute x1, waiting for transfers between devices: 2.27 us -> 5.27 us  [four_levels(): cross = lax.ppermute(cross_low, 'seq', pairs([(1, 0), (2, 3)], 1))]
    ppermute x1, starting transfers between devices: 3.92 us -> 1.82 us  [four_levels(): early = lax.ppermute(early, 'seq', pairs([(i, i) for i in range(4)], 1))]
    ppermute x1, starting transfers between devices: 4.8 us -> 6.21 us  [four_levels(): lax.ppermute(near_low, 'seq', pairs([(0, 1), (1, 0), (2, 3), (3, 2)]))]
    ppermute x1, waiting for transfers between devices: 0.01 us -> 0.68 us  [four_levels(): skip = lax.ppermute(far_send, 'seq', pairs([(0, 2), (3, 1)]))]
    pallas_call x10 -> x9, Pallas kernels: 9.56 us -> 9.54 us  [call(): pl.pallas_call(kernel, out_shape=out_shape, in_specs=[pl.BlockSpec(memory...]
  transfers between devices with their start and end apart: 13 -> 13, of which waited for: 4 -> 7; matrix products, arithmetic and copies ran while one was open for 0% -> 0% of each run, Pallas kernels for 9% -> 9%
where the time goes in v8:
time: 51.8 us; the launch traced here: 51.5 us
  starting transfers between devices  23.8 us (46%)
  waiting for transfers between devices  15.1 us (29%)
  Pallas kernels  9.54 us (18%)
  local copies, waits for them, and re-layouts  2.16 us (4%)
  between operations  0.83 us (2%)
    pallas_call x9, Pallas kernels, call(): pl.pallas_call(kernel, out_shape=out_shape, in_specs=[pl.BlockSpec(memory...  9.54 us
    ppermute x1, starting transfers between devices, four_levels(): lax.ppermute(near_low, 'seq', pairs([(0, 1), (1, 0), (2, 3), (3, 2)]))  6.21 us
    ppermute x1, waiting for transfers between devices, four_levels(): cross = lax.ppermute(cross_low, 'seq', pairs([(1, 0), (2, 3)], 1))  5.27 us
    ppermute x1, starting transfers between devices, four_levels(): skip = lax.ppermute(far_send, 'seq', pairs([(0, 2), (3, 1)]))  4.54 us
    ppermute x1, waiting for transfers between devices, four_levels(): early = lax.ppermute(early, 'seq', pairs([(i, i) for i in range(4)], 1))  4.33 us
    ppermute x1, starting transfers between devices, four_levels(): other = lax.ppermute(own, 'seq', pairs([(i, i) for i in range(4)], 1))  3.03 us
    unnamed x14, local copies, waits for them, and re-layouts  2.16 us
    ppermute x1, waiting for transfers between devices, four_levels(): other = lax.ppermute(own, 'seq', pairs([(i, i) for i in range(4)], 1))  2.04 us
  transfers between devices with their start and end apart: 13, of which 7 were waited for; matrix products, arithmetic and copies ran while one was open for 0% of the time, Pallas kernels for 9%

profile of v8, /device:TPU:0, one launch (start us, length us, event | category | flops | bytes accessed | tf_op | source)
XLA Modules:
  0.0 51.5 jit_solution(11051528701258243401)
XLA Ops:
  0.6 3.8 %shard_map.111 = (f32[1,192]{1,0:T(1,128)}, bf16[800,384]{1,0:T(8,128)(2,1)}, bf16[800,384]{1,0:T(8,128)(2,1)}, bf16[400,384]{1,0:T(8,128)(2,1)}, bf16[400,384]{1,0:T(8,128)(2,1)}) custom-call(bf16[192,768]{1,0:T(8,128)(2,1)} %refs_0_.1, bf16[192,768]{1,0:T(8,128)(2,1)} %refs_1_.1, f32[1,192]{1,0:T(1,128)} %bitcast.11, f32[6,192]{1,0:T(8,128)} %bitcast.13, ...), custom_call_target="tpu_custom_call" | custom-call | flops 1024 | bytes 1024 | tf_op jit(solution)/shard_map/pallas_call | solution.py:662
  4.4 0.0 copy-start.6
  4.5 3.0 %collective-permute-start = (bf16[800,384]{1,0:T(8,128)(2,1)}, bf16[800,384]{1,0:T(8,128)(2,1)S(1)}, u32[]{:S(2)}, u32[]{:S(2)}) collective-permute-start(bf16[800,384]{1,0:T(8,128)(2,1)} %get-tuple-element.40.own), channel_id=1, source_target_pairs={{0,4},{4,0},{8,12},{12,8},{16,20},{20,16},{24,28},{28,24},{1,5},{5... | collective-permute-start | bytes 1843208 | tf_op jit(solution)/shard_map/ppermute | solution.py:497
  7.5 1.6 %collective-permute-start.1 = (bf16[400,384]{1,0:T(8,128)(2,1)}, bf16[400,384]{1,0:T(8,128)(2,1)S(1)}, u32[]{:S(2)}, u32[]{:S(2)}) collective-permute-start(bf16[400,384]{1,0:T(8,128)(2,1)} %get-tuple-element.43), channel_id=1, source_target_pairs={{0,8},{4,12},{8,0},{12,4},{16,24},{20,28},{24,16},{28,20},{1,9},{5... | collective-permute-start | bytes 921608 | tf_op jit(solution)/shard_map/ppermute | solution.py:496
  9.1 4.5 %collective-permute-start.2 = (bf16[400,384]{1,0:T(8,128)(2,1)}, bf16[400,384]{1,0:T(8,128)(2,1)S(1)}, u32[]{:S(2)}, u32[]{:S(2)}) collective-permute-start(bf16[400,384]{1,0:T(8,128)(2,1)} %get-tuple-element.44), channel_id=1, source_target_pairs={{0,16},{4,20},{24,8},{28,12},{1,17},{5,21},{25,9},{29,13},{2,18},{... | collective-permute-start | bytes 921608 | tf_op jit(solution)/shard_map/ppermute | solution.py:498
  13.6 0.7 %collective-permute-start.4 = (bf16[400,384]{1,0:T(8,128)(2,1)}, bf16[400,384]{1,0:T(8,128)(2,1)S(1)}, u32[]{:S(2)}, u32[]{:S(2)}) collective-permute-start(bf16[400,384]{1,0:T(8,128)(2,1)} %get-tuple-element.44), channel_id=1, source_target_pairs={{8,16},{12,20},{16,8},{20,12},{9,17},{13,21},{17,9},{21,13},{10,18... | collective-permute-start | bytes 921608 | tf_op jit(solution)/shard_map/ppermute | solution.py:499
  14.3 1.1 %copy-done = bf16[800,384]{1,0:T(8,128)(2,1)S(1)} copy-done((bf16[800,384]{1,0:T(8,128)(2,1)S(1)}, bf16[800,384]{1,0:T(8,128)(2,1)}, u32[]{:S(2)}) %copy-start) | copy-done | bytes 614424
  15.4 1.1 %copy-done.2 = bf16[800,384]{1,0:T(8,128)(2,1)S(1)} copy-done((bf16[800,384]{1,0:T(8,128)(2,1)S(1)}, bf16[800,384]{1,0:T(8,128)(2,1)}, u32[]{:S(2)}) %copy-start.2) | copy-done | bytes 614424
  16.5 2.1 %shard_map.112 = (f32[1,192]{1,0:T(1,128)S(1)}, f32[768,384]{1,0:T(8,128)S(1)}, f32[768,384]{1,0:T(8,128)S(1)}) custom-call(s32[12,128]{1,0:T(8,128)S(1)} %bitcast.5, bf16[800,384]{1,0:T(8,128)(2,1)S(1)} %copy-done, bf16[800,384]{1,0:T(8,128)(2,1)S(1)} %copy-done.2), custom_call_target="tpu_custom_call" | custom-call | flops 1024 | bytes 1024 | tf_op jit(solution)/shard_map/pallas_call | solution.py:662
  18.6 0.0 collective-permute-done.1.block
  18.6 0.8 %collective-permute-start.5 = (bf16[400,384]{1,0:T(8,128)(2,1)S(1)}, bf16[400,384]{1,0:T(8,128)(2,1)S(1)}, u32[]{:S(2)}, u32[]{:S(2)}) collective-permute-start(bf16[400,384]{1,0:T(8,128)(2,1)S(1)} %shard_map.114.near), channel_id=1, source_target_pairs={{8,12},{12,8},{16,20},{20,16},{9,13},{13,9},{17,21},{21,17},{10,14... | collective-permute-start | bytes 921608 | tf_op jit(solution)/shard_map/ppermute | solution.py:509
  19.4 0.1 collective-permute-start.3
  19.5 2.0 %collective-permute-done.other = bf16[800,384]{1,0:T(8,128)(2,1)S(1)} collective-permute-done((bf16[800,384]{1,0:T(8,128)(2,1)}, bf16[800,384]{1,0:T(8,128)(2,1)S(1)}, u32[]{:S(2)}, u32[]{:S(2)}) %collective-permute-start) | collective-permute-done | bytes 614432 | tf_op jit(solution)/shard_map/ppermute | solution.py:497
  21.6 0.7 %collective-permute-done.2.skip = bf16[400,384]{1,0:T(8,128)(2,1)S(1)} collective-permute-done((bf16[400,384]{1,0:T(8,128)(2,1)}, bf16[400,384]{1,0:T(8,128)(2,1)S(1)}, u32[]{:S(2)}, u32[]{:S(2)}) %collective-permute-start.2) | collective-permute-done | bytes 307232 | tf_op jit(solution)/shard_map/ppermute | solution.py:498
  22.3 1.7 %shard_map.115 = (f32[1,192]{1,0:T(1,128)S(1)}, f32[384,384]{1,0:T(8,128)S(1)}, f32[384,384]{1,0:T(8,128)S(1)}, bf16[384,384]{1,0:T(8,128)(2,1)S(1)}, f32[384,38...) custom-call(s32[12,128]{1,0:T(8,128)S(1)} %bitcast.7, f32[1,192]{1,0:T(1,128)S(1)} %get-tuple-element.42.after, ...), custom_call_target="tpu_custom_call" | custom-call | flops 1024 | bytes 1024 | tf_op jit(solution)/shard_map/pallas_call | solution.py:662
  23.9 0.0 collective-permute-done.3.dots_near
  24.0 0.1 shard_map.116
  24.0 6.2 %collective-permute-start.7 = (bf16[384,384]{1,0:T(8,128)(2,1)S(1)}, bf16[384,384]{1,0:T(8,128)(2,1)S(1)}, u32[]{:S(2)}, u32[]{:S(2)}) collective-permute-start(bf16[384,384]{1,0:T(8,128)(2,1)S(1)} %get-tuple-element.60), channel_id=1, source_target_pairs={{0,8},{4,12},{8,0},{12,4},{16,24},{20,28},{24,16},{28,20},{1,9},{5... | collective-permute-start | bytes 884744 | tf_op jit(solution)/shard_map/ppermute | solution.py:528
  30.2 1.8 %collective-permute-start.8 = (bf16[384,384]{1,0:T(8,128)(2,1)S(1)}, bf16[384,384]{1,0:T(8,128)(2,1)S(1)}, u32[]{:S(2)}, u32[]{:S(2)}) collective-permute-start(bf16[384,384]{1,0:T(8,128)(2,1)S(1)} %get-tuple-element.61), channel_id=1, source_target_pairs={{0,4},{4,0},{8,12},{12,8},{16,20},{20,16},{24,28},{28,24},{1,5},{5... | collective-permute-start | bytes 884744 | tf_op jit(solution)/shard_map/ppermute | solution.py:516
  32.1 0.4 shard_map.117
  32.5 1.3 %collective-permute-start.10 = (bf16[384,384]{1,0:T(8,128)(2,1)S(1)}, bf16[384,384]{1,0:T(8,128)(2,1)S(1)}, u32[]{:S(2)}, u32[]{:S(2)}) collective-permute-start(bf16[384,384]{1,0:T(8,128)(2,1)S(1)} %get-tuple-element.67), channel_id=1, source_target_pairs={{8,4},{12,0},{16,28},{20,24},{9,5},{13,1},{17,29},{21,25},{10,6},{... | collective-permute-start | bytes 884744 | tf_op jit(solution)/shard_map/ppermute | solution.py:538
  33.8 1.3 %collective-permute-start.11 = (bf16[384,384]{1,0:T(8,128)(2,1)S(1)}, bf16[384,384]{1,0:T(8,128)(2,1)S(1)}, u32[]{:S(2)}, u32[]{:S(2)}) collective-permute-start(bf16[384,384]{1,0:T(8,128)(2,1)S(1)} %get-tuple-element.68), channel_id=1, source_target_pairs={{16,0},{20,4},{8,24},{12,28},{17,1},{21,5},{9,25},{13,29},{18,2},{... | collective-permute-start | bytes 884744 | tf_op jit(solution)/shard_map/ppermute | solution.py:537
  35.0 0.3 collective-permute-start.12
  35.4 0.9 %collective-permute-done.7.near = bf16[384,384]{1,0:T(8,128)(2,1)S(1)} collective-permute-done((bf16[384,384]{1,0:T(8,128)(2,1)S(1)}, bf16[384,384]{1,0:T(8,128)(2,1)S(1)}, u32[]{:S(2)}, u32[]{:S(2)}) %collective-permute-start.7) | collective-permute-done | bytes 294944 | tf_op jit(solution)/shard_map/ppermute | solution.py:528
  36.2 0.7 %collective-permute-start.9 = (bf16[384,384]{1,0:T(8,128)(2,1)S(1)}, bf16[384,384]{1,0:T(8,128)(2,1)S(1)}, u32[]{:S(2)}, u32[]{:S(2)}) collective-permute-start(bf16[384,384]{1,0:T(8,128)(2,1)S(1)} %get-tuple-element.66), channel_id=1, source_target_pairs={{8,16},{12,20},{16,8},{20,12},{9,17},{13,21},{17,9},{21,13},{10,18... | collective-permute-start | bytes 884744 | tf_op jit(solution)/shard_map/ppermute | solution.py:539
  36.9 4.3 %collective-permute-done.8.early = bf16[384,384]{1,0:T(8,128)(2,1)S(1)} collective-permute-done((bf16[384,384]{1,0:T(8,128)(2,1)S(1)}, bf16[384,384]{1,0:T(8,128)(2,1)S(1)}, u32[]{:S(2)}, u32[]{:S(2)}) %collective-permute-start.8) | collective-permute-done | bytes 294944 | tf_op jit(solution)/shard_map/ppermute | solution.py:516
  41.2 1.5 %collective-permute-start.6 = (f32[1,192]{1,0:T(1,128)S(1)}, f32[1,192]{1,0:T(1,128)S(1)}, u32[]{:S(2)}, u32[]{:S(2)}) collective-permute-start(f32[1,192]{1,0:T(1,128)S(1)} %get-tuple-element.56.dots), channel_id=1, source_target_pairs={{0,2},{1,3},{2,0},{3,1},{4,6},{5,7},{6,4},{7,5},{8,10},{9,11},{10,... | collective-permute-start | bytes 2312 | tf_op jit(solution)/shard_map/ppermute | solution.py:536
  42.7 0.3 shard_map.118
  43.0 1.8 %collective-permute-done.6.dots_far = f32[1,192]{1,0:T(1,128)S(1)} collective-permute-done((f32[1,192]{1,0:T(1,128)S(1)}, f32[1,192]{1,0:T(1,128)S(1)}, u32[]{:S(2)}, u32[]{:S(2)}) %collective-permute-start.6) | collective-permute-done | bytes 800 | tf_op jit(solution)/shard_map/ppermute | solution.py:536
  44.8 5.3 %collective-permute-done.10.cross = bf16[384,384]{1,0:T(8,128)(2,1)S(1)} collective-permute-done((bf16[384,384]{1,0:T(8,128)(2,1)S(1)}, bf16[384,384]{1,0:T(8,128)(2,1)S(1)}, u32[]{:S(2)}, u32[]{:S(2)}) %collective-permute-start.10) | collective-permute-done | bytes 294944 | tf_op jit(solution)/shard_map/ppermute | solution.py:538
  50.1 0.2 collective-permute-done.12.late
  50.2 1.2 %shard_map.119 = (bf16[192,768]{1,0:T(8,128)(2,1)}, bf16[192,768]{1,0:T(8,128)(2,1)}, bf16[192,768]{1,0:T(8,128)(2,1)}, f32[1,192]{1,0:T(1,128)}) custom-call(s32[12,128]{1,0:T(8,128)S(1)} %bitcast.10, f32[1,192]{1,0:T(1,128)S(1)} %bitcast.12, f32[1,192]{1,0:T(1,128)S(1)} %get-tuple-element.56.dots, f32[1,192]{1,0:T(1,128)S(1)} %collective-permute-done.6.dots_far, ...), custom_call_target="tpu_custom_call" | custom-call | flops 1024 | bytes 1024 | tf_op jit(solution)/shard_map/pallas_call | solution.py:662
  (17 shorter events, 0.1 us)
Async XLA Ops:
  0.6 13.7 %copy-start.4 = (s32[1536]{0:T(1024)S(1)}, s32[1536]{0:T(1024)}, u32[]{:S(2)}) copy-start(s32[1536]{0:T(1024)} %param.15) | copy-start | bytes 18436
  4.4 15.0 %copy-start.6 = (f32[1,192]{1,0:T(1,128)S(1)}, f32[1,192]{1,0:T(1,128)}, u32[]{:S(2)}) copy-start(f32[1,192]{1,0:T(1,128)} %get-tuple-element.46.dots) | copy-start | bytes 2308
  4.5 17.1 %collective-permute-start = (bf16[800,384]{1,0:T(8,128)(2,1)}, bf16[800,384]{1,0:T(8,128)(2,1)S(1)}, u32[]{:S(2)}, u32[]{:S(2)}) collective-permute-start(bf16[800,384]{1,0:T(8,128)(2,1)} %get-tuple-element.40.own), channel_id=1, source_target_pairs={{0,4},{4,0},{8,12},{12,8},{16,20},{20,16},{24,28},{28,24},{1,5},{5... | collective-permute-start | bytes 1843208 | tf_op jit(solution)/shard_map/ppermute | solution.py:497
  7.5 11.1 %collective-permute-start.1 = (bf16[400,384]{1,0:T(8,128)(2,1)}, bf16[400,384]{1,0:T(8,128)(2,1)S(1)}, u32[]{:S(2)}, u32[]{:S(2)}) collective-permute-start(bf16[400,384]{1,0:T(8,128)(2,1)} %get-tuple-element.43), channel_id=1, source_target_pairs={{0,8},{4,12},{8,0},{12,4},{16,24},{20,28},{24,16},{28,20},{1,9},{5... | collective-permute-start | bytes 921608 | tf_op jit(solution)/shard_map/ppermute | solution.py:496
  9.1 13.2 %collective-permute-start.2 = (bf16[400,384]{1,0:T(8,128)(2,1)}, bf16[400,384]{1,0:T(8,128)(2,1)S(1)}, u32[]{:S(2)}, u32[]{:S(2)}) collective-permute-start(bf16[400,384]{1,0:T(8,128)(2,1)} %get-tuple-element.44), channel_id=1, source_target_pairs={{0,16},{4,20},{24,8},{28,12},{1,17},{5,21},{25,9},{29,13},{2,18},{... | collective-permute-start | bytes 921608 | tf_op jit(solution)/shard_map/ppermute | solution.py:498
  13.6 10.3 %collective-permute-start.4 = (bf16[400,384]{1,0:T(8,128)(2,1)}, bf16[400,384]{1,0:T(8,128)(2,1)S(1)}, u32[]{:S(2)}, u32[]{:S(2)}) collective-permute-start(bf16[400,384]{1,0:T(8,128)(2,1)} %get-tuple-element.44), channel_id=1, source_target_pairs={{8,16},{12,20},{16,8},{20,12},{9,17},{13,21},{17,9},{21,13},{10,18... | collective-permute-start | bytes 921608 | tf_op jit(solution)/shard_map/ppermute | solution.py:499
  14.3 1.1 %copy-start = (bf16[800,384]{1,0:T(8,128)(2,1)S(1)}, bf16[800,384]{1,0:T(8,128)(2,1)}, u32[]{:S(2)}) copy-start(bf16[800,384]{1,0:T(8,128)(2,1)} %get-tuple-element.39.mine) | copy-start | bytes 1843204
  15.4 1.1 %copy-start.2 = (bf16[800,384]{1,0:T(8,128)(2,1)S(1)}, bf16[800,384]{1,0:T(8,128)(2,1)}, u32[]{:S(2)}) copy-start(bf16[800,384]{1,0:T(8,128)(2,1)} %get-tuple-element.40.own) | copy-start | bytes 1843204
  16.5 5.1 %copy-start.1 = (bf16[800,384]{1,0:T(8,128)(2,1)S(1)}, bf16[800,384]{1,0:T(8,128)(2,1)}, u32[]{:S(2)}) copy-start(bf16[800,384]{1,0:T(8,128)(2,1)} %get-tuple-element.39.mine) | copy-start | bytes 1843204
  18.6 3.7 %copy-start.3 = (bf16[800,384]{1,0:T(8,128)(2,1)S(1)}, bf16[800,384]{1,0:T(8,128)(2,1)}, u32[]{:S(2)}) copy-start(bf16[800,384]{1,0:T(8,128)(2,1)} %get-tuple-element.40.own) | copy-start | bytes 1843204
  18.6 13.5 %collective-permute-start.5 = (bf16[400,384]{1,0:T(8,128)(2,1)S(1)}, bf16[400,384]{1,0:T(8,128)(2,1)S(1)}, u32[]{:S(2)}, u32[]{:S(2)}) collective-permute-start(bf16[400,384]{1,0:T(8,128)(2,1)S(1)} %shard_map.114.near), channel_id=1, source_target_pairs={{8,12},{12,8},{16,20},{20,16},{9,13},{13,9},{17,21},{21,17},{10,14... | collective-permute-start | bytes 921608 | tf_op jit(solution)/shard_map/ppermute | solution.py:509
  19.4 4.5 %collective-permute-start.3 = (f32[1,192]{1,0:T(1,128)S(1)}, f32[1,192]{1,0:T(1,128)S(1)}, u32[]{:S(2)}, u32[]{:S(2)}) collective-permute-start(f32[1,192]{1,0:T(1,128)S(1)} %copy-done.6), channel_id=1, source_target_pairs={{0,1},{1,0},{2,3},{3,2},{4,5},{5,4},{6,7},{7,6},{8,9},{9,8},{10,11... | collective-permute-start | bytes 2312 | tf_op jit(solution)/shard_map/ppermute | solution.py:522
  24.0 12.2 %collective-permute-start.7 = (bf16[384,384]{1,0:T(8,128)(2,1)S(1)}, bf16[384,384]{1,0:T(8,128)(2,1)S(1)}, u32[]{:S(2)}, u32[]{:S(2)}) collective-permute-start(bf16[384,384]{1,0:T(8,128)(2,1)S(1)} %get-tuple-element.60), channel_id=1, source_target_pairs={{0,8},{4,12},{8,0},{12,4},{16,24},{20,28},{24,16},{28,20},{1,9},{5... | collective-permute-start | bytes 884744 | tf_op jit(solution)/shard_map/ppermute | solution.py:528
  30.2 11.0 %collective-permute-start.8 = (bf16[384,384]{1,0:T(8,128)(2,1)S(1)}, bf16[384,384]{1,0:T(8,128)(2,1)S(1)}, u32[]{:S(2)}, u32[]{:S(2)}) collective-permute-start(bf16[384,384]{1,0:T(8,128)(2,1)S(1)} %get-tuple-element.61), channel_id=1, source_target_pairs={{0,4},{4,0},{8,12},{12,8},{16,20},{20,16},{24,28},{28,24},{1,5},{5... | collective-permute-start | bytes 884744 | tf_op jit(solution)/shard_map/ppermute | solution.py:516
  32.5 17.6 %collective-permute-start.10 = (bf16[384,384]{1,0:T(8,128)(2,1)S(1)}, bf16[384,384]{1,0:T(8,128)(2,1)S(1)}, u32[]{:S(2)}, u32[]{:S(2)}) collective-permute-start(bf16[384,384]{1,0:T(8,128)(2,1)S(1)} %get-tuple-element.67), channel_id=1, source_target_pairs={{8,4},{12,0},{16,28},{20,24},{9,5},{13,1},{17,29},{21,25},{10,6},{... | collective-permute-start | bytes 884744 | tf_op jit(solution)/shard_map/ppermute | solution.py:538
  33.8 16.3 %collective-permute-start.11 = (bf16[384,384]{1,0:T(8,128)(2,1)S(1)}, bf16[384,384]{1,0:T(8,128)(2,1)S(1)}, u32[]{:S(2)}, u32[]{:S(2)}) collective-permute-start(bf16[384,384]{1,0:T(8,128)(2,1)S(1)} %get-tuple-element.68), channel_id=1, source_target_pairs={{16,0},{20,4},{8,24},{12,28},{17,1},{21,5},{9,25},{13,29},{18,2},{... | collective-permute-start | bytes 884744 | tf_op jit(solution)/shard_map/ppermute | solution.py:537
  35.0 15.2 %collective-permute-start.12 = (bf16[384,384]{1,0:T(8,128)(2,1)S(1)}, bf16[384,384]{1,0:T(8,128)(2,1)S(1)}, u32[]{:S(2)}, u32[]{:S(2)}) collective-permute-start(bf16[384,384]{1,0:T(8,128)(2,1)S(1)} %get-tuple-element.69), channel_id=1, source_target_pairs={{0,4},{4,0},{8,12},{12,8},{16,20},{20,16},{24,28},{28,24},{1,5},{5... | collective-permute-start | bytes 884744 | tf_op jit(solution)/shard_map/ppermute | solution.py:540
  36.2 14.0 %collective-permute-start.9 = (bf16[384,384]{1,0:T(8,128)(2,1)S(1)}, bf16[384,384]{1,0:T(8,128)(2,1)S(1)}, u32[]{:S(2)}, u32[]{:S(2)}) collective-permute-start(bf16[384,384]{1,0:T(8,128)(2,1)S(1)} %get-tuple-element.66), channel_id=1, source_target_pairs={{8,16},{12,20},{16,8},{20,12},{9,17},{13,21},{17,9},{21,13},{10,18... | collective-permute-start | bytes 884744 | tf_op jit(solution)/shard_map/ppermute | solution.py:539
  41.2 3.6 %collective-permute-start.6 = (f32[1,192]{1,0:T(1,128)S(1)}, f32[1,192]{1,0:T(1,128)S(1)}, u32[]{:S(2)}, u32[]{:S(2)}) collective-permute-start(f32[1,192]{1,0:T(1,128)S(1)} %get-tuple-element.56.dots), channel_id=1, source_target_pairs={{0,2},{1,3},{2,0},{3,1},{4,6},{5,7},{6,4},{7,5},{8,10},{9,11},{10,... | collective-permute-start | bytes 2312 | tf_op jit(solution)/shard_map/ppermute | solution.py:536
  42.7 7.5 %copy-start.5 = (f32[192]{0:T(256)S(1)}, f32[192]{0:T(256)}, u32[]{:S(2)}) copy-start(f32[192]{0:T(256)} %param.14) | copy-start | bytes 2308

commit v9 on v5

--- a/solution.py
+++ b/solution.py
@@ -455,7 +455,7 @@
 
 def four_join_kernel(
     heads, positions, logit, dots, dots_far, moving_sum, staying_sum, grads_guest, own_near,
-    middle, skip, cross, late, query_grad, key_grad, value_grad, router
+    middle, late, skip, cross, query_grad, key_grad, value_grad, router
 ):
     slots, half = moving_sum.shape[0] // 4, moving_sum.shape[1]
     shard = lax.axis_index("seq")
@@ -548,7 +548,7 @@
         functools.partial(four_join_kernel, heads),
         [shape(slots, BF16, width)] * 3 + [row],
         positions, logit, dots, dots_far, moving_sum, staying_sum, grads_guest, own_near,
-        middle, skip, cross, late,
+        middle, late, skip, cross,
     )
 
 

time: 51.9 us -> 52 us (level)
    ppermute x1, waiting for transfers between devices: 0.18 us -> 6.46 us  [four_levels(): late = lax.ppermute(late, 'seq', pairs([(i, i) for i in range(4)], 1))]
    ppermute x1, waiting for transfers between devices: 5.57 us -> 0.71 us  [four_levels(): lax.ppermute(near_low, 'seq', pairs([(0, 1), (1, 0), (2, 3), (3, 2)]))]
    ppermute x1, waiting for transfers between devices: 4.79 us -> 0.01 us  [four_levels(): cross = lax.ppermute(cross_low, 'seq', pairs([(1, 0), (2, 3)], 1))]
    ppermute x1, waiting for transfers between devices: 0.01 us -> 3.46 us  [four_levels(): early = lax.ppermute(early, 'seq', pairs([(i, i) for i in range(4)], 1))]
where the time goes in v9:
time: 52 us; the launch traced here: 51.6 us
  starting transfers between devices  24 us (46%)
  waiting for transfers between devices  15.1 us (29%)
  Pallas kernels  9.54 us (18%)
  local copies, waits for them, and re-layouts  2.16 us (4%)
  between operations  0.84 us (2%)
    pallas_call x9, Pallas kernels, call(): pl.pallas_call(kernel, out_shape=out_shape, in_specs=[pl.BlockSpec(memory...  9.54 us
    ppermute x1, waiting for transfers between devices, four_levels(): late = lax.ppermute(late, 'seq', pairs([(i, i) for i in range(4)], 1))  6.46 us
    ppermute x1, starting transfers between devices, four_levels(): lax.ppermute(near_low, 'seq', pairs([(0, 1), (1, 0), (2, 3), (3, 2)]))  6.23 us
    ppermute x1, starting transfers between devices, four_levels(): skip = lax.ppermute(far_send, 'seq', pairs([(0, 2), (3, 1)]))  4.56 us
    ppermute x1, waiting for transfers between devices, four_levels(): early = lax.ppermute(early, 'seq', pairs([(i, i) for i in range(4)], 1))  3.46 us
    ppermute x1, starting transfers between devices, four_levels(): other = lax.ppermute(own, 'seq', pairs([(i, i) for i in range(4)], 1))  3.03 us
    unnamed x14, local copies, waits for them, and re-layouts  2.16 us
    ppermute x1, waiting for transfers between devices, four_levels(): other = lax.ppermute(own, 'seq', pairs([(i, i) for i in range(4)], 1))  1.88 us
  transfers between devices with their start and end apart: 13, of which 6 were waited for; matrix products, arithmetic and copies ran while one was open for 0% of the time, Pallas kernels for 9%

profile of v9, /device:TPU:0, one launch (start us, length us, event | category | flops | bytes accessed | tf_op | source)
XLA Modules:
  0.0 51.6 jit_solution(10342403298823619243)
XLA Ops:
  0.6 3.8 %shard_map.111 = (f32[1,192]{1,0:T(1,128)}, bf16[800,384]{1,0:T(8,128)(2,1)}, bf16[800,384]{1,0:T(8,128)(2,1)}, bf16[400,384]{1,0:T(8,128)(2,1)}, bf16[400,384]{1,0:T(8,128)(2,1)}) custom-call(bf16[192,768]{1,0:T(8,128)(2,1)} %refs_0_.1, bf16[192,768]{1,0:T(8,128)(2,1)} %refs_1_.1, f32[1,192]{1,0:T(1,128)} %bitcast.11, f32[6,192]{1,0:T(8,128)} %bitcast.13, ...), custom_call_target="tpu_custom_call" | custom-call | flops 1024 | bytes 1024 | tf_op jit(solution)/shard_map/pallas_call | solution.py:662
  4.4 0.0 copy-start.6
  4.4 3.0 %collective-permute-start = (bf16[800,384]{1,0:T(8,128)(2,1)}, bf16[800,384]{1,0:T(8,128)(2,1)S(1)}, u32[]{:S(2)}, u32[]{:S(2)}) collective-permute-start(bf16[800,384]{1,0:T(8,128)(2,1)} %get-tuple-element.40.own), channel_id=1, source_target_pairs={{0,4},{4,0},{8,12},{12,8},{16,20},{20,16},{24,28},{28,24},{1,5},{5... | collective-permute-start | bytes 1843208 | tf_op jit(solution)/shard_map/ppermute | solution.py:497
  7.5 1.7 %collective-permute-start.1 = (bf16[400,384]{1,0:T(8,128)(2,1)}, bf16[400,384]{1,0:T(8,128)(2,1)S(1)}, u32[]{:S(2)}, u32[]{:S(2)}) collective-permute-start(bf16[400,384]{1,0:T(8,128)(2,1)} %get-tuple-element.43), channel_id=1, source_target_pairs={{0,8},{4,12},{8,0},{12,4},{16,24},{20,28},{24,16},{28,20},{1,9},{5... | collective-permute-start | bytes 921608 | tf_op jit(solution)/shard_map/ppermute | solution.py:496
  9.2 4.6 %collective-permute-start.2 = (bf16[400,384]{1,0:T(8,128)(2,1)}, bf16[400,384]{1,0:T(8,128)(2,1)S(1)}, u32[]{:S(2)}, u32[]{:S(2)}) collective-permute-start(bf16[400,384]{1,0:T(8,128)(2,1)} %get-tuple-element.44), channel_id=1, source_target_pairs={{0,16},{4,20},{24,8},{28,12},{1,17},{5,21},{25,9},{29,13},{2,18},{... | collective-permute-start | bytes 921608 | tf_op jit(solution)/shard_map/ppermute | solution.py:498
  13.8 0.7 %collective-permute-start.4 = (bf16[400,384]{1,0:T(8,128)(2,1)}, bf16[400,384]{1,0:T(8,128)(2,1)S(1)}, u32[]{:S(2)}, u32[]{:S(2)}) collective-permute-start(bf16[400,384]{1,0:T(8,128)(2,1)} %get-tuple-element.44), channel_id=1, source_target_pairs={{8,16},{12,20},{16,8},{20,12},{9,17},{13,21},{17,9},{21,13},{10,18... | collective-permute-start | bytes 921608 | tf_op jit(solution)/shard_map/ppermute | solution.py:499
  14.5 1.1 %copy-done = bf16[800,384]{1,0:T(8,128)(2,1)S(1)} copy-done((bf16[800,384]{1,0:T(8,128)(2,1)S(1)}, bf16[800,384]{1,0:T(8,128)(2,1)}, u32[]{:S(2)}) %copy-start) | copy-done | bytes 614424
  15.5 1.1 %copy-done.2 = bf16[800,384]{1,0:T(8,128)(2,1)S(1)} copy-done((bf16[800,384]{1,0:T(8,128)(2,1)S(1)}, bf16[800,384]{1,0:T(8,128)(2,1)}, u32[]{:S(2)}) %copy-start.2) | copy-done | bytes 614424
  16.6 2.1 %shard_map.112 = (f32[1,192]{1,0:T(1,128)S(1)}, f32[768,384]{1,0:T(8,128)S(1)}, f32[768,384]{1,0:T(8,128)S(1)}) custom-call(s32[12,128]{1,0:T(8,128)S(1)} %bitcast.5, bf16[800,384]{1,0:T(8,128)(2,1)S(1)} %copy-done, bf16[800,384]{1,0:T(8,128)(2,1)S(1)} %copy-done.2), custom_call_target="tpu_custom_call" | custom-call | flops 1024 | bytes 1024 | tf_op jit(solution)/shard_map/pallas_call | solution.py:662
  18.7 0.0 collective-permute-done.1.block
  18.8 0.8 %collective-permute-start.5 = (bf16[400,384]{1,0:T(8,128)(2,1)S(1)}, bf16[400,384]{1,0:T(8,128)(2,1)S(1)}, u32[]{:S(2)}, u32[]{:S(2)}) collective-permute-start(bf16[400,384]{1,0:T(8,128)(2,1)S(1)} %shard_map.114.near), channel_id=1, source_target_pairs={{8,12},{12,8},{16,20},{20,16},{9,13},{13,9},{17,21},{21,17},{10,14... | collective-permute-start | bytes 921608 | tf_op jit(solution)/shard_map/ppermute | solution.py:509
  19.6 0.1 collective-permute-start.3
  19.7 1.9 %collective-permute-done.other = bf16[800,384]{1,0:T(8,128)(2,1)S(1)} collective-permute-done((bf16[800,384]{1,0:T(8,128)(2,1)}, bf16[800,384]{1,0:T(8,128)(2,1)S(1)}, u32[]{:S(2)}, u32[]{:S(2)}) %collective-permute-start) | collective-permute-done | bytes 614432 | tf_op jit(solution)/shard_map/ppermute | solution.py:497
  21.6 0.8 %collective-permute-done.2.skip = bf16[400,384]{1,0:T(8,128)(2,1)S(1)} collective-permute-done((bf16[400,384]{1,0:T(8,128)(2,1)}, bf16[400,384]{1,0:T(8,128)(2,1)S(1)}, u32[]{:S(2)}, u32[]{:S(2)}) %collective-permute-start.2) | collective-permute-done | bytes 307232 | tf_op jit(solution)/shard_map/ppermute | solution.py:498
  22.4 1.7 %shard_map.115 = (f32[1,192]{1,0:T(1,128)S(1)}, f32[384,384]{1,0:T(8,128)S(1)}, f32[384,384]{1,0:T(8,128)S(1)}, bf16[384,384]{1,0:T(8,128)(2,1)S(1)}, f32[384,38...) custom-call(s32[12,128]{1,0:T(8,128)S(1)} %bitcast.7, f32[1,192]{1,0:T(1,128)S(1)} %get-tuple-element.42.after, ...), custom_call_target="tpu_custom_call" | custom-call | flops 1024 | bytes 1024 | tf_op jit(solution)/shard_map/pallas_call | solution.py:662
  24.1 0.0 collective-permute-done.3.dots_near
  24.1 0.0 collective-permute-done.4.middle
  24.1 0.1 shard_map.116
  24.2 6.2 %collective-permute-start.7 = (bf16[384,384]{1,0:T(8,128)(2,1)S(1)}, bf16[384,384]{1,0:T(8,128)(2,1)S(1)}, u32[]{:S(2)}, u32[]{:S(2)}) collective-permute-start(bf16[384,384]{1,0:T(8,128)(2,1)S(1)} %get-tuple-element.60), channel_id=1, source_target_pairs={{0,8},{4,12},{8,0},{12,4},{16,24},{20,28},{24,16},{28,20},{1,9},{5... | collective-permute-start | bytes 884744 | tf_op jit(solution)/shard_map/ppermute | solution.py:528
  30.4 1.8 %collective-permute-start.8 = (bf16[384,384]{1,0:T(8,128)(2,1)S(1)}, bf16[384,384]{1,0:T(8,128)(2,1)S(1)}, u32[]{:S(2)}, u32[]{:S(2)}) collective-permute-start(bf16[384,384]{1,0:T(8,128)(2,1)S(1)} %get-tuple-element.61), channel_id=1, source_target_pairs={{0,4},{4,0},{8,12},{12,8},{16,20},{20,16},{24,28},{28,24},{1,5},{5... | collective-permute-start | bytes 884744 | tf_op jit(solution)/shard_map/ppermute | solution.py:516
  32.2 0.4 shard_map.117
  32.6 0.4 collective-permute-start.10
  32.9 1.3 %collective-permute-start.11 = (bf16[384,384]{1,0:T(8,128)(2,1)S(1)}, bf16[384,384]{1,0:T(8,128)(2,1)S(1)}, u32[]{:S(2)}, u32[]{:S(2)}) collective-permute-start(bf16[384,384]{1,0:T(8,128)(2,1)S(1)} %get-tuple-element.68), channel_id=1, source_target_pairs={{16,0},{20,4},{8,24},{12,28},{17,1},{21,5},{9,25},{13,29},{18,2},{... | collective-permute-start | bytes 884744 | tf_op jit(solution)/shard_map/ppermute | solution.py:537
  34.2 1.3 %collective-permute-start.12 = (bf16[384,384]{1,0:T(8,128)(2,1)S(1)}, bf16[384,384]{1,0:T(8,128)(2,1)S(1)}, u32[]{:S(2)}, u32[]{:S(2)}) collective-permute-start(bf16[384,384]{1,0:T(8,128)(2,1)S(1)} %get-tuple-element.69), channel_id=1, source_target_pairs={{8,4},{12,0},{16,28},{20,24},{9,5},{13,1},{17,29},{21,25},{10,6},{... | collective-permute-start | bytes 884744 | tf_op jit(solution)/shard_map/ppermute | solution.py:538
  35.5 0.7 %collective-permute-done.7.near = bf16[384,384]{1,0:T(8,128)(2,1)S(1)} collective-permute-done((bf16[384,384]{1,0:T(8,128)(2,1)S(1)}, bf16[384,384]{1,0:T(8,128)(2,1)S(1)}, u32[]{:S(2)}, u32[]{:S(2)}) %collective-permute-start.7) | collective-permute-done | bytes 294944 | tf_op jit(solution)/shard_map/ppermute | solution.py:528
  36.2 0.7 %collective-permute-start.9 = (bf16[384,384]{1,0:T(8,128)(2,1)S(1)}, bf16[384,384]{1,0:T(8,128)(2,1)S(1)}, u32[]{:S(2)}, u32[]{:S(2)}) collective-permute-start(bf16[384,384]{1,0:T(8,128)(2,1)S(1)} %get-tuple-element.66), channel_id=1, source_target_pairs={{8,16},{12,20},{16,8},{20,12},{9,17},{13,21},{17,9},{21,13},{10,18... | collective-permute-start | bytes 884744 | tf_op jit(solution)/shard_map/ppermute | solution.py:539
  36.9 3.5 %collective-permute-done.8.early = bf16[384,384]{1,0:T(8,128)(2,1)S(1)} collective-permute-done((bf16[384,384]{1,0:T(8,128)(2,1)S(1)}, bf16[384,384]{1,0:T(8,128)(2,1)S(1)}, u32[]{:S(2)}, u32[]{:S(2)}) %collective-permute-start.8) | collective-permute-done | bytes 294944 | tf_op jit(solution)/shard_map/ppermute | solution.py:516
  40.3 1.5 %collective-permute-start.6 = (f32[1,192]{1,0:T(1,128)S(1)}, f32[1,192]{1,0:T(1,128)S(1)}, u32[]{:S(2)}, u32[]{:S(2)}) collective-permute-start(f32[1,192]{1,0:T(1,128)S(1)} %get-tuple-element.56.dots), channel_id=1, source_target_pairs={{0,2},{1,3},{2,0},{3,1},{4,6},{5,7},{6,4},{7,5},{8,10},{9,11},{10,... | collective-permute-start | bytes 2312 | tf_op jit(solution)/shard_map/ppermute | solution.py:536
  41.8 0.3 shard_map.118
  42.1 1.8 %collective-permute-done.6.dots_far = f32[1,192]{1,0:T(1,128)S(1)} collective-permute-done((f32[1,192]{1,0:T(1,128)S(1)}, f32[1,192]{1,0:T(1,128)S(1)}, u32[]{:S(2)}, u32[]{:S(2)}) %collective-permute-start.6) | collective-permute-done | bytes 800 | tf_op jit(solution)/shard_map/ppermute | solution.py:536
  43.9 6.5 %collective-permute-done.10.late = bf16[384,384]{1,0:T(8,128)(2,1)S(1)} collective-permute-done((bf16[384,384]{1,0:T(8,128)(2,1)S(1)}, bf16[384,384]{1,0:T(8,128)(2,1)S(1)}, u32[]{:S(2)}, u32[]{:S(2)}) %collective-permute-start.10) | collective-permute-done | bytes 294944 | tf_op jit(solution)/shard_map/ppermute | solution.py:540
  50.4 1.2 %shard_map.119 = (bf16[192,768]{1,0:T(8,128)(2,1)}, bf16[192,768]{1,0:T(8,128)(2,1)}, bf16[192,768]{1,0:T(8,128)(2,1)}, f32[1,192]{1,0:T(1,128)}) custom-call(s32[12,128]{1,0:T(8,128)S(1)} %bitcast.10, f32[1,192]{1,0:T(1,128)S(1)} %bitcast.12, f32[1,192]{1,0:T(1,128)S(1)} %get-tuple-element.56.dots, f32[1,192]{1,0:T(1,128)S(1)} %collective-permute-done.6.dots_far, ...), custom_call_target="tpu_custom_call" | custom-call | flops 1024 | bytes 1024 | tf_op jit(solution)/shard_map/pallas_call | solution.py:662
  (17 shorter events, 0.1 us)
Async XLA Ops:
  0.6 13.8 %copy-start.4 = (s32[1536]{0:T(1024)S(1)}, s32[1536]{0:T(1024)}, u32[]{:S(2)}) copy-start(s32[1536]{0:T(1024)} %param.15) | copy-start | bytes 18436
  4.4 15.1 %copy-start.6 = (f32[1,192]{1,0:T(1,128)S(1)}, f32[1,192]{1,0:T(1,128)}, u32[]{:S(2)}) copy-start(f32[1,192]{1,0:T(1,128)} %get-tuple-element.46.dots) | copy-start | bytes 2308
  4.4 17.1 %collective-permute-start = (bf16[800,384]{1,0:T(8,128)(2,1)}, bf16[800,384]{1,0:T(8,128)(2,1)S(1)}, u32[]{:S(2)}, u32[]{:S(2)}) collective-permute-start(bf16[800,384]{1,0:T(8,128)(2,1)} %get-tuple-element.40.own), channel_id=1, source_target_pairs={{0,4},{4,0},{8,12},{12,8},{16,20},{20,16},{24,28},{28,24},{1,5},{5... | collective-permute-start | bytes 1843208 | tf_op jit(solution)/shard_map/ppermute | solution.py:497
  7.5 11.3 %collective-permute-start.1 = (bf16[400,384]{1,0:T(8,128)(2,1)}, bf16[400,384]{1,0:T(8,128)(2,1)S(1)}, u32[]{:S(2)}, u32[]{:S(2)}) collective-permute-start(bf16[400,384]{1,0:T(8,128)(2,1)} %get-tuple-element.43), channel_id=1, source_target_pairs={{0,8},{4,12},{8,0},{12,4},{16,24},{20,28},{24,16},{28,20},{1,9},{5... | collective-permute-start | bytes 921608 | tf_op jit(solution)/shard_map/ppermute | solution.py:496
  9.2 13.2 %collective-permute-start.2 = (bf16[400,384]{1,0:T(8,128)(2,1)}, bf16[400,384]{1,0:T(8,128)(2,1)S(1)}, u32[]{:S(2)}, u32[]{:S(2)}) collective-permute-start(bf16[400,384]{1,0:T(8,128)(2,1)} %get-tuple-element.44), channel_id=1, source_target_pairs={{0,16},{4,20},{24,8},{28,12},{1,17},{5,21},{25,9},{29,13},{2,18},{... | collective-permute-start | bytes 921608 | tf_op jit(solution)/shard_map/ppermute | solution.py:498
  13.8 10.3 %collective-permute-start.4 = (bf16[400,384]{1,0:T(8,128)(2,1)}, bf16[400,384]{1,0:T(8,128)(2,1)S(1)}, u32[]{:S(2)}, u32[]{:S(2)}) collective-permute-start(bf16[400,384]{1,0:T(8,128)(2,1)} %get-tuple-element.44), channel_id=1, source_target_pairs={{8,16},{12,20},{16,8},{20,12},{9,17},{13,21},{17,9},{21,13},{10,18... | collective-permute-start | bytes 921608 | tf_op jit(solution)/shard_map/ppermute | solution.py:499
  14.5 1.1 %copy-start = (bf16[800,384]{1,0:T(8,128)(2,1)S(1)}, bf16[800,384]{1,0:T(8,128)(2,1)}, u32[]{:S(2)}) copy-start(bf16[800,384]{1,0:T(8,128)(2,1)} %get-tuple-element.39.mine) | copy-start | bytes 1843204
  15.5 1.1 %copy-start.2 = (bf16[800,384]{1,0:T(8,128)(2,1)S(1)}, bf16[800,384]{1,0:T(8,128)(2,1)}, u32[]{:S(2)}) copy-start(bf16[800,384]{1,0:T(8,128)(2,1)} %get-tuple-element.40.own) | copy-start | bytes 1843204
  16.6 4.9 %copy-start.1 = (bf16[800,384]{1,0:T(8,128)(2,1)S(1)}, bf16[800,384]{1,0:T(8,128)(2,1)}, u32[]{:S(2)}) copy-start(bf16[800,384]{1,0:T(8,128)(2,1)} %get-tuple-element.39.mine) | copy-start | bytes 1843204
  18.7 3.7 %copy-start.3 = (bf16[800,384]{1,0:T(8,128)(2,1)S(1)}, bf16[800,384]{1,0:T(8,128)(2,1)}, u32[]{:S(2)}) copy-start(bf16[800,384]{1,0:T(8,128)(2,1)} %get-tuple-element.40.own) | copy-start | bytes 1843204
  18.8 13.4 %collective-permute-start.5 = (bf16[400,384]{1,0:T(8,128)(2,1)S(1)}, bf16[400,384]{1,0:T(8,128)(2,1)S(1)}, u32[]{:S(2)}, u32[]{:S(2)}) collective-permute-start(bf16[400,384]{1,0:T(8,128)(2,1)S(1)} %shard_map.114.near), channel_id=1, source_target_pairs={{8,12},{12,8},{16,20},{20,16},{9,13},{13,9},{17,21},{21,17},{10,14... | collective-permute-start | bytes 921608 | tf_op jit(solution)/shard_map/ppermute | solution.py:509
  19.6 4.5 %collective-permute-start.3 = (f32[1,192]{1,0:T(1,128)S(1)}, f32[1,192]{1,0:T(1,128)S(1)}, u32[]{:S(2)}, u32[]{:S(2)}) collective-permute-start(f32[1,192]{1,0:T(1,128)S(1)} %copy-done.6), channel_id=1, source_target_pairs={{0,1},{1,0},{2,3},{3,2},{4,5},{5,4},{6,7},{7,6},{8,9},{9,8},{10,11... | collective-permute-start | bytes 2312 | tf_op jit(solution)/shard_map/ppermute | solution.py:522
  24.2 12.0 %collective-permute-start.7 = (bf16[384,384]{1,0:T(8,128)(2,1)S(1)}, bf16[384,384]{1,0:T(8,128)(2,1)S(1)}, u32[]{:S(2)}, u32[]{:S(2)}) collective-permute-start(bf16[384,384]{1,0:T(8,128)(2,1)S(1)} %get-tuple-element.60), channel_id=1, source_target_pairs={{0,8},{4,12},{8,0},{12,4},{16,24},{20,28},{24,16},{28,20},{1,9},{5... | collective-permute-start | bytes 884744 | tf_op jit(solution)/shard_map/ppermute | solution.py:528
  30.4 9.9 %collective-permute-start.8 = (bf16[384,384]{1,0:T(8,128)(2,1)S(1)}, bf16[384,384]{1,0:T(8,128)(2,1)S(1)}, u32[]{:S(2)}, u32[]{:S(2)}) collective-permute-start(bf16[384,384]{1,0:T(8,128)(2,1)S(1)} %get-tuple-element.61), channel_id=1, source_target_pairs={{0,4},{4,0},{8,12},{12,8},{16,20},{20,16},{24,28},{28,24},{1,5},{5... | collective-permute-start | bytes 884744 | tf_op jit(solution)/shard_map/ppermute | solution.py:516
  32.6 17.8 %collective-permute-start.10 = (bf16[384,384]{1,0:T(8,128)(2,1)S(1)}, bf16[384,384]{1,0:T(8,128)(2,1)S(1)}, u32[]{:S(2)}, u32[]{:S(2)}) collective-permute-start(bf16[384,384]{1,0:T(8,128)(2,1)S(1)} %get-tuple-element.67), channel_id=1, source_target_pairs={{0,4},{4,0},{8,12},{12,8},{16,20},{20,16},{24,28},{28,24},{1,5},{5... | collective-permute-start | bytes 884744 | tf_op jit(solution)/shard_map/ppermute | solution.py:540
  32.9 17.5 %collective-permute-start.11 = (bf16[384,384]{1,0:T(8,128)(2,1)S(1)}, bf16[384,384]{1,0:T(8,128)(2,1)S(1)}, u32[]{:S(2)}, u32[]{:S(2)}) collective-permute-start(bf16[384,384]{1,0:T(8,128)(2,1)S(1)} %get-tuple-element.68), channel_id=1, source_target_pairs={{16,0},{20,4},{8,24},{12,28},{17,1},{21,5},{9,25},{13,29},{18,2},{... | collective-permute-start | bytes 884744 | tf_op jit(solution)/shard_map/ppermute | solution.py:537
  34.2 16.2 %collective-permute-start.12 = (bf16[384,384]{1,0:T(8,128)(2,1)S(1)}, bf16[384,384]{1,0:T(8,128)(2,1)S(1)}, u32[]{:S(2)}, u32[]{:S(2)}) collective-permute-start(bf16[384,384]{1,0:T(8,128)(2,1)S(1)} %get-tuple-element.69), channel_id=1, source_target_pairs={{8,4},{12,0},{16,28},{20,24},{9,5},{13,1},{17,29},{21,25},{10,6},{... | collective-permute-start | bytes 884744 | tf_op jit(solution)/shard_map/ppermute | solution.py:538
  36.2 14.2 %collective-permute-start.9 = (bf16[384,384]{1,0:T(8,128)(2,1)S(1)}, bf16[384,384]{1,0:T(8,128)(2,1)S(1)}, u32[]{:S(2)}, u32[]{:S(2)}) collective-permute-start(bf16[384,384]{1,0:T(8,128)(2,1)S(1)} %get-tuple-element.66), channel_id=1, source_target_pairs={{8,16},{12,20},{16,8},{20,12},{9,17},{13,21},{17,9},{21,13},{10,18... | collective-permute-start | bytes 884744 | tf_op jit(solution)/shard_map/ppermute | solution.py:539
  40.3 3.6 %collective-permute-start.6 = (f32[1,192]{1,0:T(1,128)S(1)}, f32[1,192]{1,0:T(1,128)S(1)}, u32[]{:S(2)}, u32[]{:S(2)}) collective-permute-start(f32[1,192]{1,0:T(1,128)S(1)} %get-tuple-element.56.dots), channel_id=1, source_target_pairs={{0,2},{1,3},{2,0},{3,1},{4,6},{5,7},{6,4},{7,5},{8,10},{9,11},{10,... | collective-permute-start | bytes 2312 | tf_op jit(solution)/shard_map/ppermute | solution.py:536
  41.8 8.6 %copy-start.5 = (f32[192]{0:T(256)S(1)}, f32[192]{0:T(256)}, u32[]{:S(2)}) copy-start(f32[192]{0:T(256)} %param.14) | copy-start | bytes 2308
